TPU v7x, 32 devices: a whole 2x2x4 slice. The times are simulated.
32 devices in a mesh: seq: 8 (over z, y), head: 4 (over x, core).
Axes of the slice: x: 2, y: 2, z: 4, core: 2. Of those that a mesh axis runs over, the one named last changes fastest.
Arguments:
- queries: bfloat16 [4096, 8192], P('seq', 'head'), may hold values from -4 to 4
- key_vecs: bfloat16 [4096, 8192], P('seq', 'head'), may hold values from -4 to 4
- value_vecs: bfloat16 [4096, 8192], P('seq', 'head'), may hold values from -6 to 6
- log_decay: float32 [4096, 64], P('seq', 'head'), may hold values from -3 to 0, as said below
- norm_gain: float32 [8192], P('head'), may hold values from 0.1 to 1.9
- cotangent: bfloat16 [4096, 8192], P('seq', 'head'), may hold values from -6 to 6
Outputs:
- attended: bfloat16 [4096, 8192], P('seq', 'head')
- grad_queries: bfloat16 [4096, 8192], P('seq', 'head')
- grad_keys: bfloat16 [4096, 8192], P('seq', 'head')
- grad_values: bfloat16 [4096, 8192], P('seq', 'head')
Inputs may be any that keep to these rules, and one draw needn't show every extreme that they name: `log_decay`: every entry is negative.
All inputs are finite; a program needn't handle non-finite values.
Results may differ from a plain program's by a relative error of at most 0.0051.
Values sent between devices are 32-bit elements; how exact they have to be, the bound alone decides.
No kernel may reach another device: no remote copies, remote signals or barrier semaphores. Data moves between devices by JAX's collectives and lax.ppermute only.
A program may use at most 128 MiB of HBM per device.

v0:
```python
import functools

import jax
import jax.numpy as jnp
from jax import lax
from jax.experimental import pallas as pl
from jax.experimental.pallas import tpu as pltpu
from jax.sharding import PartitionSpec as P

HEAD_DIM = 128
BLOCK = 512
CHUNKS = 4
TILE = 256
epsilon = 1e-06
f32 = jnp.float32
bf16 = jnp.bfloat16

NN = (((1,), (0,)), ((), ()))
NT = (((1,), (1,)), ((), ()))
TN = (((0,), (0,)), ((), ()))


def dot(a, b, dims=NN):
    return lax.dot_general(a, b, dims, preferred_element_type=f32)


def halves(x):
    high = x.astype(bf16)
    return high, (x - high.astype(f32)).astype(bf16)


def column(row):
    return jnp.transpose(jnp.broadcast_to(row, (HEAD_DIM, row.shape[1])))


def wide(col, width):
    return jnp.concatenate([col] * (width // HEAD_DIM), axis=1)


def cumul_kernel(decay_ref, out_ref):
    decay = decay_ref[...]
    length = decay.shape[0]
    first = decay.astype(bf16)
    rest = decay - first.astype(f32)
    second = rest.astype(bf16)
    third = (rest - second.astype(f32)).astype(bf16)
    upto = lax.broadcasted_iota(jnp.int32, (length, length), 0) <= lax.broadcasted_iota(
        jnp.int32, (length, length), 1
    )
    upto = jnp.where(upto, 1.0, 0.0).astype(bf16)
    out_ref[...] = dot(first, upto, TN) + dot(second, upto, TN) + dot(third, upto, TN)


def head_row(cumul_ref, head):
    return cumul_ref[pl.ds(head, 1), :]


def trail_row(row):
    return jnp.exp(row[:, -1:] - row)


def outer_sum(left, scale_row, right):
    scaled = jnp.transpose(left.astype(f32)) * scale_row
    high, low = halves(scaled)
    return dot(high, right) + dot(low, right)


def cols(j):
    return slice(j * HEAD_DIM, (j + 1) * HEAD_DIM)


def pieces_kernel(chunk, half, y_ref, key_ref, value_ref, cumul_ref, send_ref, keep_ref):
    step = pl.program_id(0)
    group = jnp.where(step == 0, 1 - y_ref[0], y_ref[0])
    base = (2 * chunk + group) * half
    found = []
    for j in range(half):
        row = head_row(cumul_ref, base + j)
        found.append(outer_sum(key_ref[:, cols(j)], trail_row(row), value_ref[:, cols(j)]))

    @pl.when(step == 0)
    def _():
        for j in range(half):
            send_ref[j] = found[j]

    @pl.when(step == 1)
    def _():
        for j in range(half):
            keep_ref[j] = found[j]


def inner_kernel(chunk, half, query_ref, key_ref, value_ref, cumul_ref, out_ref):
    base = (2 * chunk + pl.program_id(0)) * half
    for j in range(half):
        row = head_row(cumul_ref, base + j)
        col = column(row)
        query, key, value = query_ref[:, cols(j)], key_ref[:, cols(j)], value_ref[:, cols(j)]
        for top in range(0, BLOCK, TILE):
            end = top + TILE
            scores = dot(query[top:end], key[:end], NT)
            spread = wide(col[top:end], end) - row[:, :end]
            causal = lax.broadcasted_iota(jnp.int32, (TILE, end), 0) + top >= (
                lax.broadcasted_iota(jnp.int32, (TILE, end), 1)
            )
            weights = (scores * jnp.exp(jnp.where(causal, spread, -1e30))).astype(bf16)
            out_ref[top:end, cols(j)] = dot(weights, value[:end])


def output_kernel(
    chunk, half, y_ref, inner_ref, query_ref, cot_ref, gain_ref, cumul_ref, mine_ref, theirs_ref,
    before_ref, out_ref, sums_ref, square_ref, product_ref,
):
    step = pl.program_id(0)
    group = jnp.where(step == 0, y_ref[0], 1 - y_ref[0])
    base = (2 * chunk + group) * half
    squares = jnp.zeros((BLOCK, HEAD_DIM), f32)
    products = jnp.zeros((BLOCK, HEAD_DIM), f32)
    for j in range(half):
        lead = jnp.exp(column(head_row(cumul_ref, base + j)))
        high, low = halves(jnp.where(step == 0, mine_ref[j], theirs_ref[j]))
        query = query_ref[:, cols(j)]
        out = inner_ref[:, cols(j)] + lead * (dot(query, high) + dot(query, low))
        out_ref[:, cols(j)] = out
        squares += out * out
        products += cot_ref[:, cols(j)].astype(f32) * gain_ref[:, cols(j)] * out

    @pl.when(step == 0)
    def _():
        square_ref[...] = squares
        product_ref[...] = products

    @pl.when(step == 1)
    def _():
        rows = lax.broadcasted_iota(jnp.int32, (8, HEAD_DIM), 0)
        total = before_ref[...]
        for place, part in ((0, square_ref[...] + squares), (1, product_ref[...] + products)):
            pick = jnp.where(rows == place, 1.0, 0.0).astype(bf16)
            high, low = halves(part)
            total += dot(pick, high, NT) + dot(pick, low, NT)
        sums_ref[...] = total


def grad_kernel(
    chunk, half, features, shares, y_ref, out_ref, cot_ref, gain_ref, query_ref, cumul_ref, *refs
):
    share_refs, refs = refs[:shares], refs[shares:]
    attended_ref, grad_ref, send_ref, keep_ref = refs[-4:]
    step = pl.program_id(0)
    group = jnp.where(step == 0, 1 - y_ref[0], y_ref[0])
    base = (2 * chunk + group) * half
    sums = share_refs[0][...]
    for share in share_refs[1:]:
        sums = sums + share[...]
    inverse = lax.rsqrt(sums[0:1] / features + epsilon)
    mean_term = inverse * sums[1:2] / features
    inverse_col, mean_col = column(inverse), column(mean_term)
    found = []
    for j in range(half):
        gain = gain_ref[:, cols(j)]
        normed = out_ref[:, cols(j)] * inverse_col
        attended_ref[:, cols(j)] = (normed * gain).astype(bf16)
        scaled_grad = cot_ref[:, cols(j)].astype(f32) * gain
        grad = (inverse_col * (scaled_grad - normed * mean_col)).astype(bf16)
        grad_ref[:, cols(j)] = grad
        row = head_row(cumul_ref, base + j)
        found.append(outer_sum(query_ref[:, cols(j)], jnp.exp(row), grad))

    @pl.when(step == 0)
    def _():
        for j in range(half):
            send_ref[j] = found[j]

    @pl.when(step == 1)
    def _():
        for j in range(half):
            keep_ref[j] = found[j]


def backward_kernel(
    chunk, half, y_ref, query_ref, key_ref, value_ref, grad_ref, cumul_ref, mine_ref, theirs_ref, *refs
):
    grad_query_ref, inner_key_ref, inner_value_ref = refs[-3:]
    step = pl.program_id(0)
    group = jnp.where(step == 0, y_ref[0], 1 - y_ref[0])
    base = (2 * chunk + group) * half
    for j in range(half):
        row = head_row(cumul_ref, base + j)
        col = column(row)
        query, key = query_ref[:, cols(j)], key_ref[:, cols(j)]
        value, grad = value_ref[:, cols(j)], grad_ref[:, cols(j)]
        high, low = halves(jnp.where(step == 0, mine_ref[j], theirs_ref[j]))
        outer = jnp.exp(col) * (dot(grad, high, NT) + dot(grad, low, NT))
        for top in range(0, BLOCK, TILE):
            end = top + TILE
            scores = dot(key[top:end], query[top:], NT)
            grad_scores = dot(value[top:end], grad[top:], NT)
            spread = row[:, top:] - wide(col[top:end], BLOCK - top)
            causal = lax.broadcasted_iota(jnp.int32, spread.shape, 0) <= (
                lax.broadcasted_iota(jnp.int32, spread.shape, 1)
            )
            decays = jnp.exp(jnp.where(causal, spread, -1e30))
            weights = (scores * decays).astype(bf16)
            grad_weights = (grad_scores * decays).astype(bf16)
            inner_value_ref[top:end, cols(j)] = dot(weights, grad[top:])
            inner_key_ref[top:end, cols(j)] = dot(grad_weights, query[top:])
            part = dot(grad_weights, key[top:end], TN)
            outer = part + outer if top == 0 else jnp.concatenate(
                [outer[:top], outer[top:] + part], axis=0
            )
        grad_query_ref[:, cols(j)] = outer.astype(bf16)


def final_kernel(
    chunk, half, y_ref, inner_key_ref, inner_value_ref, key_ref, value_ref, cumul_ref, mine_ref,
    theirs_ref, *refs,
):
    grad_key_ref, grad_value_ref = refs[-2:]
    step = pl.program_id(0)
    group = jnp.where(step == 0, y_ref[0], 1 - y_ref[0])
    base = (2 * chunk + group) * half
    for j in range(half):
        trail = column(trail_row(head_row(cumul_ref, base + j)))
        high, low = halves(jnp.where(step == 0, mine_ref[j], theirs_ref[j]))
        key, value = key_ref[:, cols(j)], value_ref[:, cols(j)]
        grad_key_ref[:, cols(j)] = (
            inner_key_ref[:, cols(j)] + trail * (dot(value, high, NT) + dot(value, low, NT))
        ).astype(bf16)
        grad_value_ref[:, cols(j)] = (
            inner_value_ref[:, cols(j)] + trail * (dot(key, high) + dot(key, low))
        ).astype(bf16)


def chain(sends, keeps, first, place, places, forward, first_decay, second_decay):
    count = len(sends)

    def device(where, member):
        return 2 * (where if forward else places - 1 - where) + member

    swap = [(2 * p + m, 2 * p + 1 - m) for p in range(places) for m in (0, 1)]
    received = [lax.ppermute(send, "seq", swap) for send in sends]
    firsts = [jnp.where(first, keep, got) for keep, got in zip(keeps, received)]
    pair_sums = [
        second_decay[c] * firsts[c] + jnp.where(first, received[c], keeps[c]) for c in range(count)
    ]
    pair_decay = first_decay * second_decay
    arrived = {}
    for step in range(2, count + places):
        senders = [p for p in range(places - 1) if 0 <= step - 2 - p < count]
        value = None
        for p in senders:
            c = step - 2 - p
            if p == 0:
                here = pair_sums[c]
            else:
                here = pair_decay[c] * arrived[step - 1] + pair_sums[c]
            value = here if value is None else jnp.where(place == p, here, value)
        pairs = [(device(p, m), device(p + 1, m)) for p in senders for m in (0, 1)]
        arrived[step] = lax.ppermute(value, "seq", pairs)
    mine, theirs = [], []
    for c in range(count):
        before = jnp.zeros_like(keeps[c])
        for p in range(1, places):
            before = jnp.where(place == p, arrived[c + 1 + p], before)
        after_first = first_decay[c] * before + firsts[c]
        mine.append(jnp.where(first, before, after_first))
        theirs.append(lax.ppermute(jnp.where(first, after_first, before), "seq", swap))
    return mine, theirs


def on_device(queries, key_vecs, value_vecs, log_decay, norm_gain, cotangent):
    tokens, width = queries.shape
    assert tokens == BLOCK
    heads = width // HEAD_DIM
    half = heads // (2 * CHUNKS)
    features = width * lax.axis_size("head")
    seq_count = lax.axis_size("seq")
    places = seq_count // 2
    my_index = lax.axis_index("seq")
    member = my_index % 2
    pair = my_index // 2
    member_ref = member.astype(jnp.int32).reshape(1)
    gain = norm_gain.reshape(1, width)

    group_width = half * HEAD_DIM
    state_shape = (half, HEAD_DIM, HEAD_DIM)
    state = jax.ShapeDtypeStruct(state_shape, f32)
    whole = jax.ShapeDtypeStruct((tokens, width), bf16)
    part = jax.ShapeDtypeStruct((tokens, 2 * group_width), f32)
    part_low = jax.ShapeDtypeStruct((tokens, 2 * group_width), bf16)
    sums_shape = jax.ShapeDtypeStruct((8, tokens), f32)
    any_spec = pl.BlockSpec(memory_space=pl.ANY)

    def fixed(shape):
        return pl.BlockSpec(shape, lambda i, y: (0,) * len(shape))

    def group_of(order, i, y):
        if order == "mine":
            return jnp.where(i == 0, y[0], 1 - y[0])
        if order == "theirs":
            return jnp.where(i == 0, 1 - y[0], y[0])
        return i

    def full(chunk, order, rows=tokens):
        return pl.BlockSpec((rows, group_width), lambda i, y: (0, 2 * chunk + group_of(order, i, y)))

    def local(order):
        return pl.BlockSpec((tokens, group_width), lambda i, y: (0, group_of(order, i, y)))

    def run(kernel, chunk, in_specs, out_specs, out_shape, args, scratch=(), aliases=None, cost=1.0):
        def body(y_ref, *refs):
            kernel(chunk, half, y_ref, *refs)

        return pl.pallas_call(
            body,
            out_shape=out_shape,
            grid_spec=pltpu.PrefetchScalarGridSpec(
                num_scalar_prefetch=1,
                grid=(2,),
                in_specs=in_specs,
                out_specs=out_specs,
                scratch_shapes=list(scratch),
            ),
            input_output_aliases=aliases or {},
            compiler_params=pltpu.CompilerParams(vmem_limit_bytes=32 * 1024 * 1024),
            cost_estimate=pl.CostEstimate(
                flops=int(cost * 1e9), bytes_accessed=int(cost * 2.5e6), transcendentals=0
            ),
        )(member_ref, *args)

    cumul = pl.pallas_call(
        cumul_kernel, out_shape=jax.ShapeDtypeStruct((heads, tokens), f32)
    )(log_decay)
    cumul_spec = fixed((heads, tokens))
    state_spec = fixed(state_shape)

    own_decay = jnp.exp(cumul[:, -1])
    swap = [(i, i ^ 1) for i in range(seq_count)]
    other_decay = jnp.exp(lax.ppermute(cumul[:, -1], "seq", swap))

    def kept(vector):
        grouped = vector.reshape(CHUNKS, 2, half)
        return jnp.where(member == 0, grouped[:, 0], grouped[:, 1])[:, :, None, None]

    low_decay = kept(jnp.where(member == 0, own_decay, other_decay))
    high_decay = kept(jnp.where(member == 0, other_decay, own_decay))

    sends, keeps = [], []
    for c in range(CHUNKS):
        send, keep = run(
            pieces_kernel, c, [full(c, "theirs"), full(c, "theirs"), cumul_spec],
            [state_spec] * 2, [state] * 2, (key_vecs, value_vecs, cumul), cost=1.5,
        )
        sends.append(send)
        keeps.append(keep)
    mine, theirs = chain(
        sends, keeps, member == 0, pair, places, True, low_decay, high_decay
    )
    inner = [
        run(
            lambda chunk, half, y_ref, *refs: inner_kernel(chunk, half, *refs), c,
            [full(c, "")] * 3 + [cumul_spec], local(""), part,
            (queries, key_vecs, value_vecs, cumul), cost=2.5,
        )
        for c in range(CHUNKS)
    ]

    sums = jnp.zeros(sums_shape.shape, f32)
    outs = []
    for c in range(CHUNKS):
        out, sums = run(
            output_kernel, c,
            [local("mine"), full(c, "mine"), full(c, "mine"), full(c, "mine", 1), cumul_spec,
             state_spec, state_spec, fixed(sums_shape.shape)],
            [local("mine"), fixed(sums_shape.shape)], [part, sums_shape],
            (inner[c], queries, cotangent, gain, cumul, mine[c], theirs[c], sums),
            scratch=[pltpu.VMEM((tokens, HEAD_DIM), f32)] * 2, cost=1.5,
        )
        outs.append(out)

    head_count = lax.axis_size("head")
    shares = [sums] + [
        lax.ppermute(sums, "head", [(i, (i + k) % head_count) for i in range(head_count)])
        for k in range(1, head_count)
    ]

    sends, keeps, grads = [], [], []
    attended = None
    for c in range(CHUNKS):
        before = [] if attended is None else [attended]
        attended, grad, send, keep = run(
            lambda chunk, half, *refs: grad_kernel(chunk, half, features, head_count, *refs), c,
            [local("theirs"), full(c, "theirs"), full(c, "theirs", 1), full(c, "theirs"), cumul_spec]
            + [fixed(sums_shape.shape)] * head_count + [any_spec] * len(before),
            [full(c, "theirs"), local("theirs"), state_spec, state_spec],
            [whole, part_low, state, state],
            (outs[c], cotangent, gain, queries, cumul, *shares, *before),
            aliases={6 + head_count: 0} if before else None, cost=1.5,
        )
        sends.append(send)
        keeps.append(keep)
        grads.append(grad)
    mine_after, theirs_after = chain(
        sends, keeps, member == 1, places - 1 - pair, places, False, high_decay, low_decay
    )

    grad_queries = None
    inner_grads = []
    for c in range(CHUNKS):
        before = [] if grad_queries is None else [grad_queries]
        grad_queries, inner_key, inner_value = run(
            backward_kernel, c,
            [full(c, "mine")] * 3 + [local("mine"), cumul_spec, state_spec, state_spec]
            + [any_spec] * len(before),
            [full(c, "mine"), local("mine"), local("mine")], [whole, part, part],
            (queries, key_vecs, value_vecs, grads[c], cumul, mine[c], theirs[c], *before),
            aliases={8: 0} if before else None, cost=4.0,
        )
        inner_grads.append((inner_key, inner_value))

    grad_keys = grad_values = None
    for c in range(CHUNKS):
        before = [] if grad_keys is None else [grad_keys, grad_values]
        grad_keys, grad_values = run(
            final_kernel, c,
            [local("mine")] * 2 + [full(c, "mine")] * 2 + [cumul_spec, state_spec, state_spec]
            + [any_spec] * len(before),
            [full(c, "mine")] * 2, [whole] * 2,
            (*inner_grads[c], key_vecs, value_vecs, cumul, mine_after[c], theirs_after[c], *before),
            aliases={8: 0, 9: 1} if before else None, cost=1.5,
        )
    return attended, grad_queries, grad_keys, grad_values


def solution(mesh):
    return jax.shard_map(
        on_device,
        mesh=mesh,
        in_specs=(
            P("seq", "head"),
            P("seq", "head"),
            P("seq", "head"),
            P("seq", "head"),
            P("head"),
            P("seq", "head"),
        ),
        out_specs=(P("seq", "head"), P("seq", "head"), P("seq", "head"), P("seq", "head")),
        check_vma=False,
    )
```

profile of v0, /device:TPU:0, one launch (start us, length us, event | category | flops | bytes accessed | tf_op | source)
XLA Modules:
  0.0 148.0 jit_solution(3292608968218640053)
XLA Ops:
  0.6 1.6 %copy.23.decay_ref = f32[512,16]{1,0:T(8,128)} copy(f32[512,16]{0,1:T(8,128)} %param.9) | data formatting | bytes 65536 | tf_op args[3]
  2.2 1.9 %shard_map.93.refs_3_.refs_2_.refs_4_ = f32[16,512]{1,0:T(8,128)} custom-call(f32[512,16]{1,0:T(8,128)} %copy.23.decay_ref), custom_call_target="tpu_custom_call" | custom-call | tf_op jit(solution)/shard_map/pallas_call | solution.py:330
  5.0 3.0 %collective-permute-start = (f32[16]{0:T(128)S(1)}, f32[16]{0:T(128)S(1)}, u32[]{:S(2)}, u32[]{:S(2)}) collective-permute-start(f32[16]{0:T(128)S(1)} %slice_reduce_fusion), channel_id=1, source_target_pairs={{0,4},{4,0},{8,12},{12,8},{16,20},{20,16},{24,28},{28,24},{1,5},{5... | collective-permute-start | bytes 200 | tf_op jit(solution)/shard_map/ppermute | solution.py:338
  14.0 2.1 %collective-permute-start.3 = (f32[2,128,128]{2,1,0:T(8,128)S(1)}, f32[2,128,128]{2,1,0:T(8,128)}, u32[]{:S(2)}, u32[]{:S(2)}) collective-permute-start(f32[2,128,128]{2,1,0:T(8,128)S(1)} %get-tuple-element.59), channel_id=1, source_target_pairs={{0,4},{4,0},{8,12},{12,8},{16,20},{20,16},{24,28},{28,24},{1,5},{5... | collective-permute-start | bytes 393224 | tf_op jit(solution)/shard_map/ppermute | solution.py:240
  18.1 2.1 %collective-permute-start.7 = (f32[2,128,128]{2,1,0:T(8,128)S(1)}, f32[2,128,128]{2,1,0:T(8,128)S(1)}, u32[]{:S(2)}, u32[]{:S(2)}) collective-permute-start(f32[2,128,128]{2,1,0:T(8,128)S(1)} %get-tuple-element.63), channel_id=1, source_target_pairs={{0,4},{4,0},{8,12},{12,8},{16,20},{20,16},{24,28},{28,24},{1,5},{5... | collective-permute-start | bytes 393224 | tf_op jit(solution)/shard_map/ppermute | solution.py:240
  23.3 2.1 %shard_map.101.refs_0_ = f32[512,512]{1,0:T(8,128)S(1)} custom-call(s32[1]{0:T(128)} %bitcast.y_ref, bf16[512,2048]{1,0:T(8,128)(2,1)S(1)} %copy-done.1, bf16[512,2048]{1,0:T(8,128)(2,1)S(1)} %copy-done.5, bf16[512,2048]{1,0:T(8,128)(2,1)S(1)} %copy-done.9, f32[16,512]{1,0:T(8,128)S(1)} %copy-done.13), custom_call_target="tpu_custom_call" | custom-call | flops 2500000000 | bytes 6250000 | tf_op jit(solution)/shard_map/pallas_call | solution.py:313
  26.8 3.5 %collective-permute-start.2 = (f32[2,128,128]{2,1,0:T(8,128)S(1)}, f32[2,128,128]{2,1,0:T(8,128)S(1)}, u32[]{:S(2)}, u32[]{:S(2)}) collective-permute-start(f32[2,128,128]{2,1,0:T(8,128)S(1)} %select_add_fusion.7), channel_id=1, source_target_pairs={{0,8},{4,12},{1,9},{5,13},{2,10},{6,14},{3,11},{7,15}} | collective-permute-start | bytes 393224 | tf_op jit(solution)/shard_map/ppermute | solution.py:258
  30.3 2.5 %collective-permute-done.2 = f32[2,128,128]{2,1,0:T(8,128)S(1)} collective-permute-done((f32[2,128,128]{2,1,0:T(8,128)S(1)}, f32[2,128,128]{2,1,0:T(8,128)S(1)}, u32[]{:S(2)}, u32[]{:S(2)}) %collective-permute-start.2) | collective-permute-done | bytes 131104 | tf_op jit(solution)/shard_map/ppermute | solution.py:258
  33.8 4.4 %collective-permute-start.4 = (f32[2,128,128]{2,1,0:T(8,128)S(1)}, f32[2,128,128]{2,1,0:T(8,128)S(1)}, u32[]{:S(2)}, u32[]{:S(2)}) collective-permute-start(f32[2,128,128]{2,1,0:T(8,128)S(1)} %get-tuple-element.134), channel_id=1, source_target_pairs={{0,8},{4,12},{8,16},{12,20},{1,9},{5,13},{9,17},{13,21},{2,10},{6,... | collective-permute-start | bytes 393224 | tf_op jit(solution)/shard_map/ppermute | solution.py:258
  41.3 2.2 %shard_map.100.refs_0_ = f32[512,512]{1,0:T(8,128)S(1)} custom-call(s32[1]{0:T(128)} %bitcast.y_ref, bf16[512,2048]{1,0:T(8,128)(2,1)S(1)} %copy-done.1, bf16[512,2048]{1,0:T(8,128)(2,1)S(1)} %copy-done.6, bf16[512,2048]{1,0:T(8,128)(2,1)S(1)} %copy-done.10, f32[16,512]{1,0:T(8,128)S(1)} %copy-done.13), custom_call_target="tpu_custom_call" | custom-call | flops 2500000000 | bytes 6250000 | tf_op jit(solution)/shard_map/pallas_call | solution.py:313
  44.6 1.9 %collective-permute-start.6 = (f32[2,128,128]{2,1,0:T(8,128)S(1)}, f32[2,128,128]{2,1,0:T(8,128)S(1)}, u32[]{:S(2)}, u32[]{:S(2)}) collective-permute-start(f32[2,128,128]{2,1,0:T(8,128)S(1)} %get-tuple-element.132), channel_id=1, source_target_pairs={{0,8},{4,12},{8,16},{12,20},{16,24},{20,28},{1,9},{5,13},{9,17},{1... | collective-permute-start | bytes 393224 | tf_op jit(solution)/shard_map/ppermute | solution.py:258
  46.5 2.2 %shard_map.99.refs_0_ = f32[512,512]{1,0:T(8,128)S(1)} custom-call(s32[1]{0:T(128)} %bitcast.y_ref, bf16[512,2048]{1,0:T(8,128)(2,1)S(1)} %copy-done.1, bf16[512,2048]{1,0:T(8,128)(2,1)S(1)} %copy-done.6, bf16[512,2048]{1,0:T(8,128)(2,1)S(1)} %copy-done.10, f32[16,512]{1,0:T(8,128)S(1)} %copy-done.13), custom_call_target="tpu_custom_call" | custom-call | flops 2500000000 | bytes 6250000 | tf_op jit(solution)/shard_map/pallas_call | solution.py:313
  49.1 4.4 %collective-permute-start.8 = (f32[2,128,128]{2,1,0:T(8,128)S(1)}, f32[2,128,128]{2,1,0:T(8,128)S(1)}, u32[]{:S(2)}, u32[]{:S(2)}) collective-permute-start(f32[2,128,128]{2,1,0:T(8,128)S(1)} %get-tuple-element.130), channel_id=1, source_target_pairs={{0,8},{4,12},{8,16},{12,20},{16,24},{20,28},{1,9},{5,13},{9,17},{1... | collective-permute-start | bytes 393224 | tf_op jit(solution)/shard_map/ppermute | solution.py:258
  53.5 2.2 %shard_map.94.refs_0_ = f32[512,512]{1,0:T(8,128)S(1)} custom-call(s32[1]{0:T(128)} %bitcast.y_ref, bf16[512,2048]{1,0:T(8,128)(2,1)S(1)} %copy-done.1, bf16[512,2048]{1,0:T(8,128)(2,1)S(1)} %copy-done.6, bf16[512,2048]{1,0:T(8,128)(2,1)S(1)} %copy-done.10, f32[16,512]{1,0:T(8,128)S(1)} %copy-done.13), custom_call_target="tpu_custom_call" | custom-call | flops 2500000000 | bytes 6250000 | tf_op jit(solution)/shard_map/pallas_call | solution.py:313
  57.0 1.7 %collective-permute-start.14 = (f32[2,128,128]{2,1,0:T(8,128)S(1)}, f32[2,128,128]{2,1,0:T(8,128)S(1)}, u32[]{:S(2)}, u32[]{:S(2)}) collective-permute-start(f32[2,128,128]{2,1,0:T(8,128)S(1)} %get-tuple-element.122), channel_id=1, source_target_pairs={{0,4},{4,0},{8,12},{12,8},{16,20},{20,16},{24,28},{28,24},{1,5},{5... | collective-permute-start | bytes 393224 | tf_op jit(solution)/shard_map/ppermute | solution.py:266
  59.8 1.7 %collective-permute-start.12 = (f32[2,128,128]{2,1,0:T(8,128)S(1)}, f32[2,128,128]{2,1,0:T(8,128)S(1)}, u32[]{:S(2)}, u32[]{:S(2)}) collective-permute-start(f32[2,128,128]{2,1,0:T(8,128)S(1)} %get-tuple-element.145), channel_id=1, source_target_pairs={{0,4},{4,0},{8,12},{12,8},{16,20},{20,16},{24,28},{28,24},{1,5},{5... | collective-permute-start | bytes 393224 | tf_op jit(solution)/shard_map/ppermute | solution.py:266
  76.4 2.2 %shard_map.106 = (bf16[512,2048]{1,0:T(8,128)(2,1)}, bf16[512,512]{1,0:T(8,128)(2,1)S(1)}, f32[2,128,128]{2,1,0:T(8,128)S(1)}, f32[2,128,128]{2,1,0:T(8,128)S(1)}) custom-call(s32[1]{0:T(128)} %bitcast.y_ref, f32[512,512]{1,0:T(8,128)S(1)} %copy-done.34, bf16[512,2048]{1,0:T(8,128)(2,1)S(1)} %copy-done, f32[1,2048]{1,0:T(1,128)S(1)} %bitcast.30, ...), custom_call_target="tpu_custom_call" | custom-call | flops 1500000000 | bytes 3750000 | tf_op jit(solution)/shard_map/pallas_call | solution.py:313
  78.6 1.6 %collective-permute-start.18 = (f32[2,128,128]{2,1,0:T(8,128)S(1)}, f32[2,128,128]{2,1,0:T(8,128)S(1)}, u32[]{:S(2)}, u32[]{:S(2)}) collective-permute-start(f32[2,128,128]{2,1,0:T(8,128)S(1)} %get-tuple-element.87), channel_id=1, source_target_pairs={{0,4},{4,0},{8,12},{12,8},{16,20},{20,16},{24,28},{28,24},{1,5},{5... | collective-permute-start | bytes 393224 | tf_op jit(solution)/shard_map/ppermute | solution.py:240
  80.2 2.2 %shard_map.107 = (bf16[512,2048]{1,0:T(8,128)(2,1)}, bf16[512,512]{1,0:T(8,128)(2,1)S(1)}, f32[2,128,128]{2,1,0:T(8,128)S(1)}, f32[2,128,128]{2,1,0:T(8,128)S(1)}) custom-call(s32[1]{0:T(128)} %bitcast.y_ref, f32[512,512]{1,0:T(8,128)S(1)} %copy-done.19, bf16[512,2048]{1,0:T(8,128)(2,1)S(1)} %copy-done, ...), custom_call_target="tpu_custom_call", output_to_operand_aliasing={{0}: (10, {})} | custom-call | flops 1500000000 | bytes 3750000 | tf_op jit(solution)/shard_map/pallas_call | solution.py:313
  82.8 2.2 %shard_map.108 = (bf16[512,2048]{1,0:T(8,128)(2,1)}, bf16[512,512]{1,0:T(8,128)(2,1)S(1)}, f32[2,128,128]{2,1,0:T(8,128)S(1)}, f32[2,128,128]{2,1,0:T(8,128)S(1)}) custom-call(s32[1]{0:T(128)} %bitcast.y_ref, f32[512,512]{1,0:T(8,128)S(1)} %copy-done.17, bf16[512,2048]{1,0:T(8,128)(2,1)S(1)} %copy-done, ...), custom_call_target="tpu_custom_call", output_to_operand_aliasing={{0}: (10, {})} | custom-call | flops 1500000000 | bytes 3750000 | tf_op jit(solution)/shard_map/pallas_call | solution.py:313
  84.9 1.6 %collective-permute-start.22 = (f32[2,128,128]{2,1,0:T(8,128)S(1)}, f32[2,128,128]{2,1,0:T(8,128)S(1)}, u32[]{:S(2)}, u32[]{:S(2)}) collective-permute-start(f32[2,128,128]{2,1,0:T(8,128)S(1)} %get-tuple-element.91), channel_id=1, source_target_pairs={{0,4},{4,0},{8,12},{12,8},{16,20},{20,16},{24,28},{28,24},{1,5},{5... | collective-permute-start | bytes 393224 | tf_op jit(solution)/shard_map/ppermute | solution.py:240
  87.3 2.2 %shard_map.109 = (bf16[512,2048]{1,0:T(8,128)(2,1)}, bf16[512,512]{1,0:T(8,128)(2,1)S(1)}, f32[2,128,128]{2,1,0:T(8,128)S(1)}, f32[2,128,128]{2,1,0:T(8,128)S(1)}) custom-call(s32[1]{0:T(128)} %bitcast.y_ref, f32[512,512]{1,0:T(8,128)S(1)} %get-tuple-element.67.refs_0_, bf16[512,2048]{1,0:T(8,128)(2,1)S(1)} %copy-done, ...), custom_call_target="tpu_custom_call", output_to_operand_aliasing={{0}: (10, {})} | custom-call | flops 1500000000 | bytes 3750000 | tf_op jit(solution)/shard_map/pallas_call | solution.py:313
  90.8 4.4 %shard_map.110 = (bf16[512,2048]{1,0:T(8,128)(2,1)}, f32[512,512]{1,0:T(8,128)S(1)}, f32[512,512]{1,0:T(8,128)S(1)}) custom-call(s32[1]{0:T(128)} %bitcast.y_ref, bf16[512,2048]{1,0:T(8,128)(2,1)S(1)} %copy-done.3, bf16[512,2048]{1,0:T(8,128)(2,1)S(1)} %copy-done.7, bf16[512,2048]{1,0:T(8,128)(2,1)S(1)} %copy-done.11, ...), custom_call_target="tpu_custom_call" | custom-call | flops 4000000000 | bytes 10000000 | tf_op jit(solution)/shard_map/pallas_call | solution.py:313
  96.6 4.3 %shard_map.111 = (bf16[512,2048]{1,0:T(8,128)(2,1)}, f32[512,512]{1,0:T(8,128)S(1)}, f32[512,512]{1,0:T(8,128)S(1)}) custom-call(s32[1]{0:T(128)} %bitcast.y_ref, bf16[512,2048]{1,0:T(8,128)(2,1)S(1)} %copy-done.3, bf16[512,2048]{1,0:T(8,128)(2,1)S(1)} %copy-done.7, bf16[512,2048]{1,0:T(8,128)(2,1)S(1)} %copy-done.11, ...), custom_call_target="tpu_custom_call", output_to_operand_aliasing={{0}: (8, {})} | custom-call | flops 4000000000 | bytes 10000000 | tf_op jit(solution)/shard_map/pallas_call | solution.py:313
  100.9 13.4 %collective-permute-done.23 = f32[2,128,128]{2,1,0:T(8,128)S(1)} collective-permute-done((f32[2,128,128]{2,1,0:T(8,128)S(1)}, f32[2,128,128]{2,1,0:T(8,128)S(1)}, u32[]{:S(2)}, u32[]{:S(2)}) %collective-permute-start.23) | collective-permute-done | bytes 131104 | tf_op jit(solution)/shard_map/ppermute | solution.py:258
  115.8 4.3 %shard_map.112 = (bf16[512,2048]{1,0:T(8,128)(2,1)}, f32[512,512]{1,0:T(8,128)S(1)}, f32[512,512]{1,0:T(8,128)S(1)}) custom-call(s32[1]{0:T(128)} %bitcast.y_ref, bf16[512,2048]{1,0:T(8,128)(2,1)S(1)} %copy-done.3, bf16[512,2048]{1,0:T(8,128)(2,1)S(1)} %copy-done.7, bf16[512,2048]{1,0:T(8,128)(2,1)S(1)} %copy-done.11, ...), custom_call_target="tpu_custom_call", output_to_operand_aliasing={{0}: (8, {})} | custom-call | flops 4000000000 | bytes 10000000 | tf_op jit(solution)/shard_map/pallas_call | solution.py:313
  122.7 4.4 %shard_map.113 = (bf16[512,2048]{1,0:T(8,128)(2,1)}, f32[512,512]{1,0:T(8,128)S(1)}, f32[512,512]{1,0:T(8,128)S(1)}) custom-call(s32[1]{0:T(128)} %bitcast.y_ref, bf16[512,2048]{1,0:T(8,128)(2,1)S(1)} %copy-done.3, bf16[512,2048]{1,0:T(8,128)(2,1)S(1)} %copy-done.7, bf16[512,2048]{1,0:T(8,128)(2,1)S(1)} %copy-done.11, ...), custom_call_target="tpu_custom_call", output_to_operand_aliasing={{0}: (8, {})} | custom-call | flops 4000000000 | bytes 10000000 | tf_op jit(solution)/shard_map/pallas_call | solution.py:313
  133.1 5.1 %collective-permute-done.27 = f32[2,128,128]{2,1,0:T(8,128)S(1)} collective-permute-done((f32[2,128,128]{2,1,0:T(8,128)S(1)}, f32[2,128,128]{2,1,0:T(8,128)S(1)}, u32[]{:S(2)}, u32[]{:S(2)}) %collective-permute-start.27) | collective-permute-done | bytes 131104 | tf_op jit(solution)/shard_map/ppermute | solution.py:258
  139.8 2.1 %shard_map.114 = (bf16[512,2048]{1,0:T(8,128)(2,1)}, bf16[512,2048]{1,0:T(8,128)(2,1)}) custom-call(s32[1]{0:T(128)} %bitcast.y_ref, f32[512,512]{1,0:T(8,128)S(1)} %get-tuple-element.98.refs_0_, f32[512,512]{1,0:T(8,128)S(1)} %get-tuple-element.99.refs_1_, bf16[512,2048]{1,0:T(8,128)(2,1)S(1)} %copy-done.7, bf16[512,2048]{1,0:T(8,128)(2,1)S(1)} %copy-done.11, ...), custom_call_target="tpu_custom_call" | custom-call | flops 1500000000 | bytes 3750000 | tf_op jit(solution)/shard_map/pallas_call | solution.py:313
  141.8 2.0 %shard_map.115 = (bf16[512,2048]{1,0:T(8,128)(2,1)}, bf16[512,2048]{1,0:T(8,128)(2,1)}) custom-call(s32[1]{0:T(128)} %bitcast.y_ref, f32[512,512]{1,0:T(8,128)S(1)} %get-tuple-element.96.refs_0_, f32[512,512]{1,0:T(8,128)S(1)} %get-tuple-element.97.refs_1_, bf16[512,2048]{1,0:T(8,128)(2,1)S(1)} %copy-done.7, ...), custom_call_target="tpu_custom_call", output_to_operand_aliasing={{0}: (8, {}), {1}: (9, {})} | custom-call | flops 1500000000 | bytes 3750000 | tf_op jit(solution)/shard_map/pallas_call | solution.py:313
  143.9 2.0 %shard_map.116 = (bf16[512,2048]{1,0:T(8,128)(2,1)}, bf16[512,2048]{1,0:T(8,128)(2,1)}) custom-call(s32[1]{0:T(128)} %bitcast.y_ref, f32[512,512]{1,0:T(8,128)S(1)} %get-tuple-element.94.refs_0_, f32[512,512]{1,0:T(8,128)S(1)} %get-tuple-element.95.refs_1_, bf16[512,2048]{1,0:T(8,128)(2,1)S(1)} %copy-done.7, ...), custom_call_target="tpu_custom_call", output_to_operand_aliasing={{0}: (8, {}), {1}: (9, {})} | custom-call | flops 1500000000 | bytes 3750000 | tf_op jit(solution)/shard_map/pallas_call | solution.py:313
  145.9 2.0 %shard_map.117 = (bf16[512,2048]{1,0:T(8,128)(2,1)}, bf16[512,2048]{1,0:T(8,128)(2,1)}) custom-call(s32[1]{0:T(128)} %bitcast.y_ref, f32[512,512]{1,0:T(8,128)S(1)} %get-tuple-element.84.refs_0_, f32[512,512]{1,0:T(8,128)S(1)} %get-tuple-element.85.refs_1_, bf16[512,2048]{1,0:T(8,128)(2,1)S(1)} %copy-done.7, ...), custom_call_target="tpu_custom_call", output_to_operand_aliasing={{0}: (8, {}), {1}: (9, {})} | custom-call | flops 1500000000 | bytes 3750000 | tf_op jit(solution)/shard_map/pallas_call | solution.py:313
  (171 shorter events, 51.3 us)
Async XLA Ops:
  5.0 21.5 %collective-permute-start = (f32[16]{0:T(128)S(1)}, f32[16]{0:T(128)S(1)}, u32[]{:S(2)}, u32[]{:S(2)}) collective-permute-start(f32[16]{0:T(128)S(1)} %slice_reduce_fusion), channel_id=1, source_target_pairs={{0,4},{4,0},{8,12},{12,8},{16,20},{20,16},{24,28},{28,24},{1,5},{5... | collective-permute-start | bytes 200 | tf_op jit(solution)/shard_map/ppermute | solution.py:338
  12.9 13.8 %collective-permute-start.1 = (f32[2,128,128]{2,1,0:T(8,128)S(1)}, f32[2,128,128]{2,1,0:T(8,128)S(1)}, u32[]{:S(2)}, u32[]{:S(2)}) collective-permute-start(f32[2,128,128]{2,1,0:T(8,128)S(1)} %get-tuple-element.57), channel_id=1, source_target_pairs={{0,4},{4,0},{8,12},{12,8},{16,20},{20,16},{24,28},{28,24},{1,5},{5... | collective-permute-start | bytes 393224 | tf_op jit(solution)/shard_map/ppermute | solution.py:240
  14.0 16.3 %collective-permute-start.3 = (f32[2,128,128]{2,1,0:T(8,128)S(1)}, f32[2,128,128]{2,1,0:T(8,128)}, u32[]{:S(2)}, u32[]{:S(2)}) collective-permute-start(f32[2,128,128]{2,1,0:T(8,128)S(1)} %get-tuple-element.59), channel_id=1, source_target_pairs={{0,4},{4,0},{8,12},{12,8},{16,20},{20,16},{24,28},{28,24},{1,5},{5... | collective-permute-start | bytes 393224 | tf_op jit(solution)/shard_map/ppermute | solution.py:240
  17.0 26.5 %collective-permute-start.5 = (f32[2,128,128]{2,1,0:T(8,128)S(1)}, f32[2,128,128]{2,1,0:T(8,128)}, u32[]{:S(2)}, u32[]{:S(2)}) collective-permute-start(f32[2,128,128]{2,1,0:T(8,128)S(1)} %get-tuple-element.61), channel_id=1, source_target_pairs={{0,4},{4,0},{8,12},{12,8},{16,20},{20,16},{24,28},{28,24},{1,5},{5... | collective-permute-start | bytes 393224 | tf_op jit(solution)/shard_map/ppermute | solution.py:240
  18.1 30.6 %collective-permute-start.7 = (f32[2,128,128]{2,1,0:T(8,128)S(1)}, f32[2,128,128]{2,1,0:T(8,128)S(1)}, u32[]{:S(2)}, u32[]{:S(2)}) collective-permute-start(f32[2,128,128]{2,1,0:T(8,128)S(1)} %get-tuple-element.63), channel_id=1, source_target_pairs={{0,4},{4,0},{8,12},{12,8},{16,20},{20,16},{24,28},{28,24},{1,5},{5... | collective-permute-start | bytes 393224 | tf_op jit(solution)/shard_map/ppermute | solution.py:240
  26.8 6.0 %collective-permute-start.2 = (f32[2,128,128]{2,1,0:T(8,128)S(1)}, f32[2,128,128]{2,1,0:T(8,128)S(1)}, u32[]{:S(2)}, u32[]{:S(2)}) collective-permute-start(f32[2,128,128]{2,1,0:T(8,128)S(1)} %select_add_fusion.7), channel_id=1, source_target_pairs={{0,8},{4,12},{1,9},{5,13},{2,10},{6,14},{3,11},{7,15}} | collective-permute-start | bytes 393224 | tf_op jit(solution)/shard_map/ppermute | solution.py:258
  33.8 9.8 %collective-permute-start.4 = (f32[2,128,128]{2,1,0:T(8,128)S(1)}, f32[2,128,128]{2,1,0:T(8,128)S(1)}, u32[]{:S(2)}, u32[]{:S(2)}) collective-permute-start(f32[2,128,128]{2,1,0:T(8,128)S(1)} %get-tuple-element.134), channel_id=1, source_target_pairs={{0,8},{4,12},{8,16},{12,20},{1,9},{5,13},{9,17},{13,21},{2,10},{6,... | collective-permute-start | bytes 393224 | tf_op jit(solution)/shard_map/ppermute | solution.py:258
  44.6 4.4 %collective-permute-start.6 = (f32[2,128,128]{2,1,0:T(8,128)S(1)}, f32[2,128,128]{2,1,0:T(8,128)S(1)}, u32[]{:S(2)}, u32[]{:S(2)}) collective-permute-start(f32[2,128,128]{2,1,0:T(8,128)S(1)} %get-tuple-element.132), channel_id=1, source_target_pairs={{0,8},{4,12},{8,16},{12,20},{16,24},{20,28},{1,9},{5,13},{9,17},{1... | collective-permute-start | bytes 393224 | tf_op jit(solution)/shard_map/ppermute | solution.py:258
  49.1 6.9 %collective-permute-start.8 = (f32[2,128,128]{2,1,0:T(8,128)S(1)}, f32[2,128,128]{2,1,0:T(8,128)S(1)}, u32[]{:S(2)}, u32[]{:S(2)}) collective-permute-start(f32[2,128,128]{2,1,0:T(8,128)S(1)} %get-tuple-element.130), channel_id=1, source_target_pairs={{0,8},{4,12},{8,16},{12,20},{16,24},{20,28},{1,9},{5,13},{9,17},{1... | collective-permute-start | bytes 393224 | tf_op jit(solution)/shard_map/ppermute | solution.py:258
  56.1 0.7 collective-permute-start.9
  57.0 6.3 %collective-permute-start.14 = (f32[2,128,128]{2,1,0:T(8,128)S(1)}, f32[2,128,128]{2,1,0:T(8,128)S(1)}, u32[]{:S(2)}, u32[]{:S(2)}) collective-permute-start(f32[2,128,128]{2,1,0:T(8,128)S(1)} %get-tuple-element.122), channel_id=1, source_target_pairs={{0,4},{4,0},{8,12},{12,8},{16,20},{20,16},{24,28},{28,24},{1,5},{5... | collective-permute-start | bytes 393224 | tf_op jit(solution)/shard_map/ppermute | solution.py:266
  58.6 6.1 %collective-permute-start.13 = (f32[2,128,128]{2,1,0:T(8,128)S(1)}, f32[2,128,128]{2,1,0:T(8,128)S(1)}, u32[]{:S(2)}, u32[]{:S(2)}) collective-permute-start(f32[2,128,128]{2,1,0:T(8,128)S(1)} %get-tuple-element.143), channel_id=1, source_target_pairs={{0,4},{4,0},{8,12},{12,8},{16,20},{20,16},{24,28},{28,24},{1,5},{5... | collective-permute-start | bytes 393224 | tf_op jit(solution)/shard_map/ppermute | solution.py:266
  59.1 2.5 %collective-permute-start.10 = (f32[2,128,128]{2,1,0:T(8,128)S(1)}, f32[2,128,128]{2,1,0:T(8,128)S(1)}, u32[]{:S(2)}, u32[]{:S(2)}) collective-permute-start(f32[2,128,128]{2,1,0:T(8,128)S(1)} %multiply_add_fusion.9), channel_id=1, source_target_pairs={{16,24},{20,28},{17,25},{21,29},{18,26},{22,30},{19,27},{23,31}} | collective-permute-start | bytes 393224 | tf_op jit(solution)/shard_map/ppermute | solution.py:258
  59.8 6.4 %collective-permute-start.12 = (f32[2,128,128]{2,1,0:T(8,128)S(1)}, f32[2,128,128]{2,1,0:T(8,128)S(1)}, u32[]{:S(2)}, u32[]{:S(2)}) collective-permute-start(f32[2,128,128]{2,1,0:T(8,128)S(1)} %get-tuple-element.145), channel_id=1, source_target_pairs={{0,4},{4,0},{8,12},{12,8},{16,20},{20,16},{24,28},{28,24},{1,5},{5... | collective-permute-start | bytes 393224 | tf_op jit(solution)/shard_map/ppermute | solution.py:266
  61.7 6.0 %collective-permute-start.11 = (f32[2,128,128]{2,1,0:T(8,128)S(1)}, f32[2,128,128]{2,1,0:T(8,128)S(1)}, u32[]{:S(2)}, u32[]{:S(2)}) collective-permute-start(f32[2,128,128]{2,1,0:T(8,128)S(1)} %get-tuple-element.128), channel_id=1, source_target_pairs={{0,4},{4,0},{8,12},{12,8},{16,20},{20,16},{24,28},{28,24},{1,5},{5... | collective-permute-start | bytes 393224 | tf_op jit(solution)/shard_map/ppermute | solution.py:266
  69.1 3.2 %collective-permute-start.15 = (f32[8,512]{1,0:T(8,128)S(1)}, f32[8,512]{1,0:T(8,128)S(1)}, u32[]{:S(2)}, u32[]{:S(2)}) collective-permute-start(f32[8,512]{1,0:T(8,128)S(1)} %get-tuple-element.68.refs_5_), channel_id=1, source_target_pairs={{0,1},{1,2},{2,3},{3,0},{4,5},{5,6},{6,7},{7,4},{8,9},{9,10},{10,1... | collective-permute-start | bytes 49160 | tf_op jit(solution)/shard_map/ppermute | solution.py:382
  69.2 3.8 %collective-permute-start.16 = (f32[8,512]{1,0:T(8,128)S(1)}, f32[8,512]{1,0:T(8,128)S(1)}, u32[]{:S(2)}, u32[]{:S(2)}) collective-permute-start(f32[8,512]{1,0:T(8,128)S(1)} %get-tuple-element.68.refs_5_), channel_id=1, source_target_pairs={{0,2},{1,3},{2,0},{3,1},{4,6},{5,7},{6,4},{7,5},{8,10},{9,11},{10,... | collective-permute-start | bytes 49160 | tf_op jit(solution)/shard_map/ppermute | solution.py:382
  70.8 2.8 %collective-permute-start.17 = (f32[8,512]{1,0:T(8,128)S(1)}, f32[8,512]{1,0:T(8,128)S(1)}, u32[]{:S(2)}, u32[]{:S(2)}) collective-permute-start(f32[8,512]{1,0:T(8,128)S(1)} %get-tuple-element.68.refs_5_), channel_id=1, source_target_pairs={{0,3},{1,0},{2,1},{3,2},{4,7},{5,4},{6,5},{7,6},{8,11},{9,8},{10,9... | collective-permute-start | bytes 49160 | tf_op jit(solution)/shard_map/ppermute | solution.py:382
  78.6 8.0 %collective-permute-start.18 = (f32[2,128,128]{2,1,0:T(8,128)S(1)}, f32[2,128,128]{2,1,0:T(8,128)S(1)}, u32[]{:S(2)}, u32[]{:S(2)}) collective-permute-start(f32[2,128,128]{2,1,0:T(8,128)S(1)} %get-tuple-element.87), channel_id=1, source_target_pairs={{0,4},{4,0},{8,12},{12,8},{16,20},{20,16},{24,28},{28,24},{1,5},{5... | collective-permute-start | bytes 393224 | tf_op jit(solution)/shard_map/ppermute | solution.py:240
  82.3 7.6 %collective-permute-start.20 = (f32[2,128,128]{2,1,0:T(8,128)S(1)}, f32[2,128,128]{2,1,0:T(8,128)S(1)}, u32[]{:S(2)}, u32[]{:S(2)}) collective-permute-start(f32[2,128,128]{2,1,0:T(8,128)S(1)} %get-tuple-element.89), channel_id=1, source_target_pairs={{0,4},{4,0},{8,12},{12,8},{16,20},{20,16},{24,28},{28,24},{1,5},{5... | collective-permute-start | bytes 393224 | tf_op jit(solution)/shard_map/ppermute | solution.py:240
  84.9 10.2 %collective-permute-start.22 = (f32[2,128,128]{2,1,0:T(8,128)S(1)}, f32[2,128,128]{2,1,0:T(8,128)S(1)}, u32[]{:S(2)}, u32[]{:S(2)}) collective-permute-start(f32[2,128,128]{2,1,0:T(8,128)S(1)} %get-tuple-element.91), channel_id=1, source_target_pairs={{0,4},{4,0},{8,12},{12,8},{16,20},{20,16},{24,28},{28,24},{1,5},{5... | collective-permute-start | bytes 393224 | tf_op jit(solution)/shard_map/ppermute | solution.py:240
  86.6 3.3 %collective-permute-start.19 = (f32[2,128,128]{2,1,0:T(8,128)S(1)}, f32[2,128,128]{2,1,0:T(8,128)S(1)}, u32[]{:S(2)}, u32[]{:S(2)}) collective-permute-start(f32[2,128,128]{2,1,0:T(8,128)S(1)} %select_add_fusion.3), channel_id=1, source_target_pairs={{24,16},{28,20},{25,17},{29,21},{26,18},{30,22},{27,19},{31,23}} | collective-permute-start | bytes 393224 | tf_op jit(solution)/shard_map/ppermute | solution.py:258
  89.5 11.4 %collective-permute-start.24 = (f32[2,128,128]{2,1,0:T(8,128)S(1)}, f32[2,128,128]{2,1,0:T(8,128)S(1)}, u32[]{:S(2)}, u32[]{:S(2)}) collective-permute-start(f32[2,128,128]{2,1,0:T(8,128)S(1)} %get-tuple-element.93), channel_id=1, source_target_pairs={{0,4},{4,0},{8,12},{12,8},{16,20},{20,16},{24,28},{28,24},{1,5},{5... | collective-permute-start | bytes 393224 | tf_op jit(solution)/shard_map/ppermute | solution.py:240
  90.1 5.1 %collective-permute-start.21 = (f32[2,128,128]{2,1,0:T(8,128)S(1)}, f32[2,128,128]{2,1,0:T(8,128)S(1)}, u32[]{:S(2)}, u32[]{:S(2)}) collective-permute-start(f32[2,128,128]{2,1,0:T(8,128)S(1)} %get-tuple-element.120), channel_id=1, source_target_pairs={{24,16},{28,20},{16,8},{20,12},{25,17},{29,21},{17,9},{21,13},{26,... | collective-permute-start | bytes 393224 | tf_op jit(solution)/shard_map/ppermute | solution.py:258
  95.3 19.1 %collective-permute-start.23 = (f32[2,128,128]{2,1,0:T(8,128)S(1)}, f32[2,128,128]{2,1,0:T(8,128)S(1)}, u32[]{:S(2)}, u32[]{:S(2)}) collective-permute-start(f32[2,128,128]{2,1,0:T(8,128)S(1)} %get-tuple-element.118), channel_id=1, source_target_pairs={{24,16},{28,20},{16,8},{20,12},{8,0},{12,4},{25,17},{29,21},{17,9}... | collective-permute-start | bytes 393224 | tf_op jit(solution)/shard_map/ppermute | solution.py:258
  114.5 6.9 %collective-permute-start.25 = (f32[2,128,128]{2,1,0:T(8,128)S(1)}, f32[2,128,128]{2,1,0:T(8,128)S(1)}, u32[]{:S(2)}, u32[]{:S(2)}) collective-permute-start(f32[2,128,128]{2,1,0:T(8,128)S(1)} %get-tuple-element.116), channel_id=1, source_target_pairs={{24,16},{28,20},{16,8},{20,12},{8,0},{12,4},{25,17},{29,21},{17,9}... | collective-permute-start | bytes 393224 | tf_op jit(solution)/shard_map/ppermute | solution.py:258
  121.4 6.9 %collective-permute-start.26 = (f32[2,128,128]{2,1,0:T(8,128)S(1)}, f32[2,128,128]{2,1,0:T(8,128)S(1)}, u32[]{:S(2)}, u32[]{:S(2)}) collective-permute-start(f32[2,128,128]{2,1,0:T(8,128)S(1)} %add_select_fusion), channel_id=1, source_target_pairs={{16,8},{20,12},{8,0},{12,4},{17,9},{21,13},{9,1},{13,5},{18,10},{2... | collective-permute-start | bytes 393224 | tf_op jit(solution)/shard_map/ppermute | solution.py:258
  128.5 11.3 %collective-permute-start.31 = (f32[2,128,128]{2,1,0:T(8,128)S(1)}, f32[2,128,128]{2,1,0:T(8,128)S(1)}, u32[]{:S(2)}, u32[]{:S(2)}) collective-permute-start(f32[2,128,128]{2,1,0:T(8,128)S(1)} %get-tuple-element.108), channel_id=1, source_target_pairs={{0,4},{4,0},{8,12},{12,8},{16,20},{20,16},{24,28},{28,24},{1,5},{5... | collective-permute-start | bytes 393224 | tf_op jit(solution)/shard_map/ppermute | solution.py:266
  129.2 12.7 %collective-permute-start.30 = (f32[2,128,128]{2,1,0:T(8,128)S(1)}, f32[2,128,128]{2,1,0:T(8,128)S(1)}, u32[]{:S(2)}, u32[]{:S(2)}) collective-permute-start(f32[2,128,128]{2,1,0:T(8,128)S(1)} %get-tuple-element.139), channel_id=1, source_target_pairs={{0,4},{4,0},{8,12},{12,8},{16,20},{20,16},{24,28},{28,24},{1,5},{5... | collective-permute-start | bytes 393224 | tf_op jit(solution)/shard_map/ppermute | solution.py:266
  130.5 13.3 %collective-permute-start.29 = (f32[2,128,128]{2,1,0:T(8,128)S(1)}, f32[2,128,128]{2,1,0:T(8,128)S(1)}, u32[]{:S(2)}, u32[]{:S(2)}) collective-permute-start(f32[2,128,128]{2,1,0:T(8,128)S(1)} %get-tuple-element.141), channel_id=1, source_target_pairs={{0,4},{4,0},{8,12},{12,8},{16,20},{20,16},{24,28},{28,24},{1,5},{5... | collective-permute-start | bytes 393224 | tf_op jit(solution)/shard_map/ppermute | solution.py:266
  131.3 6.9 %collective-permute-start.27 = (f32[2,128,128]{2,1,0:T(8,128)S(1)}, f32[2,128,128]{2,1,0:T(8,128)S(1)}, u32[]{:S(2)}, u32[]{:S(2)}) collective-permute-start(f32[2,128,128]{2,1,0:T(8,128)S(1)} %multiply_add_fusion.4), channel_id=1, source_target_pairs={{8,0},{12,4},{9,1},{13,5},{10,2},{14,6},{11,3},{15,7}} | collective-permute-start | bytes 393224 | tf_op jit(solution)/shard_map/ppermute | solution.py:258
  138.2 7.7 %collective-permute-start.28 = (f32[2,128,128]{2,1,0:T(8,128)S(1)}, f32[2,128,128]{2,1,0:T(8,128)S(1)}, u32[]{:S(2)}, u32[]{:S(2)}) collective-permute-start(f32[2,128,128]{2,1,0:T(8,128)S(1)} %get-tuple-element.114), channel_id=1, source_target_pairs={{0,4},{4,0},{8,12},{12,8},{16,20},{20,16},{24,28},{28,24},{1,5},{5... | collective-permute-start | bytes 393224 | tf_op jit(solution)/shard_map/ppermute | solution.py:266
  (41 other events, 221.3 us)
where the time goes:
time: 149 us; the launch traced here: 148 us
  Pallas kernels  54.2 us (36%)
  starting transfers between devices  46 us (31%)
  waiting for transfers between devices  25.4 us (17%)
  local copies, waits for them, and re-layouts  16.9 us (11%)
  other arithmetic  4.03 us (3%)
  between operations  1.54 us (1%)
    pallas_call x24, Pallas kernels, run(): pl.pallas_call(body, out_shape=out_shape, grid_spec=pltpu.PrefetchScalarG...  52.3 us
    ppermute x12, waiting for transfers between devices, chain(): arrived[step] = lax.ppermute(value, 'seq', pairs)  23.9 us
    ppermute x12, starting transfers between devices, chain(): arrived[step] = lax.ppermute(value, 'seq', pairs)  22.2 us
    unnamed x83, local copies, waits for them, and re-layouts  15.8 us
    ppermute x8, starting transfers between devices, chain(): lax.ppermute(jnp.where(first, after_first, before), 'seq', swap)  9.39 us
    ppermute x8, starting transfers between devices, chain(): received = [lax.ppermute(send, 'seq', swap) for send in sends]  8.36 us
    ppermute x1, starting transfers between devices, on_device(): other_decay = jnp.exp(lax.ppermute(cumul[:, -1], 'seq', swap))  3.03 us
    ppermute x3, starting transfers between devices, on_device(): lax.ppermute(sums, 'head', [(i, (i + k) % head_count) for i in range(head...  3 us
  transfers between devices with their start and end apart: 32, of which 10 were waited for; matrix products, arithmetic and copies ran while one was open for 2% of the time, Pallas kernels for 32%

commit v1 on v0

v1 whole, which is shorter than its diff:
```python
import functools

import jax
import jax.numpy as jnp
from jax import lax
from jax.experimental import pallas as pl
from jax.experimental.pallas import tpu as pltpu
from jax.sharding import PartitionSpec as P

HEAD_DIM = 128
BLOCK = 512
CHUNKS = 2
TILE = 256
epsilon = 1e-06
f32 = jnp.float32
bf16 = jnp.bfloat16

NN = (((1,), (0,)), ((), ()))
NT = (((1,), (1,)), ((), ()))
TN = (((0,), (0,)), ((), ()))


def dot(a, b, dims=NN):
    return lax.dot_general(a, b, dims, preferred_element_type=f32)


def halves(x):
    high = x.astype(bf16)
    return high, (x - high.astype(f32)).astype(bf16)


def column(row):
    return jnp.transpose(jnp.broadcast_to(row, (HEAD_DIM, row.shape[1])))


def wide(col, width):
    return jnp.concatenate([col] * (width // HEAD_DIM), axis=1)


def cumul_kernel(decay_ref, out_ref):
    decay = decay_ref[...]
    length = decay.shape[1]
    first = decay.astype(bf16)
    rest = decay - first.astype(f32)
    second = rest.astype(bf16)
    third = (rest - second.astype(f32)).astype(bf16)
    upto = lax.broadcasted_iota(jnp.int32, (length, length), 0) <= lax.broadcasted_iota(
        jnp.int32, (length, length), 1
    )
    upto = jnp.where(upto, 1.0, 0.0).astype(bf16)
    out_ref[...] = dot(first, upto) + dot(second, upto) + dot(third, upto)


def trail_row(row):
    return jnp.exp(row[:, -1:] - row)


def outer_sum(left, scale_row, right):
    scaled = jnp.transpose(left.astype(f32)) * scale_row
    high, low = halves(scaled)
    return dot(high, right) + dot(low, right)


def cols(j):
    return slice(j * HEAD_DIM, (j + 1) * HEAD_DIM)


class Part:
    def __init__(self, chunk, slot, half):
        self.chunk, self.slot, self.half = chunk, slot, half
        self.steps = 2 if half % 2 == 0 else 1
        self.per_step = half // self.steps

    def group(self, info):
        return info[0] if self.slot == "mine" else 1 - info[0]

    def row(self, cumul_ref, info, j):
        head = (2 * self.chunk + self.group(info)) * self.half + pl.program_id(0) * self.per_step + j
        return cumul_ref[pl.ds(head, 1), :]

    def state_rows(self, j):
        start = (pl.program_id(0) * self.per_step + j) * HEAD_DIM
        return pl.ds(pl.multiple_of(start, HEAD_DIM), HEAD_DIM)


def store_decays(part, info, cumul_ref, out_ref):
    for j in range(part.per_step):
        row = part.row(cumul_ref, info, j)
        place = part.half * HEAD_DIM + pl.program_id(0) * part.per_step + j
        out_ref[pl.ds(place, 1), :] = jnp.broadcast_to(jnp.exp(row[:, -1:]), (1, HEAD_DIM))


def pieces_kernel(part, info, key_ref, value_ref, cumul_ref, out_ref):
    for j in range(part.per_step):
        row = part.row(cumul_ref, info, j)
        out_ref[part.state_rows(j), :] = outer_sum(
            key_ref[:, cols(j)], trail_row(row), value_ref[:, cols(j)]
        )
    store_decays(part, info, cumul_ref, out_ref)


def inner_kernel(part, info, query_ref, key_ref, value_ref, cumul_ref, out_ref):
    for j in range(part.per_step):
        row = part.row(cumul_ref, info, j)
        col = column(row)
        query, key, value = query_ref[:, cols(j)], key_ref[:, cols(j)], value_ref[:, cols(j)]
        for top in range(0, BLOCK, TILE):
            end = top + TILE
            scores = dot(query[top:end], key[:end], NT)
            spread = wide(col[top:end], end) - row[:, :end]
            causal = lax.broadcasted_iota(jnp.int32, (TILE, end), 0) + top >= (
                lax.broadcasted_iota(jnp.int32, (TILE, end), 1)
            )
            weights = (scores * jnp.exp(jnp.where(causal, spread, -1e30))).astype(bf16)
            out_ref[top:end, cols(j)] = dot(weights, value[:end])


def output_kernel(
    part, info, inner_ref, query_ref, cot_ref, gain_ref, cumul_ref, state_ref, before_ref,
    out_ref, sums_ref, square_ref, product_ref,
):
    step = pl.program_id(0)
    squares = jnp.zeros((BLOCK, HEAD_DIM), f32)
    products = jnp.zeros((BLOCK, HEAD_DIM), f32)
    for j in range(part.per_step):
        lead = jnp.exp(column(part.row(cumul_ref, info, j)))
        high, low = halves(state_ref[part.state_rows(j), :])
        query = query_ref[:, cols(j)]
        out = inner_ref[:, cols(j)] + lead * (dot(query, high) + dot(query, low))
        out_ref[:, cols(j)] = out
        squares += out * out
        products += cot_ref[:, cols(j)].astype(f32) * gain_ref[:, cols(j)] * out

    @pl.when(step == 0)
    def _():
        square_ref[...] = squares
        product_ref[...] = products

    @pl.when(step > 0)
    def _():
        square_ref[...] += squares
        product_ref[...] += products

    @pl.when(step == part.steps - 1)
    def _():
        rows = lax.broadcasted_iota(jnp.int32, (8, HEAD_DIM), 0)
        total = before_ref[...]
        for place, ref in ((0, square_ref), (1, product_ref)):
            pick = jnp.where(rows == place, 1.0, 0.0).astype(bf16)
            high, low = halves(ref[...])
            total += dot(pick, high, NT) + dot(pick, low, NT)
        sums_ref[...] = total


def grad_kernel(features, part, info, out_ref, cot_ref, gain_ref, query_ref, cumul_ref, *refs):
    shares, (attended_ref, grad_ref, piece_ref) = refs[:-3], refs[-3:]
    sums = shares[0][...]
    for share in shares[1:]:
        sums = sums + share[...]
    inverse = lax.rsqrt(sums[0:1] / features + epsilon)
    mean_term = inverse * sums[1:2] / features
    inverse_col, mean_col = column(inverse), column(mean_term)
    for j in range(part.per_step):
        gain = gain_ref[:, cols(j)]
        normed = out_ref[:, cols(j)] * inverse_col
        attended_ref[:, cols(j)] = (normed * gain).astype(bf16)
        scaled_grad = cot_ref[:, cols(j)].astype(f32) * gain
        grad = (inverse_col * (scaled_grad - normed * mean_col)).astype(bf16)
        grad_ref[:, cols(j)] = grad
        row = part.row(cumul_ref, info, j)
        piece_ref[part.state_rows(j), :] = outer_sum(query_ref[:, cols(j)], jnp.exp(row), grad)
    store_decays(part, info, cumul_ref, piece_ref)


def backward_kernel(
    part, info, query_ref, key_ref, value_ref, grad_ref, cumul_ref, state_ref,
    grad_query_ref, inner_key_ref, inner_value_ref,
):
    for j in range(part.per_step):
        row = part.row(cumul_ref, info, j)
        col = column(row)
        query, key = query_ref[:, cols(j)], key_ref[:, cols(j)]
        value, grad = value_ref[:, cols(j)], grad_ref[:, cols(j)]
        high, low = halves(state_ref[part.state_rows(j), :])
        outer = jnp.exp(col) * (dot(grad, high, NT) + dot(grad, low, NT))
        for top in range(0, BLOCK, TILE):
            end = top + TILE
            scores = dot(key[top:end], query[top:], NT)
            grad_scores = dot(value[top:end], grad[top:], NT)
            spread = row[:, top:] - wide(col[top:end], BLOCK - top)
            causal = lax.broadcasted_iota(jnp.int32, spread.shape, 0) <= (
                lax.broadcasted_iota(jnp.int32, spread.shape, 1)
            )
            decays = jnp.exp(jnp.where(causal, spread, -1e30))
            weights = (scores * decays).astype(bf16)
            grad_weights = (grad_scores * decays).astype(bf16)
            inner_value_ref[top:end, cols(j)] = dot(weights, grad[top:])
            inner_key_ref[top:end, cols(j)] = dot(grad_weights, query[top:])
            inner_query = dot(grad_weights, key[top:end], TN)
            outer = inner_query + outer if top == 0 else jnp.concatenate(
                [outer[:top], outer[top:] + inner_query], axis=0
            )
        grad_query_ref[:, cols(j)] = outer.astype(bf16)


def final_kernel(
    part, info, inner_key_ref, inner_value_ref, key_ref, value_ref, cumul_ref, state_ref,
    grad_key_ref, grad_value_ref,
):
    for j in range(part.per_step):
        trail = column(trail_row(part.row(cumul_ref, info, j)))
        high, low = halves(state_ref[part.state_rows(j), :])
        key, value = key_ref[:, cols(j)], value_ref[:, cols(j)]
        grad_key_ref[:, cols(j)] = (
            inner_key_ref[:, cols(j)] + trail * (dot(value, high, NT) + dot(value, low, NT))
        ).astype(bf16)
        grad_value_ref[:, cols(j)] = (
            inner_value_ref[:, cols(j)] + trail * (dot(key, high) + dot(key, low))
        ).astype(bf16)


def ordered(is_first, half, j, keep_ref, got_ref):
    rows = slice(j * HEAD_DIM, (j + 1) * HEAD_DIM)
    place = slice(half * HEAD_DIM + j, half * HEAD_DIM + j + 1)
    keep, got = keep_ref[rows, :], got_ref[rows, :]
    keep_decay, got_decay = keep_ref[place, :], got_ref[place, :]
    return (
        jnp.where(is_first, keep, got),
        jnp.where(is_first, got, keep),
        jnp.where(is_first, keep_decay, got_decay),
        jnp.where(is_first, got_decay, keep_decay),
    )


def hop_kernel(half, senders, info, *refs):
    out_ref, arrived_ref = refs[-1], refs[-2]
    for index, p in enumerate(senders):
        keep_ref, got_ref = refs[2 * index], refs[2 * index + 1]

        @pl.when(info[2] == p)
        def _():
            for j in range(half):
                first, second, first_decay, second_decay = ordered(
                    info[1] == 1, half, j, keep_ref, got_ref
                )
                value = second_decay * first + second
                if p > 0:
                    value += (first_decay * second_decay) * arrived_ref[cols(j), :]
                out_ref[cols(j), :] = value


def last_kernel(half, info, keep_ref, got_ref, *refs):
    arrived, (mine_ref, send_ref) = refs[:-2], refs[-2:]
    is_first = info[1] == 1
    for p in range(len(arrived) + 1):

        @pl.when(info[2] == p)
        def _():
            for j in range(half):
                first, _, first_decay, _ = ordered(is_first, half, j, keep_ref, got_ref)
                if p == 0:
                    before, after = jnp.zeros_like(first), first
                else:
                    before = arrived[p - 1][cols(j), :]
                    after = first_decay * before + first
                mine_ref[cols(j), :] = jnp.where(is_first, before, after)
                send_ref[cols(j), :] = jnp.where(is_first, after, before)


def on_device(queries, key_vecs, value_vecs, log_decay, norm_gain, cotangent):
    tokens, width = queries.shape
    assert tokens == BLOCK
    heads = width // HEAD_DIM
    half = heads // (2 * CHUNKS)
    head_count = lax.axis_size("head")
    features = width * head_count
    places = lax.axis_size("seq") // 2
    my_index = lax.axis_index("seq")
    member, pair = my_index % 2, my_index // 2
    gain = norm_gain.reshape(1, width)

    any_spec = pl.BlockSpec(memory_space=pl.ANY)
    wide_state = jax.ShapeDtypeStruct((half * HEAD_DIM + 8, HEAD_DIM), f32)
    state = jax.ShapeDtypeStruct((half * HEAD_DIM, HEAD_DIM), f32)
    whole = jax.ShapeDtypeStruct((tokens, width), bf16)
    local = jax.ShapeDtypeStruct((tokens, half * HEAD_DIM), f32)
    local_low = jax.ShapeDtypeStruct((tokens, half * HEAD_DIM), bf16)
    sums_shape = jax.ShapeDtypeStruct((8, tokens), f32)
    forward_info = jnp.stack([member, 1 - member, pair]).astype(jnp.int32)
    backward_info = jnp.stack([member, member, places - 1 - pair]).astype(jnp.int32)

    def run(kernel, info, grid, ins, outs, scratch=(), after=(), aliases=None, cost=1.0):
        used = len(ins)
        after = [x for i, x in enumerate(after) if not any(x is y for y in after[:i])]

        def body(info_ref, *refs):
            kernel(info_ref, *refs[:used], *refs[used + len(after):])

        return pl.pallas_call(
            body,
            out_shape=[shape for shape, _ in outs],
            grid_spec=pltpu.PrefetchScalarGridSpec(
                num_scalar_prefetch=1,
                grid=(grid,),
                in_specs=[spec for _, spec in ins] + [any_spec] * len(after),
                out_specs=[spec for _, spec in outs],
                scratch_shapes=list(scratch),
            ),
            input_output_aliases=aliases or {},
            compiler_params=pltpu.CompilerParams(vmem_limit_bytes=16 * 1024 * 1024),
            cost_estimate=pl.CostEstimate(
                flops=int(cost * 1e9), bytes_accessed=int(cost * 2.5e6), transcendentals=0
            ),
        )(info, *[array for array, _ in ins], *after)

    def fixed(shape):
        return pl.BlockSpec(shape, lambda i, info: (0,) * len(shape))

    def plain(array):
        return array, fixed(array.shape)

    def give(shape):
        return shape, fixed(shape.shape)

    class Views(Part):
        def full(self, array, rows=tokens):
            return array, self.full_spec(rows)

        def full_spec(self, rows=tokens):
            return pl.BlockSpec(
                (rows, self.per_step * HEAD_DIM),
                lambda i, info: (0, (2 * self.chunk + self.group(info)) * self.steps + i),
            )

        def local(self, array):
            return array, pl.BlockSpec((tokens, self.per_step * HEAD_DIM), lambda i, info: (0, i))

        def call(self, kernel, ins, outs, **options):
            return run(functools.partial(kernel, self), forward_info, self.steps, ins, outs, **options)

    mine_parts = [Views(c, "mine", half) for c in range(CHUNKS)]
    their_parts = [Views(c, "theirs", half) for c in range(CHUNKS)]

    cumul = pl.pallas_call(
        cumul_kernel, out_shape=jax.ShapeDtypeStruct((heads, tokens), f32)
    )(log_decay.T)

    swap = [(2 * p + m, 2 * p + 1 - m) for p in range(places) for m in (0, 1)]

    def chain(make_piece, info, forward, early, filler, on_mine):
        step = 1 if forward else -1
        ring = [
            (2 * p + m, 2 * ((p + step) % places) + m) for p in range(places) for m in (0, 1)
        ]
        received, last = [], ()
        for c in range(CHUNKS):
            sent = make_piece(their_parts[c], last)
            received.append(lax.ppermute(sent, "seq", swap))
            last = (sent,)
        keeps = []
        for c in range(CHUNKS):
            keeps.append(make_piece(mine_parts[c], last))
            last = (keeps[-1],)
        for work in early:
            last = (work(last),)
        arrived, mine, theirs = {}, [], []
        for r in range(2, CHUNKS + places + 1):
            if r < CHUNKS + places:
                senders = [p for p in range(places - 1) if 0 <= r - 2 - p < CHUNKS]
                ins = []
                for p in senders:
                    ins += [plain(keeps[r - 2 - p]), plain(received[r - 2 - p])]
                ins.append(plain(arrived[r - 1]) if r > 2 else plain(keeps[0]))
                value, = run(
                    functools.partial(hop_kernel, half, senders), info, 1, ins, [give(state)],
                    after=last, cost=0.3,
                )
                arrived[r] = lax.ppermute(value, "seq", ring)
                last = (value,)
            c = r - 1 - places
            if 0 <= c:
                ins = [plain(keeps[c]), plain(received[c])]
                ins += [plain(arrived[c + 1 + p]) for p in range(1, places)]
                own, send = run(
                    functools.partial(last_kernel, half), info, 1, ins, [give(state)] * 2,
                    after=last, cost=0.3,
                )
                theirs.append(lax.ppermute(send, "seq", swap))
                mine.append(own)
                last = (send,)
                filler.append(functools.partial(on_mine, c, own))
            if filler:
                last = (filler.pop(0)(last),)
        while filler:
            last = (filler.pop(0)(last),)
        return mine, theirs, last

    def forward_piece(part, after):
        return part.call(
            pieces_kernel, [part.full(key_vecs), part.full(value_vecs), plain(cumul)],
            [give(wide_state)], after=after, cost=1.0,
        )[0]

    inner, outs = {}, {}
    state_sums = [jnp.zeros(sums_shape.shape, f32)]

    def inner_work(part, after):
        inner[part], = part.call(
            inner_kernel,
            [part.full(queries), part.full(key_vecs), part.full(value_vecs), plain(cumul)],
            [part.local(local)], after=after, cost=2.2,
        )
        return inner[part]

    def output_work(part, before, after):
        outs[part], sums = part.call(
            output_kernel,
            [part.local(inner[part]), part.full(queries), part.full(cotangent), part.full(gain, 1),
             plain(cumul), plain(before), plain(state_sums[0])],
            [part.local(local), give(sums_shape)],
            scratch=[pltpu.VMEM((tokens, HEAD_DIM), f32)] * 2, after=after, cost=1.4,
        )
        state_sums[0] = sums
        return sums

    inner_order = [part for c in range(CHUNKS) for part in (mine_parts[c], their_parts[c])]
    works = [functools.partial(inner_work, part) for part in inner_order]
    mine, theirs, last = chain(
        forward_piece, forward_info, True, works[:1], works[1:],
        lambda c, own, after: output_work(mine_parts[c], own, after),
    )
    for c in range(CHUNKS):
        last = (output_work(their_parts[c], theirs[c], last),)

    sums = state_sums[0]
    shares = [sums] + [
        lax.ppermute(sums, "head", [(i, (i + k) % head_count) for i in range(head_count)])
        for k in range(1, head_count)
    ]

    attended, grad_queries, grad_keys, grad_values = [], [], [], []
    grads, inner_grads = {}, {}

    def target(held):
        return tuple(held[-1:])

    def backward_piece(part, after):
        before = target(attended)
        whole_out, grads[part], piece = part.call(
            functools.partial(grad_kernel, features),
            [part.local(outs[part]), part.full(cotangent), part.full(gain, 1), part.full(queries),
             plain(cumul)] + [plain(share) for share in shares],
            [(whole, part.full_spec()), part.local(local_low), give(wide_state)],
            after=before + tuple(after), aliases={6 + head_count: 0} if before else None, cost=2.0,
        )
        attended.append(whole_out)
        return piece

    def backward_work(part, before, after):
        held = target(grad_queries)
        whole_out, *inner_grads[part] = part.call(
            backward_kernel,
            [part.full(queries), part.full(key_vecs), part.full(value_vecs),
             part.local(grads[part]), plain(cumul), plain(before)],
            [(whole, part.full_spec()), part.local(local), part.local(local)],
            after=held + tuple(after), aliases={7: 0} if held else None, cost=4.3,
        )
        grad_queries.append(whole_out)
        return inner_grads[part][0]

    def final_work(part, before, after):
        held = target(grad_keys) + target(grad_values)
        whole_key, whole_value = part.call(
            final_kernel,
            [part.local(inner_grads[part][0]), part.local(inner_grads[part][1]),
             part.full(key_vecs), part.full(value_vecs), plain(cumul), plain(before)],
            [(whole, part.full_spec())] * 2,
            after=held + tuple(after), aliases={7: 0, 8: 1} if held else None, cost=2.0,
        )
        grad_keys.append(whole_key)
        grad_values.append(whole_value)
        return whole_key

    works = []
    for c in range(CHUNKS):
        works.append(functools.partial(backward_work, mine_parts[c], mine[c]))
        works.append(functools.partial(backward_work, their_parts[c], theirs[c]))
    mine_after, theirs_after, last = chain(
        backward_piece, backward_info, False, [], works,
        lambda c, own, after: final_work(mine_parts[c], own, after),
    )
    for c in range(CHUNKS):
        final_work(their_parts[c], theirs_after[c], last)
        last = ()
    return attended[-1], grad_queries[-1], grad_keys[-1], grad_values[-1]


def solution(mesh):
    return jax.shard_map(
        on_device,
        mesh=mesh,
        in_specs=(
            P("seq", "head"),
            P("seq", "head"),
            P("seq", "head"),
            P("seq", "head"),
            P("head"),
            P("seq", "head"),
        ),
        out_specs=(P("seq", "head"), P("seq", "head"), P("seq", "head"), P("seq", "head")),
        check_vma=False,
    )
```

time: 149 us -> 135 us (0.906)
  Pallas kernels: 54.2 us -> 74.7 us
  starting transfers between devices: 46 us -> 27.8 us
  local copies, waits for them, and re-layouts: 16.9 us -> 10.3 us
  waiting for transfers between devices: 25.4 us -> 20.8 us
  other arithmetic: 4.03 us -> 0.15 us
    pallas_call x24 -> x36, Pallas kernels: 52.3 us -> 73.1 us  [run(): pl.pallas_call(body, out_shape=[shape for shape, _ in outs], grid_spec=pl...]
    ppermute x29 -> x16, starting transfers between devices: 43 us -> 26.1 us  [the longest x8 16.6 us: chain(): arrived[r] = lax.ppermute(value, 'seq', ring)]
    ppermute x29 -> x16, waiting for transfers between devices: 24 us -> 17.9 us  [the longest x8 16.2 us: chain(): arrived[r] = lax.ppermute(value, 'seq', ring)]
    unnamed x83 -> x52, local copies, waits for them, and re-layouts: 15.8 us -> 10.2 us
    select_n x19 -> x0, other arithmetic: 3.68 us -> none  [the longest x8 2.63 us: chain(): value = here if value is None else jnp.where(place == p, here, value)]
  transfers between devices with their start and end apart: 32 -> 19, of which waited for: 10 -> 6; matrix products, arithmetic and copies ran while one was open for 2% -> 0% of each run, Pallas kernels for 32% -> 45%
where the time goes in v1:
time: 135 us
  Pallas kernels  74.7 us (55%)
  starting transfers between devices  27.8 us (21%)
  waiting for transfers between devices  20.8 us (15%)
  local copies, waits for them, and re-layouts  10.3 us (8%)
    pallas_call x36, Pallas kernels, run(): pl.pallas_call(body, out_shape=[shape for shape, _ in outs], grid_spec=pl...  73.1 us
    ppermute x8, starting transfers between devices, chain(): arrived[r] = lax.ppermute(value, 'seq', ring)  16.6 us
    ppermute x8, waiting for transfers between devices, chain(): arrived[r] = lax.ppermute(value, 'seq', ring)  16.2 us
    unnamed x52, local copies, waits for them, and re-layouts  10.2 us
    ppermute x4, starting transfers between devices, chain(): received.append(lax.ppermute(sent, 'seq', swap))  5.14 us
    ppermute x4, starting transfers between devices, chain(): theirs.append(lax.ppermute(send, 'seq', swap))  4.32 us
    ppermute x3, waiting for transfers between devices, on_device(): lax.ppermute(sums, 'head', [(i, (i + k) % head_count) for i in range(head...  2.92 us
  transfers between devices with their start and end apart: 19, of which 6 were waited for; matrix products, arithmetic and copies ran while one was open for 0% of the time, Pallas kernels for 45%

profile of v1, /device:TPU:0, one launch (start us, length us, event | category | flops | bytes accessed | tf_op | source)
XLA Modules:
  0.0 134.8 jit_solution(8896728843380794133)
XLA Ops:
  0.6 1.7 %shard_map.93.refs_2_.refs_3_.refs_4_ = f32[16,512]{1,0:T(8,128)} custom-call(f32[16,512]{1,0:T(8,128)} %bitcast.14), custom_call_target="tpu_custom_call" | custom-call | tf_op jit(solution)/shard_map/pallas_call | solution.py:344
  7.8 3.0 %collective-permute-start.1 = (f32[520,128]{1,0:T(8,128)S(1)}, f32[520,128]{1,0:T(8,128)S(1)}, u32[]{:S(2)}, u32[]{:S(2)}) collective-permute-start(f32[520,128]{1,0:T(8,128)S(1)} %shard_map.94.refs_3_), channel_id=1, source_target_pairs={{0,4},{4,0},{8,12},{12,8},{16,20},{20,16},{24,28},{28,24},{1,5},{5... | collective-permute-start | bytes 798728 | tf_op jit(solution)/shard_map/ppermute | solution.py:358
  15.5 2.7 %shard_map.98.refs_3_.refs_0_ = f32[512,512]{1,0:T(8,128)S(1)} custom-call(s32[3]{0:T(128)S(1)} %pad_add_fusion.info_ref, bf16[512,2048]{1,0:T(8,128)(2,1)S(1)} %copy-done.7, bf16[512,2048]{1,0:T(8,128)(2,1)S(1)} %copy-done, bf16[512,2048]{1,0:T(8,128)(2,1)S(1)} %copy-done.2, f32[16,512]{1,0:T(8,128)S(1)} %copy-done.10, f32[520,128]{1,0:T(8,128)S(1)} %shard_map.97.refs_4_.refs_0_), custom_call_target="tpu_custom_call" | custom-call | flops 2200000000 | bytes 5500000 | tf_op jit(solution)/shard_map/pallas_call | solution.py:299
  18.9 2.1 %collective-permute-start.2 = (f32[512,128]{1,0:T(8,128)S(1)}, f32[512,128]{1,0:T(8,128)S(1)}, u32[]{:S(2)}, u32[]{:S(2)}) collective-permute-start(f32[512,128]{1,0:T(8,128)S(1)} %shard_map.99.refs_4_), channel_id=1, source_target_pairs={{0,8},{4,12},{8,16},{12,20},{16,24},{20,28},{24,0},{28,4},{1,9},{5... | collective-permute-start | bytes 786440 | tf_op jit(solution)/shard_map/ppermute | solution.py:378
  21.0 2.7 %shard_map.100.refs_5_.refs_0_ = f32[512,512]{1,0:T(8,128)S(1)} custom-call(s32[3]{0:T(128)S(1)} %pad_add_fusion.info_ref, bf16[512,2048]{1,0:T(8,128)(2,1)S(1)} %copy-done.7, bf16[512,2048]{1,0:T(8,128)(2,1)S(1)} %copy-done.1, bf16[512,2048]{1,0:T(8,128)(2,1)S(1)} %copy-done.2, f32[16,512]{1,0:T(8,128)S(1)} %copy-done.11, f32[512,128]{1,0:T(8,128)S(1)} %shard_map.99.refs_4_), custom_call_target="tpu_custom_call" | custom-call | flops 2200000000 | bytes 5500000 | tf_op jit(solution)/shard_map/pallas_call | solution.py:299
  23.8 5.0 %collective-permute-done.2.refs_4_.refs_2_ = f32[512,128]{1,0:T(8,128)S(1)} collective-permute-done((f32[512,128]{1,0:T(8,128)S(1)}, f32[512,128]{1,0:T(8,128)S(1)}, u32[]{:S(2)}, u32[]{:S(2)}) %collective-permute-start.2) | collective-permute-done | bytes 262176 | tf_op jit(solution)/shard_map/ppermute | solution.py:378
  29.5 2.7 %shard_map.102.refs_5_.refs_0_ = f32[512,512]{1,0:T(8,128)S(1)} custom-call(s32[3]{0:T(128)S(1)} %pad_add_fusion.info_ref, bf16[512,2048]{1,0:T(8,128)(2,1)S(1)} %copy-done.7, bf16[512,2048]{1,0:T(8,128)(2,1)S(1)} %copy-done.1, bf16[512,2048]{1,0:T(8,128)(2,1)S(1)} %copy-done.3, f32[16,512]{1,0:T(8,128)S(1)} %copy-done.11, f32[512,128]{1,0:T(8,128)S(1)} %shard_map.101.refs_4_), custom_call_target="tpu_custom_call" | custom-call | flops 2200000000 | bytes 5500000 | tf_op jit(solution)/shard_map/pallas_call | solution.py:299
  32.2 5.9 %collective-permute-done.3.refs_4_.refs_3_.refs_2_ = f32[512,128]{1,0:T(8,128)S(1)} collective-permute-done((f32[512,128]{1,0:T(8,128)S(1)}, f32[512,128]{1,0:T(8,128)S(1)}, u32[]{:S(2)}, u32[]{:S(2)}) %collective-permute-start.3) | collective-permute-done | bytes 262176 | tf_op jit(solution)/shard_map/ppermute | solution.py:378
  38.7 2.8 %shard_map.104.refs_3_.refs_0_ = f32[512,512]{1,0:T(8,128)S(1)} custom-call(s32[3]{0:T(128)S(1)} %pad_add_fusion.info_ref, bf16[512,2048]{1,0:T(8,128)(2,1)S(1)} %copy-done.7, bf16[512,2048]{1,0:T(8,128)(2,1)S(1)} %copy-done.1, bf16[512,2048]{1,0:T(8,128)(2,1)S(1)} %copy-done.3, f32[16,512]{1,0:T(8,128)S(1)} %copy-done.11, f32[512,128]{1,0:T(8,128)S(1)} %shard_map.103.refs_4_), custom_call_target="tpu_custom_call" | custom-call | flops 2200000000 | bytes 5500000 | tf_op jit(solution)/shard_map/pallas_call | solution.py:299
  41.5 5.4 %collective-permute-done.4.refs_2_.refs_4_.refs_3_ = f32[512,128]{1,0:T(8,128)S(1)} collective-permute-done((f32[512,128]{1,0:T(8,128)S(1)}, f32[512,128]{1,0:T(8,128)S(1)}, u32[]{:S(2)}, u32[]{:S(2)}) %collective-permute-start.4) | collective-permute-done | bytes 262176 | tf_op jit(solution)/shard_map/ppermute | solution.py:378
  56.2 2.0 %shard_map.107 = (f32[512,512]{1,0:T(8,128)S(1)}, f32[8,512]{1,0:T(8,128)S(1)}) custom-call(s32[3]{0:T(128)S(1)} %pad_add_fusion.info_ref, f32[512,512]{1,0:T(8,128)S(1)} %copy-done.15, bf16[512,2048]{1,0:T(8,128)(2,1)S(1)} %copy-done.8, bf16[512,2048]{1,0:T(8,128)(2,1)S(1)} %copy-done.5, f32[1,2048]{1,0:T(1,128)S(1)} %bitcast.6, f32[16,512]{1,0:T(8,128)S(1)} %copy-done.11, ...), custom_call_target="tpu_custom_call" | custom-call | flops 1400000000 | bytes 3500000 | tf_op jit(solution)/shard_map/pallas_call | solution.py:299
  60.6 1.9 %shard_map.109 = (f32[512,512]{1,0:T(8,128)S(1)}, f32[8,512]{1,0:T(8,128)S(1)}) custom-call(s32[3]{0:T(128)S(1)} %pad_add_fusion.info_ref, f32[512,512]{1,0:T(8,128)S(1)} %copy-done.19, bf16[512,2048]{1,0:T(8,128)(2,1)S(1)} %copy-done.9, bf16[512,2048]{1,0:T(8,128)(2,1)S(1)} %copy-done.6, f32[1,2048]{1,0:T(1,128)S(1)} %bitcast.7, f32[16,512]{1,0:T(8,128)S(1)} %copy-done.11, ...), custom_call_target="tpu_custom_call" | custom-call | flops 1400000000 | bytes 3500000 | tf_op jit(solution)/shard_map/pallas_call | solution.py:299
  62.6 1.9 %shard_map.110 = (f32[512,512]{1,0:T(8,128)S(1)}, f32[8,512]{1,0:T(8,128)S(1)}) custom-call(s32[3]{0:T(128)S(1)} %pad_add_fusion.info_ref, f32[512,512]{1,0:T(8,128)S(1)} %copy-done.17, bf16[512,2048]{1,0:T(8,128)(2,1)S(1)} %copy-done.9, bf16[512,2048]{1,0:T(8,128)(2,1)S(1)} %copy-done.6, f32[1,2048]{1,0:T(1,128)S(1)} %bitcast.8, f32[16,512]{1,0:T(8,128)S(1)} %copy-done.11, ...), custom_call_target="tpu_custom_call" | custom-call | flops 1400000000 | bytes 3500000 | tf_op jit(solution)/shard_map/pallas_call | solution.py:299
  66.2 1.9 %shard_map.111 = (f32[512,512]{1,0:T(8,128)S(1)}, f32[8,512]{1,0:T(8,128)S(1)}) custom-call(s32[3]{0:T(128)S(1)} %pad_add_fusion.info_ref, f32[512,512]{1,0:T(8,128)S(1)} %copy-done.13, bf16[512,2048]{1,0:T(8,128)(2,1)S(1)} %copy-done.9, bf16[512,2048]{1,0:T(8,128)(2,1)S(1)} %copy-done.6, f32[1,2048]{1,0:T(1,128)S(1)} %bitcast.9, f32[16,512]{1,0:T(8,128)S(1)} %copy-done.11, ...), custom_call_target="tpu_custom_call" | custom-call | flops 1400000000 | bytes 3500000 | tf_op jit(solution)/shard_map/pallas_call | solution.py:299
  70.0 2.0 %collective-permute-done.9.refs_7_ = f32[8,512]{1,0:T(8,128)S(1)} collective-permute-done((f32[8,512]{1,0:T(8,128)S(1)}, f32[8,512]{1,0:T(8,128)S(1)}, u32[]{:S(2)}, u32[]{:S(2)}) %collective-permute-start.9) | collective-permute-done | bytes 16416 | tf_op jit(solution)/shard_map/ppermute | solution.py:437
  73.0 2.5 %shard_map.112 = (bf16[512,2048]{1,0:T(8,128)(2,1)}, bf16[512,512]{1,0:T(8,128)(2,1)S(1)}, f32[520,128]{1,0:T(8,128)S(1)}) custom-call(s32[3]{0:T(128)S(1)} %pad_add_fusion.info_ref, f32[512,512]{1,0:T(8,128)S(1)} %get-tuple-element.63.refs_0_, bf16[512,2048]{1,0:T(8,128)(2,1)S(1)} %copy-done.6, f32[1,2048]{1,0:T(1,128)S(1)} %bitcast.10, ...), custom_call_target="tpu_custom_call" | custom-call | flops 2000000000 | bytes 5000000 | tf_op jit(solution)/shard_map/pallas_call | solution.py:299
  76.1 2.5 %shard_map.113 = (bf16[512,2048]{1,0:T(8,128)(2,1)}, bf16[512,512]{1,0:T(8,128)(2,1)S(1)}, f32[520,128]{1,0:T(8,128)S(1)}) custom-call(s32[3]{0:T(128)S(1)} %pad_add_fusion.info_ref, f32[512,512]{1,0:T(8,128)S(1)} %get-tuple-element.62.refs_0_, bf16[512,2048]{1,0:T(8,128)(2,1)S(1)} %copy-done.6, ...), custom_call_target="tpu_custom_call", output_to_operand_aliasing={{0}: (10, {})} | custom-call | flops 2000000000 | bytes 5000000 | tf_op jit(solution)/shard_map/pallas_call | solution.py:299
  79.9 2.5 %shard_map.114 = (bf16[512,2048]{1,0:T(8,128)(2,1)}, bf16[512,512]{1,0:T(8,128)(2,1)S(1)}, f32[520,128]{1,0:T(8,128)S(1)}) custom-call(s32[3]{0:T(128)S(1)} %pad_add_fusion.info_ref, f32[512,512]{1,0:T(8,128)S(1)} %get-tuple-element.61.refs_0_, bf16[512,2048]{1,0:T(8,128)(2,1)S(1)} %copy-done.6, ...), custom_call_target="tpu_custom_call", output_to_operand_aliasing={{0}: (10, {})} | custom-call | flops 2000000000 | bytes 5000000 | tf_op jit(solution)/shard_map/pallas_call | solution.py:299
  82.4 2.5 %shard_map.115 = (bf16[512,2048]{1,0:T(8,128)(2,1)}, bf16[512,512]{1,0:T(8,128)(2,1)S(1)}, f32[520,128]{1,0:T(8,128)S(1)}) custom-call(s32[3]{0:T(128)S(1)} %pad_add_fusion.info_ref, f32[512,512]{1,0:T(8,128)S(1)} %get-tuple-element.57.refs_0_, bf16[512,2048]{1,0:T(8,128)(2,1)S(1)} %copy-done.6, ...), custom_call_target="tpu_custom_call", output_to_operand_aliasing={{0}: (10, {})} | custom-call | flops 2000000000 | bytes 5000000 | tf_op jit(solution)/shard_map/pallas_call | solution.py:299
  85.4 3.9 %collective-permute-start.13 = (f32[512,128]{1,0:T(8,128)S(1)}, f32[512,128]{1,0:T(8,128)S(1)}, u32[]{:S(2)}, u32[]{:S(2)}) collective-permute-start(f32[512,128]{1,0:T(8,128)S(1)} %shard_map.116.refs_6_), channel_id=1, source_target_pairs={{0,24},{4,28},{8,0},{12,4},{16,8},{20,12},{24,16},{28,20},{1,25},{... | collective-permute-start | bytes 786440 | tf_op jit(solution)/shard_map/ppermute | solution.py:378
  89.3 4.9 %shard_map.117 = (bf16[512,2048]{1,0:T(8,128)(2,1)}, f32[512,512]{1,0:T(8,128)S(1)}, f32[512,512]{1,0:T(8,128)S(1)}) custom-call(s32[3]{0:T(128)S(1)} %pad_add_fusion.info_ref, bf16[512,2048]{1,0:T(8,128)(2,1)S(1)} %copy-done.9, bf16[512,2048]{1,0:T(8,128)(2,1)S(1)} %copy-done.1, bf16[512,2048]{1,0:T(8,128)(2,1)S(1)} %copy-done.4, ...), custom_call_target="tpu_custom_call" | custom-call | flops 4300000256 | bytes 10750000 | tf_op jit(solution)/shard_map/pallas_call | solution.py:299
  94.7 3.4 %collective-permute-start.14 = (f32[512,128]{1,0:T(8,128)S(1)}, f32[512,128]{1,0:T(8,128)S(1)}, u32[]{:S(2)}, u32[]{:S(2)}) collective-permute-start(f32[512,128]{1,0:T(8,128)S(1)} %shard_map.118.refs_7_), channel_id=1, source_target_pairs={{0,24},{4,28},{8,0},{12,4},{16,8},{20,12},{24,16},{28,20},{1,25},{... | collective-permute-start | bytes 786440 | tf_op jit(solution)/shard_map/ppermute | solution.py:378
  98.1 4.9 %shard_map.119 = (bf16[512,2048]{1,0:T(8,128)(2,1)}, f32[512,512]{1,0:T(8,128)S(1)}, f32[512,512]{1,0:T(8,128)S(1)}) custom-call(s32[3]{0:T(128)S(1)} %pad_add_fusion.info_ref, bf16[512,2048]{1,0:T(8,128)(2,1)S(1)} %copy-done.9, bf16[512,2048]{1,0:T(8,128)(2,1)S(1)} %copy-done.1, bf16[512,2048]{1,0:T(8,128)(2,1)S(1)} %copy-done.4, ...), custom_call_target="tpu_custom_call", output_to_operand_aliasing={{0}: (7, {})} | custom-call | flops 4300000256 | bytes 10750000 | tf_op jit(solution)/shard_map/pallas_call | solution.py:299
  103.6 3.4 %collective-permute-start.15 = (f32[512,128]{1,0:T(8,128)S(1)}, f32[512,128]{1,0:T(8,128)S(1)}, u32[]{:S(2)}, u32[]{:S(2)}) collective-permute-start(f32[512,128]{1,0:T(8,128)S(1)} %shard_map.120.refs_7_), channel_id=1, source_target_pairs={{0,24},{4,28},{8,0},{12,4},{16,8},{20,12},{24,16},{28,20},{1,25},{... | collective-permute-start | bytes 786440 | tf_op jit(solution)/shard_map/ppermute | solution.py:378
  106.9 4.9 %shard_map.121 = (bf16[512,2048]{1,0:T(8,128)(2,1)}, f32[512,512]{1,0:T(8,128)S(1)}, f32[512,512]{1,0:T(8,128)S(1)}) custom-call(s32[3]{0:T(128)S(1)} %pad_add_fusion.info_ref, bf16[512,2048]{1,0:T(8,128)(2,1)S(1)} %copy-done.9, bf16[512,2048]{1,0:T(8,128)(2,1)S(1)} %copy-done.1, bf16[512,2048]{1,0:T(8,128)(2,1)S(1)} %copy-done.4, ...), custom_call_target="tpu_custom_call", output_to_operand_aliasing={{0}: (7, {})} | custom-call | flops 4300000256 | bytes 10750000 | tf_op jit(solution)/shard_map/pallas_call | solution.py:299
  112.3 3.8 %collective-permute-start.16 = (f32[512,128]{1,0:T(8,128)S(1)}, f32[512,128]{1,0:T(8,128)S(1)}, u32[]{:S(2)}, u32[]{:S(2)}) collective-permute-start(f32[512,128]{1,0:T(8,128)S(1)} %shard_map.122.refs_5_), channel_id=1, source_target_pairs={{0,24},{4,28},{8,0},{12,4},{16,8},{20,12},{24,16},{28,20},{1,25},{... | collective-permute-start | bytes 786440 | tf_op jit(solution)/shard_map/ppermute | solution.py:378
  117.2 4.9 %shard_map.124 = (bf16[512,2048]{1,0:T(8,128)(2,1)}, f32[512,512]{1,0:T(8,128)S(1)}, f32[512,512]{1,0:T(8,128)S(1)}) custom-call(s32[3]{0:T(128)S(1)} %pad_add_fusion.info_ref, bf16[512,2048]{1,0:T(8,128)(2,1)S(1)} %copy-done.9, bf16[512,2048]{1,0:T(8,128)(2,1)S(1)} %copy-done.1, bf16[512,2048]{1,0:T(8,128)(2,1)S(1)} %copy-done.4, ...), custom_call_target="tpu_custom_call", output_to_operand_aliasing={{0}: (7, {})} | custom-call | flops 4300000256 | bytes 10750000 | tf_op jit(solution)/shard_map/pallas_call | solution.py:299
  122.7 1.7 %collective-permute-start.17 = (f32[512,128]{1,0:T(8,128)S(1)}, f32[512,128]{1,0:T(8,128)S(1)}, u32[]{:S(2)}, u32[]{:S(2)}) collective-permute-start(f32[512,128]{1,0:T(8,128)S(1)} %get-tuple-element.86.refs_6_), channel_id=1, source_target_pairs={{0,4},{4,0},{8,12},{12,8},{16,20},{20,16},{24,28},{28,24},{1,5},{5... | collective-permute-start | bytes 786440 | tf_op jit(solution)/shard_map/ppermute | solution.py:388
  124.5 2.6 %shard_map.126 = (bf16[512,2048]{1,0:T(8,128)(2,1)}, bf16[512,2048]{1,0:T(8,128)(2,1)}) custom-call(s32[3]{0:T(128)S(1)} %pad_add_fusion.info_ref, f32[512,512]{1,0:T(8,128)S(1)} %get-tuple-element.77.refs_5_.refs_0_, f32[512,512]{1,0:T(8,128)S(1)} %get-tuple-element.90.refs_1_, bf16[512,2048]{1,0:T(8,128)(2,1)S(1)} %copy-done.1, ...), custom_call_target="tpu_custom_call" | custom-call | flops 2000000000 | bytes 5000000 | tf_op jit(solution)/shard_map/pallas_call | solution.py:299
  127.1 2.6 %shard_map.127 = (bf16[512,2048]{1,0:T(8,128)(2,1)}, bf16[512,2048]{1,0:T(8,128)(2,1)}) custom-call(s32[3]{0:T(128)S(1)} %pad_add_fusion.info_ref, f32[512,512]{1,0:T(8,128)S(1)} %get-tuple-element.81.refs_3_.refs_0_, f32[512,512]{1,0:T(8,128)S(1)} %get-tuple-element.88.refs_1_, ...), custom_call_target="tpu_custom_call", output_to_operand_aliasing={{0}: (7, {}), {1}: (8, {})} | custom-call | flops 2000000000 | bytes 5000000 | tf_op jit(solution)/shard_map/pallas_call | solution.py:299
  129.7 2.6 %shard_map.128 = (bf16[512,2048]{1,0:T(8,128)(2,1)}, bf16[512,2048]{1,0:T(8,128)(2,1)}) custom-call(s32[3]{0:T(128)S(1)} %pad_add_fusion.info_ref, f32[512,512]{1,0:T(8,128)S(1)} %get-tuple-element.79.refs_5_.refs_0_, f32[512,512]{1,0:T(8,128)S(1)} %get-tuple-element.87.refs_1_, ...), custom_call_target="tpu_custom_call", output_to_operand_aliasing={{0}: (7, {}), {1}: (8, {})} | custom-call | flops 2000000000 | bytes 5000000 | tf_op jit(solution)/shard_map/pallas_call | solution.py:299
  132.2 2.6 %shard_map.129 = (bf16[512,2048]{1,0:T(8,128)(2,1)}, bf16[512,2048]{1,0:T(8,128)(2,1)}) custom-call(s32[3]{0:T(128)S(1)} %pad_add_fusion.info_ref, f32[512,512]{1,0:T(8,128)S(1)} %get-tuple-element.84.refs_5_.refs_0_, f32[512,512]{1,0:T(8,128)S(1)} %get-tuple-element.85.refs_1_, ...), custom_call_target="tpu_custom_call", output_to_operand_aliasing={{0}: (7, {}), {1}: (8, {})} | custom-call | flops 2000000000 | bytes 5000000 | tf_op jit(solution)/shard_map/pallas_call | solution.py:299
  (98 shorter events, 34.2 us)
Async XLA Ops:
  7.8 10.5 %collective-permute-start.1 = (f32[520,128]{1,0:T(8,128)S(1)}, f32[520,128]{1,0:T(8,128)S(1)}, u32[]{:S(2)}, u32[]{:S(2)}) collective-permute-start(f32[520,128]{1,0:T(8,128)S(1)} %shard_map.94.refs_3_), channel_id=1, source_target_pairs={{0,4},{4,0},{8,12},{12,8},{16,20},{20,16},{24,28},{28,24},{1,5},{5... | collective-permute-start | bytes 798728 | tf_op jit(solution)/shard_map/ppermute | solution.py:358
  12.3 11.4 %collective-permute-start = (f32[520,128]{1,0:T(8,128)S(1)}, f32[520,128]{1,0:T(8,128)S(1)}, u32[]{:S(2)}, u32[]{:S(2)}) collective-permute-start(f32[520,128]{1,0:T(8,128)S(1)} %shard_map.95.refs_3_), channel_id=1, source_target_pairs={{0,4},{4,0},{8,12},{12,8},{16,20},{20,16},{24,28},{28,24},{1,5},{5... | collective-permute-start | bytes 798728 | tf_op jit(solution)/shard_map/ppermute | solution.py:358
  15.5 5.5 %copy-start.11 = (f32[16,512]{1,0:T(8,128)S(1)}, f32[16,512]{1,0:T(8,128)}, u32[]{:S(2)}) copy-start(f32[16,512]{1,0:T(8,128)} %shard_map.93.refs_2_.refs_3_.refs_4_) | copy-start | bytes 98308
  18.3 5.5 %copy-start.14 = (f32[512,512]{1,0:T(8,128)}, f32[512,512]{1,0:T(8,128)S(1)}, u32[]{:S(2)}) copy-start(f32[512,512]{1,0:T(8,128)S(1)} %shard_map.98.refs_3_.refs_0_) | copy-start | bytes 3145732
  18.3 2.7 %copy-start.1 = (bf16[512,2048]{1,0:T(8,128)(2,1)S(1)}, bf16[512,2048]{1,0:T(8,128)(2,1)}, u32[]{:S(2)}) copy-start(bf16[512,2048]{1,0:T(8,128)(2,1)} %refs_2_.31) | copy-start | bytes 6291460
  18.9 9.8 %collective-permute-start.2 = (f32[512,128]{1,0:T(8,128)S(1)}, f32[512,128]{1,0:T(8,128)S(1)}, u32[]{:S(2)}, u32[]{:S(2)}) collective-permute-start(f32[512,128]{1,0:T(8,128)S(1)} %shard_map.99.refs_4_), channel_id=1, source_target_pairs={{0,8},{4,12},{8,16},{12,20},{16,24},{20,28},{24,0},{28,4},{1,9},{5... | collective-permute-start | bytes 786440 | tf_op jit(solution)/shard_map/ppermute | solution.py:378
  23.7 8.5 %copy-start.16 = (f32[512,512]{1,0:T(8,128)}, f32[512,512]{1,0:T(8,128)S(1)}, u32[]{:S(2)}) copy-start(f32[512,512]{1,0:T(8,128)S(1)} %shard_map.100.refs_5_.refs_0_) | copy-start | bytes 3145732
  23.8 5.7 %copy-start.3 = (bf16[512,2048]{1,0:T(8,128)(2,1)S(1)}, bf16[512,2048]{1,0:T(8,128)(2,1)}, u32[]{:S(2)}) copy-start(bf16[512,2048]{1,0:T(8,128)(2,1)} %refs_3_.15) | copy-start | bytes 6291460
  29.4 8.7 %collective-permute-start.3 = (f32[512,128]{1,0:T(8,128)S(1)}, f32[512,128]{1,0:T(8,128)S(1)}, u32[]{:S(2)}, u32[]{:S(2)}) collective-permute-start(f32[512,128]{1,0:T(8,128)S(1)} %shard_map.101.refs_4_), channel_id=1, source_target_pairs={{0,8},{4,12},{8,16},{12,20},{16,24},{20,28},{24,0},{28,4},{1,9},{5... | collective-permute-start | bytes 786440 | tf_op jit(solution)/shard_map/ppermute | solution.py:378
  32.2 6.5 %copy-start.18 = (f32[512,512]{1,0:T(8,128)}, f32[512,512]{1,0:T(8,128)S(1)}, u32[]{:S(2)}) copy-start(f32[512,512]{1,0:T(8,128)S(1)} %shard_map.102.refs_5_.refs_0_) | copy-start | bytes 3145732
  38.7 8.2 %collective-permute-start.4 = (f32[512,128]{1,0:T(8,128)S(1)}, f32[512,128]{1,0:T(8,128)S(1)}, u32[]{:S(2)}, u32[]{:S(2)}) collective-permute-start(f32[512,128]{1,0:T(8,128)S(1)} %shard_map.103.refs_4_), channel_id=1, source_target_pairs={{0,8},{4,12},{8,16},{12,20},{16,24},{20,28},{24,0},{28,4},{1,9},{5... | collective-permute-start | bytes 786440 | tf_op jit(solution)/shard_map/ppermute | solution.py:378
  41.5 11.5 %copy-start.25 = (f32[2048]{0:T(1024)S(1)}, f32[2048]{0:T(1024)}, u32[]{:S(2)}) copy-start(f32[2048]{0:T(1024)} %param.10) | copy-start | bytes 24580
  49.1 9.0 %collective-permute-start.5 = (f32[512,128]{1,0:T(8,128)}, f32[512,128]{1,0:T(8,128)}, u32[]{:S(2)}, u32[]{:S(2)}) collective-permute-start(f32[512,128]{1,0:T(8,128)} %shard_map.105.refs_5_), channel_id=1, source_target_pairs={{0,8},{4,12},{8,16},{12,20},{16,24},{20,28},{24,0},{28,4},{1,9},{5... | collective-permute-start | bytes 786440 | tf_op jit(solution)/shard_map/ppermute | solution.py:378
  51.7 10.9 %collective-permute-start.7 = (f32[512,128]{1,0:T(8,128)S(1)}, f32[512,128]{1,0:T(8,128)S(1)}, u32[]{:S(2)}, u32[]{:S(2)}) collective-permute-start(f32[512,128]{1,0:T(8,128)S(1)} %get-tuple-element.53.refs_7_), channel_id=1, source_target_pairs={{0,4},{4,0},{8,12},{12,8},{16,20},{20,16},{24,28},{28,24},{1,5},{5... | collective-permute-start | bytes 786440 | tf_op jit(solution)/shard_map/ppermute | solution.py:388
  56.2 2.0 %copy-start.22 = (f32[512,128]{1,0:T(8,128)S(1)}, f32[512,128]{1,0:T(8,128)}, u32[]{:S(2)}) copy-start(f32[512,128]{1,0:T(8,128)} %copy-done.20) | copy-start | bytes 786436
  56.2 4.4 %copy-start.6 = (bf16[512,2048]{1,0:T(8,128)(2,1)S(1)}, bf16[512,2048]{1,0:T(8,128)(2,1)}, u32[]{:S(2)}) copy-start(bf16[512,2048]{1,0:T(8,128)(2,1)} %refs_1_.35) | copy-start | bytes 6291460
  56.2 4.4 %copy-start.9 = (bf16[512,2048]{1,0:T(8,128)(2,1)S(1)}, bf16[512,2048]{1,0:T(8,128)(2,1)}, u32[]{:S(2)}) copy-start(bf16[512,2048]{1,0:T(8,128)(2,1)} %refs_0_.23) | copy-start | bytes 6291460
  56.2 4.4 %copy-start.19 = (f32[512,512]{1,0:T(8,128)S(1)}, f32[512,512]{1,0:T(8,128)}, u32[]{:S(2)}) copy-start(f32[512,512]{1,0:T(8,128)} %copy-done.18) | copy-start | bytes 3145732
  59.8 6.4 %collective-permute-start.6 = (f32[512,128]{1,0:T(8,128)S(1)}, f32[512,128]{1,0:T(8,128)S(1)}, u32[]{:S(2)}, u32[]{:S(2)}) collective-permute-start(f32[512,128]{1,0:T(8,128)S(1)} %get-tuple-element.56.refs_7_), channel_id=1, source_target_pairs={{0,4},{4,0},{8,12},{12,8},{16,20},{20,16},{24,28},{28,24},{1,5},{5... | collective-permute-start | bytes 786440 | tf_op jit(solution)/shard_map/ppermute | solution.py:388
  62.6 3.6 %copy-start.13 = (f32[512,512]{1,0:T(8,128)S(1)}, f32[512,512]{1,0:T(8,128)}, u32[]{:S(2)}) copy-start(f32[512,512]{1,0:T(8,128)} %copy-done.12) | copy-start | bytes 3145732
  68.2 1.9 %collective-permute-start.10 = (f32[8,512]{1,0:T(8,128)S(1)}, f32[8,512]{1,0:T(8,128)S(1)}, u32[]{:S(2)}, u32[]{:S(2)}) collective-permute-start(f32[8,512]{1,0:T(8,128)S(1)} %get-tuple-element.60.refs_5_), channel_id=1, source_target_pairs={{0,3},{1,0},{2,1},{3,2},{4,7},{5,4},{6,5},{7,6},{8,11},{9,8},{10,9... | collective-permute-start | bytes 49160 | tf_op jit(solution)/shard_map/ppermute | solution.py:437
  68.2 3.8 %collective-permute-start.9 = (f32[8,512]{1,0:T(8,128)S(1)}, f32[8,512]{1,0:T(8,128)S(1)}, u32[]{:S(2)}, u32[]{:S(2)}) collective-permute-start(f32[8,512]{1,0:T(8,128)S(1)} %get-tuple-element.60.refs_5_), channel_id=1, source_target_pairs={{0,2},{1,3},{2,0},{3,1},{4,6},{5,7},{6,4},{7,5},{8,10},{9,11},{10,... | collective-permute-start | bytes 49160 | tf_op jit(solution)/shard_map/ppermute | solution.py:437
  69.8 3.2 %collective-permute-start.8 = (f32[8,512]{1,0:T(8,128)S(1)}, f32[8,512]{1,0:T(8,128)S(1)}, u32[]{:S(2)}, u32[]{:S(2)}) collective-permute-start(f32[8,512]{1,0:T(8,128)S(1)} %get-tuple-element.60.refs_5_), channel_id=1, source_target_pairs={{0,1},{1,2},{2,3},{3,0},{4,5},{5,6},{6,7},{7,4},{8,9},{9,10},{10,1... | collective-permute-start | bytes 49160 | tf_op jit(solution)/shard_map/ppermute | solution.py:437
  75.4 9.4 %collective-permute-start.11 = (f32[520,128]{1,0:T(8,128)S(1)}, f32[520,128]{1,0:T(8,128)S(1)}, u32[]{:S(2)}, u32[]{:S(2)}) collective-permute-start(f32[520,128]{1,0:T(8,128)S(1)} %get-tuple-element.65.refs_10_), channel_id=1, source_target_pairs={{0,4},{4,0},{8,12},{12,8},{16,20},{20,16},{24,28},{28,24},{1,5},{5... | collective-permute-start | bytes 798728 | tf_op jit(solution)/shard_map/ppermute | solution.py:358
  78.6 15.6 %collective-permute-start.12 = (f32[520,128]{1,0:T(8,128)S(1)}, f32[520,128]{1,0:T(8,128)S(1)}, u32[]{:S(2)}, u32[]{:S(2)}) collective-permute-start(f32[520,128]{1,0:T(8,128)S(1)} %get-tuple-element.67.refs_10_), channel_id=1, source_target_pairs={{0,4},{4,0},{8,12},{12,8},{16,20},{20,16},{24,28},{28,24},{1,5},{5... | collective-permute-start | bytes 798728 | tf_op jit(solution)/shard_map/ppermute | solution.py:358
  82.4 6.9 %copy-start.4 = (bf16[512,2048]{1,0:T(8,128)(2,1)S(1)}, bf16[512,2048]{1,0:T(8,128)(2,1)}, u32[]{:S(2)}) copy-start(bf16[512,2048]{1,0:T(8,128)(2,1)} %refs_3_.15) | copy-start | bytes 6291460
  85.4 8.8 %collective-permute-start.13 = (f32[512,128]{1,0:T(8,128)S(1)}, f32[512,128]{1,0:T(8,128)S(1)}, u32[]{:S(2)}, u32[]{:S(2)}) collective-permute-start(f32[512,128]{1,0:T(8,128)S(1)} %shard_map.116.refs_6_), channel_id=1, source_target_pairs={{0,24},{4,28},{8,0},{12,4},{16,8},{20,12},{24,16},{28,20},{1,25},{... | collective-permute-start | bytes 786440 | tf_op jit(solution)/shard_map/ppermute | solution.py:378
  94.7 8.3 %collective-permute-start.14 = (f32[512,128]{1,0:T(8,128)S(1)}, f32[512,128]{1,0:T(8,128)S(1)}, u32[]{:S(2)}, u32[]{:S(2)}) collective-permute-start(f32[512,128]{1,0:T(8,128)S(1)} %shard_map.118.refs_7_), channel_id=1, source_target_pairs={{0,24},{4,28},{8,0},{12,4},{16,8},{20,12},{24,16},{28,20},{1,25},{... | collective-permute-start | bytes 786440 | tf_op jit(solution)/shard_map/ppermute | solution.py:378
  103.6 8.2 %collective-permute-start.15 = (f32[512,128]{1,0:T(8,128)S(1)}, f32[512,128]{1,0:T(8,128)S(1)}, u32[]{:S(2)}, u32[]{:S(2)}) collective-permute-start(f32[512,128]{1,0:T(8,128)S(1)} %shard_map.120.refs_7_), channel_id=1, source_target_pairs={{0,24},{4,28},{8,0},{12,4},{16,8},{20,12},{24,16},{28,20},{1,25},{... | collective-permute-start | bytes 786440 | tf_op jit(solution)/shard_map/ppermute | solution.py:378
  112.3 9.8 %collective-permute-start.16 = (f32[512,128]{1,0:T(8,128)S(1)}, f32[512,128]{1,0:T(8,128)S(1)}, u32[]{:S(2)}, u32[]{:S(2)}) collective-permute-start(f32[512,128]{1,0:T(8,128)S(1)} %shard_map.122.refs_5_), channel_id=1, source_target_pairs={{0,24},{4,28},{8,0},{12,4},{16,8},{20,12},{24,16},{28,20},{1,25},{... | collective-permute-start | bytes 786440 | tf_op jit(solution)/shard_map/ppermute | solution.py:378
  116.8 12.9 %collective-permute-start.18 = (f32[512,128]{1,0:T(8,128)S(1)}, f32[512,128]{1,0:T(8,128)S(1)}, u32[]{:S(2)}, u32[]{:S(2)}) collective-permute-start(f32[512,128]{1,0:T(8,128)S(1)} %get-tuple-element.82.refs_7_), channel_id=1, source_target_pairs={{0,4},{4,0},{8,12},{12,8},{16,20},{20,16},{24,28},{28,24},{1,5},{5... | collective-permute-start | bytes 786440 | tf_op jit(solution)/shard_map/ppermute | solution.py:388
  122.7 9.5 %collective-permute-start.17 = (f32[512,128]{1,0:T(8,128)S(1)}, f32[512,128]{1,0:T(8,128)S(1)}, u32[]{:S(2)}, u32[]{:S(2)}) collective-permute-start(f32[512,128]{1,0:T(8,128)S(1)} %get-tuple-element.86.refs_6_), channel_id=1, source_target_pairs={{0,4},{4,0},{8,12},{12,8},{16,20},{20,16},{24,28},{28,24},{1,5},{5... | collective-permute-start | bytes 786440 | tf_op jit(solution)/shard_map/ppermute | solution.py:388
  (13 other events, 17.5 us)

commit v2 on v1

--- a/solution.py
+++ b/solution.py
@@ -37,8 +37,7 @@
     return jnp.concatenate([col] * (width // HEAD_DIM), axis=1)
 
 
-def cumul_kernel(decay_ref, out_ref):
-    decay = decay_ref[...]
+def cumulative(decay):
     length = decay.shape[1]
     first = decay.astype(bf16)
     rest = decay - first.astype(f32)
@@ -48,7 +47,7 @@
         jnp.int32, (length, length), 1
     )
     upto = jnp.where(upto, 1.0, 0.0).astype(bf16)
-    out_ref[...] = dot(first, upto) + dot(second, upto) + dot(third, upto)
+    return dot(first, upto) + dot(second, upto) + dot(third, upto)
 
 
 def trail_row(row):
@@ -72,7 +71,7 @@
         self.per_step = half // self.steps
 
     def group(self, info):
-        return info[0] if self.slot == "mine" else 1 - info[0]
+        return info[0][0] if self.slot == "mine" else 1 - info[0][0]
 
     def row(self, cumul_ref, info, j):
         head = (2 * self.chunk + self.group(info)) * self.half + pl.program_id(0) * self.per_step + j
@@ -97,6 +96,14 @@
             key_ref[:, cols(j)], trail_row(row), value_ref[:, cols(j)]
         )
     store_decays(part, info, cumul_ref, out_ref)
+
+
+def first_pieces_kernel(part, info, key_ref, value_ref, decay_ref, out_ref, cumul_ref):
+    @pl.when(pl.program_id(0) == 0)
+    def _():
+        cumul_ref[...] = cumulative(decay_ref[...])
+
+    pieces_kernel(part, info, key_ref, value_ref, cumul_ref, out_ref)
 
 
 def inner_kernel(part, info, query_ref, key_ref, value_ref, cumul_ref, out_ref):
@@ -232,16 +239,24 @@
     )
 
 
-def hop_kernel(half, senders, info, *refs):
+def scan_position(places, forward, info):
+    member, pair = info[0][0], info[1][0]
+    if forward:
+        return member == 0, pair
+    return member == 1, places - 1 - pair
+
+
+def hop_kernel(half, senders, position, info, *refs):
+    is_first, place = position(info)
     out_ref, arrived_ref = refs[-1], refs[-2]
     for index, p in enumerate(senders):
         keep_ref, got_ref = refs[2 * index], refs[2 * index + 1]
 
-        @pl.when(info[2] == p)
+        @pl.when(place == p)
         def _():
             for j in range(half):
                 first, second, first_decay, second_decay = ordered(
-                    info[1] == 1, half, j, keep_ref, got_ref
+                    is_first, half, j, keep_ref, got_ref
                 )
                 value = second_decay * first + second
                 if p > 0:
@@ -249,12 +264,12 @@
                 out_ref[cols(j), :] = value
 
 
-def last_kernel(half, info, keep_ref, got_ref, *refs):
+def last_kernel(half, position, info, keep_ref, got_ref, *refs):
     arrived, (mine_ref, send_ref) = refs[:-2], refs[-2:]
-    is_first = info[1] == 1
+    is_first, place = position(info)
     for p in range(len(arrived) + 1):
 
-        @pl.when(info[2] == p)
+        @pl.when(place == p)
         def _():
             for j in range(half):
                 first, _, first_decay, _ = ordered(is_first, half, j, keep_ref, got_ref)
@@ -286,35 +301,34 @@
     local = jax.ShapeDtypeStruct((tokens, half * HEAD_DIM), f32)
     local_low = jax.ShapeDtypeStruct((tokens, half * HEAD_DIM), bf16)
     sums_shape = jax.ShapeDtypeStruct((8, tokens), f32)
-    forward_info = jnp.stack([member, 1 - member, pair]).astype(jnp.int32)
-    backward_info = jnp.stack([member, member, places - 1 - pair]).astype(jnp.int32)
-
-    def run(kernel, info, grid, ins, outs, scratch=(), after=(), aliases=None, cost=1.0):
+    info = (member.astype(jnp.int32).reshape(1), pair.astype(jnp.int32).reshape(1))
+
+    def run(kernel, grid, ins, outs, scratch=(), after=(), aliases=None, cost=1.0):
         used = len(ins)
         after = [x for i, x in enumerate(after) if not any(x is y for y in after[:i])]
 
-        def body(info_ref, *refs):
-            kernel(info_ref, *refs[:used], *refs[used + len(after):])
+        def body(member_ref, pair_ref, *refs):
+            kernel((member_ref, pair_ref), *refs[:used], *refs[used + len(after):])
 
         return pl.pallas_call(
             body,
             out_shape=[shape for shape, _ in outs],
             grid_spec=pltpu.PrefetchScalarGridSpec(
-                num_scalar_prefetch=1,
+                num_scalar_prefetch=2,
                 grid=(grid,),
                 in_specs=[spec for _, spec in ins] + [any_spec] * len(after),
                 out_specs=[spec for _, spec in outs],
                 scratch_shapes=list(scratch),
             ),
             input_output_aliases=aliases or {},
-            compiler_params=pltpu.CompilerParams(vmem_limit_bytes=16 * 1024 * 1024),
+            compiler_params=pltpu.CompilerParams(vmem_limit_bytes=60 * 1024 * 1024),
             cost_estimate=pl.CostEstimate(
                 flops=int(cost * 1e9), bytes_accessed=int(cost * 2.5e6), transcendentals=0
             ),
-        )(info, *[array for array, _ in ins], *after)
+        )(*info, *[array for array, _ in ins], *after)
 
     def fixed(shape):
-        return pl.BlockSpec(shape, lambda i, info: (0,) * len(shape))
+        return pl.BlockSpec(shape, lambda i, *info: (0,) * len(shape))
 
     def plain(array):
         return array, fixed(array.shape)
@@ -329,29 +343,26 @@
         def full_spec(self, rows=tokens):
             return pl.BlockSpec(
                 (rows, self.per_step * HEAD_DIM),
-                lambda i, info: (0, (2 * self.chunk + self.group(info)) * self.steps + i),
+                lambda i, *info: (0, (2 * self.chunk + self.group(info)) * self.steps + i),
             )
 
         def local(self, array):
-            return array, pl.BlockSpec((tokens, self.per_step * HEAD_DIM), lambda i, info: (0, i))
+            return array, pl.BlockSpec((tokens, self.per_step * HEAD_DIM), lambda i, *info: (0, i))
 
         def call(self, kernel, ins, outs, **options):
-            return run(functools.partial(kernel, self), forward_info, self.steps, ins, outs, **options)
+            return run(functools.partial(kernel, self), self.steps, ins, outs, **options)
 
     mine_parts = [Views(c, "mine", half) for c in range(CHUNKS)]
     their_parts = [Views(c, "theirs", half) for c in range(CHUNKS)]
 
-    cumul = pl.pallas_call(
-        cumul_kernel, out_shape=jax.ShapeDtypeStruct((heads, tokens), f32)
-    )(log_decay.T)
-
     swap = [(2 * p + m, 2 * p + 1 - m) for p in range(places) for m in (0, 1)]
 
-    def chain(make_piece, info, forward, early, filler, on_mine):
-        step = 1 if forward else -1
-        ring = [
-            (2 * p + m, 2 * ((p + step) % places) + m) for p in range(places) for m in (0, 1)
-        ]
+    def chain(make_piece, forward, early, filler, on_mine):
+        position = functools.partial(scan_position, places, forward)
+
+        def device(place, m):
+            return 2 * (place if forward else places - 1 - place) + m
+
         received, last = [], ()
         for c in range(CHUNKS):
             sent = make_piece(their_parts[c], last)
@@ -372,17 +383,18 @@
                     ins += [plain(keeps[r - 2 - p]), plain(received[r - 2 - p])]
                 ins.append(plain(arrived[r - 1]) if r > 2 else plain(keeps[0]))
                 value, = run(
-                    functools.partial(hop_kernel, half, senders), info, 1, ins, [give(state)],
+                    functools.partial(hop_kernel, half, senders, position), 1, ins, [give(state)],
                     after=last, cost=0.3,
                 )
-                arrived[r] = lax.ppermute(value, "seq", ring)
+                pairs = [(device(p, m), device(p + 1, m)) for p in senders for m in (0, 1)]
+                arrived[r] = lax.ppermute(value, "seq", pairs)
                 last = (value,)
             c = r - 1 - places
             if 0 <= c:
                 ins = [plain(keeps[c]), plain(received[c])]
                 ins += [plain(arrived[c + 1 + p]) for p in range(1, places)]
                 own, send = run(
-                    functools.partial(last_kernel, half), info, 1, ins, [give(state)] * 2,
+                    functools.partial(last_kernel, half, position), 1, ins, [give(state)] * 2,
                     after=last, cost=0.3,
                 )
                 theirs.append(lax.ppermute(send, "seq", swap))
@@ -395,19 +407,34 @@
             last = (filler.pop(0)(last),)
         return mine, theirs, last
 
+    held_cumul = []
+
     def forward_piece(part, after):
+        if not held_cumul:
+            piece, cumul = part.call(
+                first_pieces_kernel,
+                [part.full(key_vecs), part.full(value_vecs), plain(log_decay.T)],
+                [give(wide_state), give(jax.ShapeDtypeStruct((heads, tokens), f32))], cost=1.0,
+            )
+            held_cumul.append(cumul)
+            return piece
+        cumul = held_cumul[0]
         return part.call(
             pieces_kernel, [part.full(key_vecs), part.full(value_vecs), plain(cumul)],
             [give(wide_state)], after=after, cost=1.0,
         )[0]
 
     inner, outs = {}, {}
+
+    def cumul_in():
+        return plain(held_cumul[0])
+
     state_sums = [jnp.zeros(sums_shape.shape, f32)]
 
     def inner_work(part, after):
         inner[part], = part.call(
             inner_kernel,
-            [part.full(queries), part.full(key_vecs), part.full(value_vecs), plain(cumul)],
+            [part.full(queries), part.full(key_vecs), part.full(value_vecs), cumul_in()],
             [part.local(local)], after=after, cost=2.2,
         )
         return inner[part]
@@ -416,7 +443,7 @@
         outs[part], sums = part.call(
             output_kernel,
             [part.local(inner[part]), part.full(queries), part.full(cotangent), part.full(gain, 1),
-             plain(cumul), plain(before), plain(state_sums[0])],
+             cumul_in(), plain(before), plain(state_sums[0])],
             [part.local(local), give(sums_shape)],
             scratch=[pltpu.VMEM((tokens, HEAD_DIM), f32)] * 2, after=after, cost=1.4,
         )
@@ -426,7 +453,7 @@
     inner_order = [part for c in range(CHUNKS) for part in (mine_parts[c], their_parts[c])]
     works = [functools.partial(inner_work, part) for part in inner_order]
     mine, theirs, last = chain(
-        forward_piece, forward_info, True, works[:1], works[1:],
+        forward_piece, True, works[:1], works[1:],
         lambda c, own, after: output_work(mine_parts[c], own, after),
     )
     for c in range(CHUNKS):
@@ -449,9 +476,9 @@
         whole_out, grads[part], piece = part.call(
             functools.partial(grad_kernel, features),
             [part.local(outs[part]), part.full(cotangent), part.full(gain, 1), part.full(queries),
-             plain(cumul)] + [plain(share) for share in shares],
+             cumul_in()] + [plain(share) for share in shares],
             [(whole, part.full_spec()), part.local(local_low), give(wide_state)],
-            after=before + tuple(after), aliases={6 + head_count: 0} if before else None, cost=2.0,
+            after=before + tuple(after), aliases={7 + head_count: 0} if before else None, cost=2.0,
         )
         attended.append(whole_out)
         return piece
@@ -461,9 +488,9 @@
         whole_out, *inner_grads[part] = part.call(
             backward_kernel,
             [part.full(queries), part.full(key_vecs), part.full(value_vecs),
-             part.local(grads[part]), plain(cumul), plain(before)],
+             part.local(grads[part]), cumul_in(), plain(before)],
             [(whole, part.full_spec()), part.local(local), part.local(local)],
-            after=held + tuple(after), aliases={7: 0} if held else None, cost=4.3,
+            after=held + tuple(after), aliases={8: 0} if held else None, cost=4.3,
         )
         grad_queries.append(whole_out)
         return inner_grads[part][0]
@@ -473,9 +500,9 @@
         whole_key, whole_value = part.call(
             final_kernel,
             [part.local(inner_grads[part][0]), part.local(inner_grads[part][1]),
-             part.full(key_vecs), part.full(value_vecs), plain(cumul), plain(before)],
+             part.full(key_vecs), part.full(value_vecs), cumul_in(), plain(before)],
             [(whole, part.full_spec())] * 2,
-            after=held + tuple(after), aliases={7: 0, 8: 1} if held else None, cost=2.0,
+            after=held + tuple(after), aliases={8: 0, 9: 1} if held else None, cost=2.0,
         )
         grad_keys.append(whole_key)
         grad_values.append(whole_value)
@@ -486,7 +513,7 @@
         works.append(functools.partial(backward_work, mine_parts[c], mine[c]))
         works.append(functools.partial(backward_work, their_parts[c], theirs[c]))
     mine_after, theirs_after, last = chain(
-        backward_piece, backward_info, False, [], works,
+        backward_piece, False, [], works,
         lambda c, own, after: final_work(mine_parts[c], own, after),
     )
     for c in range(CHUNKS):

time: 135 us -> 163 us (1.21)
  Pallas kernels: 74.7 us -> 111 us
  waiting for transfers between devices: 20.8 us -> 15.1 us
  starting transfers between devices: 27.8 us -> 24.3 us
    pallas_call x36, Pallas kernels: 73.1 us -> 111 us  [run(): pl.pallas_call(body, out_shape=[shape for shape, _ in outs], grid_spec=pl...]
    ppermute x8, waiting for transfers between devices: 16.2 us -> 11.9 us  [chain(): arrived[r] = lax.ppermute(value, 'seq', pairs)]
    ppermute x8, starting transfers between devices: 16.6 us -> 13.4 us  [chain(): arrived[r] = lax.ppermute(value, 'seq', pairs)]
    pallas_call x1 -> x0, Pallas kernels: 1.66 us -> none  [on_device(): pl.pallas_call(cumul_kernel, out_shape=jax.ShapeDtypeStruct((heads, token...]
    ppermute x4, waiting for transfers between devices: 1.66 us -> 0.01 us  [chain(): theirs.append(lax.ppermute(send, 'seq', swap))]
    unnamed x52 -> x38, local copies, waits for them, and re-layouts: 10.2 us -> 10.6 us
  transfers between devices with their start and end apart: 19 -> 19, of which waited for: 6 -> 5; matrix products, arithmetic and copies ran while one was open for 0% -> 0% of each run, Pallas kernels for 45% -> 53%
where the time goes in v2:
time: 163 us; the launch traced here: 162 us
  Pallas kernels  111 us (68%)
  starting transfers between devices  24.3 us (15%)
  waiting for transfers between devices  15.1 us (9%)
  local copies, waits for them, and re-layouts  11.2 us (7%)
    pallas_call x36, Pallas kernels, run(): pl.pallas_call(body, out_shape=[shape for shape, _ in outs], grid_spec=pl...  111 us
    ppermute x8, starting transfers between devices, chain(): arrived[r] = lax.ppermute(value, 'seq', pairs)  13.4 us
    ppermute x8, waiting for transfers between devices, chain(): arrived[r] = lax.ppermute(value, 'seq', pairs)  11.9 us
    unnamed x38, local copies, waits for them, and re-layouts  10.6 us
    ppermute x4, starting transfers between devices, chain(): received.append(lax.ppermute(sent, 'seq', swap))  5.1 us
    ppermute x4, starting transfers between devices, chain(): theirs.append(lax.ppermute(send, 'seq', swap))  4.05 us
  transfers between devices with their start and end apart: 19, of which 5 were waited for; matrix products, arithmetic and copies ran while one was open for 0% of the time, Pallas kernels for 53%

profile of v2, /device:TPU:0, one launch (start us, length us, event | category | flops | bytes accessed | tf_op | source)
XLA Modules:
  0.0 162.3 jit_solution(7774065224973594155)
XLA Ops:
  0.6 2.8 %shard_map.93 = (f32[520,128]{1,0:T(8,128)}, f32[16,512]{1,0:T(8,128)}) custom-call(s32[1]{0:T(128)} %bitcast.member_ref, s32[1]{0:T(128)} %bitcast.1.pair_ref, bf16[512,2048]{1,0:T(8,128)(2,1)} %refs_2_.31, bf16[512,2048]{1,0:T(8,128)(2,1)} %refs_3_.15, f32[16,512]{1,0:T(8,128)} %bitcast.12), custom_call_target="tpu_custom_call" | custom-call | flops 1000000000 | bytes 2500000 | tf_op jit(solution)/shard_map/pallas_call | solution.py:313
  3.5 3.0 %collective-permute-start.1 = (f32[520,128]{1,0:T(8,128)}, f32[520,128]{1,0:T(8,128)S(1)}, u32[]{:S(2)}, u32[]{:S(2)}) collective-permute-start(f32[520,128]{1,0:T(8,128)} %get-tuple-element.55.refs_3_), channel_id=1, source_target_pairs={{0,4},{4,0},{8,12},{12,8},{16,20},{20,16},{24,28},{28,24},{1,5},{5... | collective-permute-start | bytes 798728 | tf_op jit(solution)/shard_map/ppermute | solution.py:369
  6.4 2.5 %shard_map.94.refs_3_ = f32[520,128]{1,0:T(8,128)} custom-call(s32[1]{0:T(128)} %bitcast.member_ref, s32[1]{0:T(128)} %bitcast.1.pair_ref, bf16[512,2048]{1,0:T(8,128)(2,1)} %refs_2_.31, bf16[512,2048]{1,0:T(8,128)(2,1)} %refs_3_.15, f32[16,512]{1,0:T(8,128)} %get-tuple-element.54.refs_2_.refs_3_.refs_4_, f32[520,128]{1,0:T(8,128)} %get-tuple-element.55.refs_3_), custom_call_target="tpu_custom_call" | custom-call | flops 1000000000 | bytes 2500000 | tf_op jit(solution)/shard_map/pallas_call | solution.py:313
  8.9 2.5 %shard_map.95.refs_3_.refs_0_.refs_2_ = f32[520,128]{1,0:T(8,128)} custom-call(s32[1]{0:T(128)} %bitcast.member_ref, s32[1]{0:T(128)} %bitcast.1.pair_ref, bf16[512,2048]{1,0:T(8,128)(2,1)} %refs_2_.31, bf16[512,2048]{1,0:T(8,128)(2,1)} %refs_3_.15, f32[16,512]{1,0:T(8,128)} %get-tuple-element.54.refs_2_.refs_3_.refs_4_, f32[520,128]{1,0:T(8,128)} %shard_map.94.refs_3_), custom_call_target="tpu_custom_call" | custom-call | flops 1000000000 | bytes 2500000 | tf_op jit(solution)/shard_map/pallas_call | solution.py:313
  11.5 2.5 %shard_map.96.refs_4_.refs_0_ = f32[520,128]{1,0:T(8,128)} custom-call(s32[1]{0:T(128)} %bitcast.member_ref, s32[1]{0:T(128)} %bitcast.1.pair_ref, bf16[512,2048]{1,0:T(8,128)(2,1)} %refs_2_.31, bf16[512,2048]{1,0:T(8,128)(2,1)} %refs_3_.15, f32[16,512]{1,0:T(8,128)} %get-tuple-element.54.refs_2_.refs_3_.refs_4_, f32[520,128]{1,0:T(8,128)} %shard_map.95.refs_3_.refs_0_.refs_2_), custom_call_target="tpu_custom_call" | custom-call | flops 1000000000 | bytes 2500000 | tf_op jit(solution)/shard_map/pallas_call | solution.py:313
  14.0 3.8 %shard_map.97.refs_3_.refs_0_ = f32[512,512]{1,0:T(8,128)} custom-call(s32[1]{0:T(128)} %bitcast.member_ref, s32[1]{0:T(128)} %bitcast.1.pair_ref, bf16[512,2048]{1,0:T(8,128)(2,1)} %refs_0_.23, bf16[512,2048]{1,0:T(8,128)(2,1)} %refs_2_.31, bf16[512,2048]{1,0:T(8,128)(2,1)} %refs_3_.15, f32[16,512]{1,0:T(8,128)} %get-tuple-element.54.refs_2_.refs_3_.refs_4_, ...), custom_call_target="tpu_custom_call" | custom-call | flops 2200000000 | bytes 5500000 | tf_op jit(solution)/shard_map/pallas_call | solution.py:313
  20.4 3.9 %collective-permute-start.2 = (f32[512,128]{1,0:T(8,128)}, f32[512,128]{1,0:T(8,128)S(1)}, u32[]{:S(2)}, u32[]{:S(2)}) collective-permute-start(f32[512,128]{1,0:T(8,128)} %shard_map.98.refs_4_), channel_id=1, source_target_pairs={{0,8},{4,12},{1,9},{5,13},{2,10},{6,14},{3,11},{7,15}} | collective-permute-start | bytes 786440 | tf_op jit(solution)/shard_map/ppermute | solution.py:390
  24.3 3.8 %shard_map.99.refs_5_.refs_0_ = f32[512,512]{1,0:T(8,128)} custom-call(s32[1]{0:T(128)} %bitcast.member_ref, s32[1]{0:T(128)} %bitcast.1.pair_ref, bf16[512,2048]{1,0:T(8,128)(2,1)} %refs_0_.23, bf16[512,2048]{1,0:T(8,128)(2,1)} %refs_2_.31, bf16[512,2048]{1,0:T(8,128)(2,1)} %refs_3_.15, f32[16,512]{1,0:T(8,128)} %get-tuple-element.54.refs_2_.refs_3_.refs_4_, ...), custom_call_target="tpu_custom_call" | custom-call | flops 2200000000 | bytes 5500000 | tf_op jit(solution)/shard_map/pallas_call | solution.py:313
  32.3 4.3 %collective-permute-start.3 = (f32[512,128]{1,0:T(8,128)}, f32[512,128]{1,0:T(8,128)S(1)}, u32[]{:S(2)}, u32[]{:S(2)}) collective-permute-start(f32[512,128]{1,0:T(8,128)} %shard_map.100.refs_4_), channel_id=1, source_target_pairs={{0,8},{4,12},{8,16},{12,20},{1,9},{5,13},{9,17},{13,21},{2,10},{6,... | collective-permute-start | bytes 786440 | tf_op jit(solution)/shard_map/ppermute | solution.py:390
  36.7 3.8 %shard_map.101.refs_5_.refs_0_ = f32[512,512]{1,0:T(8,128)} custom-call(s32[1]{0:T(128)} %bitcast.member_ref, s32[1]{0:T(128)} %bitcast.1.pair_ref, bf16[512,2048]{1,0:T(8,128)(2,1)} %refs_0_.23, bf16[512,2048]{1,0:T(8,128)(2,1)} %refs_2_.31, bf16[512,2048]{1,0:T(8,128)(2,1)} %refs_3_.15, f32[16,512]{1,0:T(8,128)} %get-tuple-element.54.refs_2_.refs_3_.refs_4_, ...), custom_call_target="tpu_custom_call" | custom-call | flops 2200000000 | bytes 5500000 | tf_op jit(solution)/shard_map/pallas_call | solution.py:313
  44.4 3.9 %shard_map.103.refs_3_.refs_0_ = f32[512,512]{1,0:T(8,128)} custom-call(s32[1]{0:T(128)} %bitcast.member_ref, s32[1]{0:T(128)} %bitcast.1.pair_ref, bf16[512,2048]{1,0:T(8,128)(2,1)} %refs_0_.23, bf16[512,2048]{1,0:T(8,128)(2,1)} %refs_2_.31, bf16[512,2048]{1,0:T(8,128)(2,1)} %refs_3_.15, f32[16,512]{1,0:T(8,128)} %get-tuple-element.54.refs_2_.refs_3_.refs_4_, ...), custom_call_target="tpu_custom_call" | custom-call | flops 2200000000 | bytes 5500000 | tf_op jit(solution)/shard_map/pallas_call | solution.py:313
  55.7 3.3 %shard_map.106 = (f32[512,512]{1,0:T(8,128)}, f32[8,512]{1,0:T(8,128)}) custom-call(s32[1]{0:T(128)} %bitcast.member_ref, s32[1]{0:T(128)} %bitcast.1.pair_ref, f32[512,512]{1,0:T(8,128)} %shard_map.97.refs_3_.refs_0_, bf16[512,2048]{1,0:T(8,128)(2,1)} %refs_0_.23, bf16[512,2048]{1,0:T(8,128)(2,1)} %refs_1_.35, f32[1,2048]{1,0:T(1,128)} %bitcast.4, ...), custom_call_target="tpu_custom_call" | custom-call | flops 1400000000 | bytes 3500000 | tf_op jit(solution)/shard_map/pallas_call | solution.py:313
  59.6 2.1 %shard_map.107 = (f32[512,128]{1,0:T(8,128)}, f32[512,128]{1,0:T(8,128)}) custom-call(s32[1]{0:T(128)} %bitcast.member_ref, s32[1]{0:T(128)} %bitcast.1.pair_ref, f32[520,128]{1,0:T(8,128)} %shard_map.96.refs_4_.refs_0_, f32[520,128]{1,0:T(8,128)} %copy-done.2, f32[512,128]{1,0:T(8,128)} %copy-done.5, f32[512,128]{1,0:T(8,128)} %copy-done.7, ...), custom_call_target="tpu_custom_call" | custom-call | flops 300000000 | bytes 750000 | tf_op jit(solution)/shard_map/pallas_call | solution.py:313
  62.3 3.2 %shard_map.108 = (f32[512,512]{1,0:T(8,128)}, f32[8,512]{1,0:T(8,128)}) custom-call(s32[1]{0:T(128)} %bitcast.member_ref, s32[1]{0:T(128)} %bitcast.1.pair_ref, f32[512,512]{1,0:T(8,128)} %shard_map.101.refs_5_.refs_0_, bf16[512,2048]{1,0:T(8,128)(2,1)} %refs_0_.23, bf16[512,2048]{1,0:T(8,128)(2,1)} %refs_1_.35, f32[1,2048]{1,0:T(1,128)} %bitcast.5, ...), custom_call_target="tpu_custom_call" | custom-call | flops 1400000000 | bytes 3500000 | tf_op jit(solution)/shard_map/pallas_call | solution.py:313
  66.3 3.2 %shard_map.109 = (f32[512,512]{1,0:T(8,128)}, f32[8,512]{1,0:T(8,128)}) custom-call(s32[1]{0:T(128)} %bitcast.member_ref, s32[1]{0:T(128)} %bitcast.1.pair_ref, f32[512,512]{1,0:T(8,128)} %shard_map.99.refs_5_.refs_0_, bf16[512,2048]{1,0:T(8,128)(2,1)} %refs_0_.23, bf16[512,2048]{1,0:T(8,128)(2,1)} %refs_1_.35, f32[1,2048]{1,0:T(1,128)} %bitcast.6, ...), custom_call_target="tpu_custom_call" | custom-call | flops 1400000000 | bytes 3500000 | tf_op jit(solution)/shard_map/pallas_call | solution.py:313
  70.2 3.2 %shard_map.110 = (f32[512,512]{1,0:T(8,128)}, f32[8,512]{1,0:T(8,128)}) custom-call(s32[1]{0:T(128)} %bitcast.member_ref, s32[1]{0:T(128)} %bitcast.1.pair_ref, f32[512,512]{1,0:T(8,128)} %shard_map.103.refs_3_.refs_0_, bf16[512,2048]{1,0:T(8,128)(2,1)} %refs_0_.23, bf16[512,2048]{1,0:T(8,128)(2,1)} %refs_1_.35, f32[1,2048]{1,0:T(1,128)} %bitcast.7, ...), custom_call_target="tpu_custom_call" | custom-call | flops 1400000000 | bytes 3500000 | tf_op jit(solution)/shard_map/pallas_call | solution.py:313
  75.1 2.3 %collective-permute-done.9.refs_7_ = f32[8,512]{1,0:T(8,128)S(1)} collective-permute-done((f32[8,512]{1,0:T(8,128)}, f32[8,512]{1,0:T(8,128)S(1)}, u32[]{:S(2)}, u32[]{:S(2)}) %collective-permute-start.9) | collective-permute-done | bytes 16416 | tf_op jit(solution)/shard_map/ppermute | solution.py:464
  78.9 3.2 %shard_map.111 = (bf16[512,2048]{1,0:T(8,128)(2,1)}, bf16[512,512]{1,0:T(8,128)(2,1)}, f32[520,128]{1,0:T(8,128)}) custom-call(s32[1]{0:T(128)} %bitcast.member_ref, s32[1]{0:T(128)} %bitcast.1.pair_ref, f32[512,512]{1,0:T(8,128)} %get-tuple-element.67.refs_0_, bf16[512,2048]{1,0:T(8,128)(2,1)} %refs_1_.35, f32[1,2048]{1,0:T(1,128)} %bitcast.8, ...), custom_call_target="tpu_custom_call" | custom-call | flops 2000000000 | bytes 5000000 | tf_op jit(solution)/shard_map/pallas_call | solution.py:313
  83.6 3.2 %shard_map.112 = (bf16[512,2048]{1,0:T(8,128)(2,1)}, bf16[512,512]{1,0:T(8,128)(2,1)}, f32[520,128]{1,0:T(8,128)}) custom-call(s32[1]{0:T(128)} %bitcast.member_ref, s32[1]{0:T(128)} %bitcast.1.pair_ref, f32[512,512]{1,0:T(8,128)} %get-tuple-element.66.refs_0_, bf16[512,2048]{1,0:T(8,128)(2,1)} %refs_1_.35, ...), custom_call_target="tpu_custom_call", output_to_operand_aliasing={{0}: (11, {})} | custom-call | flops 2000000000 | bytes 5000000 | tf_op jit(solution)/shard_map/pallas_call | solution.py:313
  87.4 3.2 %shard_map.113 = (bf16[512,2048]{1,0:T(8,128)(2,1)}, bf16[512,512]{1,0:T(8,128)(2,1)}, f32[520,128]{1,0:T(8,128)}) custom-call(s32[1]{0:T(128)} %bitcast.member_ref, s32[1]{0:T(128)} %bitcast.1.pair_ref, f32[512,512]{1,0:T(8,128)} %get-tuple-element.65.refs_0_, bf16[512,2048]{1,0:T(8,128)(2,1)} %refs_1_.35, ...), custom_call_target="tpu_custom_call", output_to_operand_aliasing={{0}: (11, {})} | custom-call | flops 2000000000 | bytes 5000000 | tf_op jit(solution)/shard_map/pallas_call | solution.py:313
  90.6 3.2 %shard_map.114 = (bf16[512,2048]{1,0:T(8,128)(2,1)}, bf16[512,512]{1,0:T(8,128)(2,1)}, f32[520,128]{1,0:T(8,128)}) custom-call(s32[1]{0:T(128)} %bitcast.member_ref, s32[1]{0:T(128)} %bitcast.1.pair_ref, f32[512,512]{1,0:T(8,128)} %get-tuple-element.61.refs_0_, bf16[512,2048]{1,0:T(8,128)(2,1)} %refs_1_.35, ...), custom_call_target="tpu_custom_call", output_to_operand_aliasing={{0}: (11, {})} | custom-call | flops 2000000000 | bytes 5000000 | tf_op jit(solution)/shard_map/pallas_call | solution.py:313
  97.0 5.6 %shard_map.116 = (bf16[512,2048]{1,0:T(8,128)(2,1)}, f32[512,512]{1,0:T(8,128)}, f32[512,512]{1,0:T(8,128)}) custom-call(s32[1]{0:T(128)} %bitcast.member_ref, s32[1]{0:T(128)} %bitcast.1.pair_ref, bf16[512,2048]{1,0:T(8,128)(2,1)} %refs_0_.23, bf16[512,2048]{1,0:T(8,128)(2,1)} %refs_2_.31, bf16[512,2048]{1,0:T(8,128)(2,1)} %refs_3_.15, ...), custom_call_target="tpu_custom_call" | custom-call | flops 4300000256 | bytes 10750000 | tf_op jit(solution)/shard_map/pallas_call | solution.py:313
  106.1 5.6 %shard_map.118 = (bf16[512,2048]{1,0:T(8,128)(2,1)}, f32[512,512]{1,0:T(8,128)}, f32[512,512]{1,0:T(8,128)}) custom-call(s32[1]{0:T(128)} %bitcast.member_ref, s32[1]{0:T(128)} %bitcast.1.pair_ref, bf16[512,2048]{1,0:T(8,128)(2,1)} %refs_0_.23, bf16[512,2048]{1,0:T(8,128)(2,1)} %refs_2_.31, ...), custom_call_target="tpu_custom_call", output_to_operand_aliasing={{0}: (8, {})} | custom-call | flops 4300000256 | bytes 10750000 | tf_op jit(solution)/shard_map/pallas_call | solution.py:313
  115.7 5.6 %shard_map.120 = (bf16[512,2048]{1,0:T(8,128)(2,1)}, f32[512,512]{1,0:T(8,128)}, f32[512,512]{1,0:T(8,128)}) custom-call(s32[1]{0:T(128)} %bitcast.member_ref, s32[1]{0:T(128)} %bitcast.1.pair_ref, bf16[512,2048]{1,0:T(8,128)(2,1)} %refs_0_.23, bf16[512,2048]{1,0:T(8,128)(2,1)} %refs_2_.31, ...), custom_call_target="tpu_custom_call", output_to_operand_aliasing={{0}: (8, {})} | custom-call | flops 4300000256 | bytes 10750000 | tf_op jit(solution)/shard_map/pallas_call | solution.py:313
  121.3 9.9 %collective-permute-done.15.refs_2_.refs_4_.refs_3_ = f32[512,128]{1,0:T(8,128)S(1)} collective-permute-done((f32[512,128]{1,0:T(8,128)}, f32[512,128]{1,0:T(8,128)S(1)}, u32[]{:S(2)}, u32[]{:S(2)}) %collective-permute-start.15) | collective-permute-done | bytes 262176 | tf_op jit(solution)/shard_map/ppermute | solution.py:390
  134.9 2.2 %shard_map.122 = (f32[512,128]{1,0:T(8,128)}, f32[512,128]{1,0:T(8,128)}) custom-call(s32[1]{0:T(128)} %bitcast.member_ref, s32[1]{0:T(128)} %bitcast.1.pair_ref, f32[520,128]{1,0:T(8,128)} %get-tuple-element.73.refs_10_.refs_0_.refs_2_, f32[520,128]{1,0:T(8,128)} %copy-done.1, f32[512,128]{1,0:T(8,128)} %copy-done.8, f32[512,128]{1,0:T(8,128)} %copy-done.4, ...), custom_call_target="tpu_custom_call" | custom-call | flops 300000000 | bytes 750000 | tf_op jit(solution)/shard_map/pallas_call | solution.py:313
  138.6 5.6 %shard_map.123 = (bf16[512,2048]{1,0:T(8,128)(2,1)}, f32[512,512]{1,0:T(8,128)}, f32[512,512]{1,0:T(8,128)}) custom-call(s32[1]{0:T(128)} %bitcast.member_ref, s32[1]{0:T(128)} %bitcast.1.pair_ref, bf16[512,2048]{1,0:T(8,128)(2,1)} %refs_0_.23, bf16[512,2048]{1,0:T(8,128)(2,1)} %refs_2_.31, ...), custom_call_target="tpu_custom_call", output_to_operand_aliasing={{0}: (8, {})} | custom-call | flops 4300000256 | bytes 10750000 | tf_op jit(solution)/shard_map/pallas_call | solution.py:313
  144.9 2.2 %shard_map.124 = (f32[512,128]{1,0:T(8,128)}, f32[512,128]{1,0:T(8,128)}) custom-call(s32[1]{0:T(128)} %bitcast.member_ref, s32[1]{0:T(128)} %bitcast.1.pair_ref, f32[520,128]{1,0:T(8,128)} %get-tuple-element.79.refs_3_.refs_0_, f32[520,128]{1,0:T(8,128)} %copy-done, f32[512,128]{1,0:T(8,128)} %copy-done.4, f32[512,128]{1,0:T(8,128)} %copy-done.6, ...), custom_call_target="tpu_custom_call" | custom-call | flops 300000000 | bytes 750000 | tf_op jit(solution)/shard_map/pallas_call | solution.py:313
  147.6 3.3 %shard_map.125 = (bf16[512,2048]{1,0:T(8,128)(2,1)}, bf16[512,2048]{1,0:T(8,128)(2,1)}) custom-call(s32[1]{0:T(128)} %bitcast.member_ref, s32[1]{0:T(128)} %bitcast.1.pair_ref, f32[512,512]{1,0:T(8,128)} %get-tuple-element.81.refs_5_.refs_0_, f32[512,512]{1,0:T(8,128)} %get-tuple-element.94.refs_1_, bf16[512,2048]{1,0:T(8,128)(2,1)} %refs_2_.31, ...), custom_call_target="tpu_custom_call" | custom-call | flops 2000000000 | bytes 5000000 | tf_op jit(solution)/shard_map/pallas_call | solution.py:313
  150.9 3.3 %shard_map.126 = (bf16[512,2048]{1,0:T(8,128)(2,1)}, bf16[512,2048]{1,0:T(8,128)(2,1)}) custom-call(s32[1]{0:T(128)} %bitcast.member_ref, s32[1]{0:T(128)} %bitcast.1.pair_ref, f32[512,512]{1,0:T(8,128)} %get-tuple-element.85.refs_3_.refs_0_, f32[512,512]{1,0:T(8,128)} %get-tuple-element.92.refs_1_, ...), custom_call_target="tpu_custom_call", output_to_operand_aliasing={{0}: (8, {}), {1}: (9, {})} | custom-call | flops 2000000000 | bytes 5000000 | tf_op jit(solution)/shard_map/pallas_call | solution.py:313
  155.0 3.3 %shard_map.127 = (bf16[512,2048]{1,0:T(8,128)(2,1)}, bf16[512,2048]{1,0:T(8,128)(2,1)}) custom-call(s32[1]{0:T(128)} %bitcast.member_ref, s32[1]{0:T(128)} %bitcast.1.pair_ref, f32[512,512]{1,0:T(8,128)} %get-tuple-element.83.refs_5_.refs_0_, f32[512,512]{1,0:T(8,128)} %get-tuple-element.91.refs_1_, ...), custom_call_target="tpu_custom_call", output_to_operand_aliasing={{0}: (8, {}), {1}: (9, {})} | custom-call | flops 2000000000 | bytes 5000000 | tf_op jit(solution)/shard_map/pallas_call | solution.py:313
  159.0 3.3 %shard_map.128 = (bf16[512,2048]{1,0:T(8,128)(2,1)}, bf16[512,2048]{1,0:T(8,128)(2,1)}) custom-call(s32[1]{0:T(128)} %bitcast.member_ref, s32[1]{0:T(128)} %bitcast.1.pair_ref, f32[512,512]{1,0:T(8,128)} %get-tuple-element.88.refs_5_.refs_0_, f32[512,512]{1,0:T(8,128)} %get-tuple-element.89.refs_1_, ...), custom_call_target="tpu_custom_call", output_to_operand_aliasing={{0}: (8, {}), {1}: (9, {})} | custom-call | flops 2000000000 | bytes 5000000 | tf_op jit(solution)/shard_map/pallas_call | solution.py:313
  (81 shorter events, 44.6 us)
Async XLA Ops:
  3.5 14.3 %collective-permute-start.1 = (f32[520,128]{1,0:T(8,128)}, f32[520,128]{1,0:T(8,128)S(1)}, u32[]{:S(2)}, u32[]{:S(2)}) collective-permute-start(f32[520,128]{1,0:T(8,128)} %get-tuple-element.55.refs_3_), channel_id=1, source_target_pairs={{0,4},{4,0},{8,12},{12,8},{16,20},{20,16},{24,28},{28,24},{1,5},{5... | collective-permute-start | bytes 798728 | tf_op jit(solution)/shard_map/ppermute | solution.py:369
  8.9 19.2 %collective-permute-start = (f32[520,128]{1,0:T(8,128)}, f32[520,128]{1,0:T(8,128)S(1)}, u32[]{:S(2)}, u32[]{:S(2)}) collective-permute-start(f32[520,128]{1,0:T(8,128)} %shard_map.94.refs_3_), channel_id=1, source_target_pairs={{0,4},{4,0},{8,12},{12,8},{16,20},{20,16},{24,28},{28,24},{1,5},{5... | collective-permute-start | bytes 798728 | tf_op jit(solution)/shard_map/ppermute | solution.py:369
  17.8 0.7 copy-start.3
  20.4 9.2 %collective-permute-start.2 = (f32[512,128]{1,0:T(8,128)}, f32[512,128]{1,0:T(8,128)S(1)}, u32[]{:S(2)}, u32[]{:S(2)}) collective-permute-start(f32[512,128]{1,0:T(8,128)} %shard_map.98.refs_4_), channel_id=1, source_target_pairs={{0,8},{4,12},{1,9},{5,13},{2,10},{6,14},{3,11},{7,15}} | collective-permute-start | bytes 786440 | tf_op jit(solution)/shard_map/ppermute | solution.py:390
  28.2 1.4 copy-start.2
  29.6 0.7 copy-start.9
  32.3 8.7 %collective-permute-start.3 = (f32[512,128]{1,0:T(8,128)}, f32[512,128]{1,0:T(8,128)S(1)}, u32[]{:S(2)}, u32[]{:S(2)}) collective-permute-start(f32[512,128]{1,0:T(8,128)} %shard_map.100.refs_4_), channel_id=1, source_target_pairs={{0,8},{4,12},{8,16},{12,20},{1,9},{5,13},{9,17},{13,21},{2,10},{6,... | collective-permute-start | bytes 786440 | tf_op jit(solution)/shard_map/ppermute | solution.py:390
  41.0 0.7 copy-start.5
  43.7 4.6 %collective-permute-start.4 = (f32[512,128]{1,0:T(8,128)}, f32[512,128]{1,0:T(8,128)S(1)}, u32[]{:S(2)}, u32[]{:S(2)}) collective-permute-start(f32[512,128]{1,0:T(8,128)} %shard_map.102.refs_4_), channel_id=1, source_target_pairs={{8,16},{12,20},{16,24},{20,28},{9,17},{13,21},{17,25},{21,29},{10,... | collective-permute-start | bytes 786440 | tf_op jit(solution)/shard_map/ppermute | solution.py:390
  48.3 0.7 copy-start.7
  50.8 8.1 %collective-permute-start.5 = (f32[512,128]{1,0:T(8,128)}, f32[512,128]{1,0:T(8,128)S(1)}, u32[]{:S(2)}, u32[]{:S(2)}) collective-permute-start(f32[512,128]{1,0:T(8,128)} %shard_map.104.refs_5_), channel_id=1, source_target_pairs={{16,24},{20,28},{17,25},{21,29},{18,26},{22,30},{19,27},{23,31}} | collective-permute-start | bytes 786440 | tf_op jit(solution)/shard_map/ppermute | solution.py:390
  53.6 12.0 %collective-permute-start.7 = (f32[512,128]{1,0:T(8,128)}, f32[512,128]{1,0:T(8,128)S(1)}, u32[]{:S(2)}, u32[]{:S(2)}) collective-permute-start(f32[512,128]{1,0:T(8,128)} %get-tuple-element.57.refs_7_), channel_id=1, source_target_pairs={{0,4},{4,0},{8,12},{12,8},{16,20},{20,16},{24,28},{28,24},{1,5},{5... | collective-permute-start | bytes 786440 | tf_op jit(solution)/shard_map/ppermute | solution.py:400
  61.8 7.7 %collective-permute-start.6 = (f32[512,128]{1,0:T(8,128)}, f32[512,128]{1,0:T(8,128)S(1)}, u32[]{:S(2)}, u32[]{:S(2)}) collective-permute-start(f32[512,128]{1,0:T(8,128)} %get-tuple-element.60.refs_7_), channel_id=1, source_target_pairs={{0,4},{4,0},{8,12},{12,8},{16,20},{20,16},{24,28},{28,24},{1,5},{5... | collective-permute-start | bytes 786440 | tf_op jit(solution)/shard_map/ppermute | solution.py:400
  65.5 0.7 copy-start.11
  69.5 0.7 copy-start.10
  73.4 1.7 %collective-permute-start.10 = (f32[8,512]{1,0:T(8,128)}, f32[8,512]{1,0:T(8,128)S(1)}, u32[]{:S(2)}, u32[]{:S(2)}) collective-permute-start(f32[8,512]{1,0:T(8,128)} %get-tuple-element.64.refs_5_), channel_id=1, source_target_pairs={{0,3},{1,0},{2,1},{3,2},{4,7},{5,4},{6,5},{7,6},{8,11},{9,8},{10,9... | collective-permute-start | bytes 49160 | tf_op jit(solution)/shard_map/ppermute | solution.py:464
  73.4 4.0 %collective-permute-start.9 = (f32[8,512]{1,0:T(8,128)}, f32[8,512]{1,0:T(8,128)S(1)}, u32[]{:S(2)}, u32[]{:S(2)}) collective-permute-start(f32[8,512]{1,0:T(8,128)} %get-tuple-element.64.refs_5_), channel_id=1, source_target_pairs={{0,2},{1,3},{2,0},{3,1},{4,6},{5,7},{6,4},{7,5},{8,10},{9,11},{10,... | collective-permute-start | bytes 49160 | tf_op jit(solution)/shard_map/ppermute | solution.py:464
  75.0 3.4 %collective-permute-start.8 = (f32[8,512]{1,0:T(8,128)}, f32[8,512]{1,0:T(8,128)S(1)}, u32[]{:S(2)}, u32[]{:S(2)}) collective-permute-start(f32[8,512]{1,0:T(8,128)} %get-tuple-element.64.refs_5_), channel_id=1, source_target_pairs={{0,1},{1,2},{2,3},{3,0},{4,5},{5,6},{6,7},{7,4},{8,9},{9,10},{10,1... | collective-permute-start | bytes 49160 | tf_op jit(solution)/shard_map/ppermute | solution.py:464
  75.1 3.2 %copy-start.16 = (f32[8,512]{1,0:T(8,128)}, f32[8,512]{1,0:T(8,128)S(1)}, u32[]{:S(2)}) copy-start(f32[8,512]{1,0:T(8,128)S(1)} %collective-permute-done.10.refs_8_) | copy-start | bytes 49156
  77.4 0.9 copy-start.17
  82.1 11.7 %collective-permute-start.11 = (f32[520,128]{1,0:T(8,128)}, f32[520,128]{1,0:T(8,128)S(1)}, u32[]{:S(2)}, u32[]{:S(2)}) collective-permute-start(f32[520,128]{1,0:T(8,128)} %get-tuple-element.69.refs_10_), channel_id=1, source_target_pairs={{0,4},{4,0},{8,12},{12,8},{16,20},{20,16},{24,28},{28,24},{1,5},{5... | collective-permute-start | bytes 798728 | tf_op jit(solution)/shard_map/ppermute | solution.py:369
  86.8 15.9 %collective-permute-start.12 = (f32[520,128]{1,0:T(8,128)}, f32[520,128]{1,0:T(8,128)S(1)}, u32[]{:S(2)}, u32[]{:S(2)}) collective-permute-start(f32[520,128]{1,0:T(8,128)} %get-tuple-element.71.refs_10_), channel_id=1, source_target_pairs={{0,4},{4,0},{8,12},{12,8},{16,20},{20,16},{24,28},{28,24},{1,5},{5... | collective-permute-start | bytes 798728 | tf_op jit(solution)/shard_map/ppermute | solution.py:369
  96.3 6.3 %collective-permute-start.13 = (f32[512,128]{1,0:T(8,128)}, f32[512,128]{1,0:T(8,128)S(1)}, u32[]{:S(2)}, u32[]{:S(2)}) collective-permute-start(f32[512,128]{1,0:T(8,128)} %shard_map.115.refs_6_), channel_id=1, source_target_pairs={{24,16},{28,20},{25,17},{29,21},{26,18},{30,22},{27,19},{31,23}} | collective-permute-start | bytes 786440 | tf_op jit(solution)/shard_map/ppermute | solution.py:390
  102.6 0.8 copy-start.8
  105.4 6.3 %collective-permute-start.14 = (f32[512,128]{1,0:T(8,128)}, f32[512,128]{1,0:T(8,128)S(1)}, u32[]{:S(2)}, u32[]{:S(2)}) collective-permute-start(f32[512,128]{1,0:T(8,128)} %shard_map.117.refs_7_), channel_id=1, source_target_pairs={{24,16},{28,20},{16,8},{20,12},{25,17},{29,21},{17,9},{21,13},{26,... | collective-permute-start | bytes 786440 | tf_op jit(solution)/shard_map/ppermute | solution.py:390
  111.7 0.7 copy-start.4
  114.4 16.8 %collective-permute-start.15 = (f32[512,128]{1,0:T(8,128)}, f32[512,128]{1,0:T(8,128)S(1)}, u32[]{:S(2)}, u32[]{:S(2)}) collective-permute-start(f32[512,128]{1,0:T(8,128)} %shard_map.119.refs_7_), channel_id=1, source_target_pairs={{16,8},{20,12},{8,0},{12,4},{17,9},{21,13},{9,1},{13,5},{18,10},{2... | collective-permute-start | bytes 786440 | tf_op jit(solution)/shard_map/ppermute | solution.py:390
  133.7 10.6 %collective-permute-start.16 = (f32[512,128]{1,0:T(8,128)}, f32[512,128]{1,0:T(8,128)S(1)}, u32[]{:S(2)}, u32[]{:S(2)}) collective-permute-start(f32[512,128]{1,0:T(8,128)} %shard_map.121.refs_5_), channel_id=1, source_target_pairs={{8,0},{12,4},{9,1},{13,5},{10,2},{14,6},{11,3},{15,7}} | collective-permute-start | bytes 786440 | tf_op jit(solution)/shard_map/ppermute | solution.py:390
  137.1 17.1 %collective-permute-start.18 = (f32[512,128]{1,0:T(8,128)}, f32[512,128]{1,0:T(8,128)S(1)}, u32[]{:S(2)}, u32[]{:S(2)}) collective-permute-start(f32[512,128]{1,0:T(8,128)} %get-tuple-element.86.refs_7_), channel_id=1, source_target_pairs={{0,4},{4,0},{8,12},{12,8},{16,20},{20,16},{24,28},{28,24},{1,5},{5... | collective-permute-start | bytes 786440 | tf_op jit(solution)/shard_map/ppermute | solution.py:400
  147.1 11.2 %collective-permute-start.17 = (f32[512,128]{1,0:T(8,128)}, f32[512,128]{1,0:T(8,128)S(1)}, u32[]{:S(2)}, u32[]{:S(2)}) collective-permute-start(f32[512,128]{1,0:T(8,128)} %get-tuple-element.90.refs_6_), channel_id=1, source_target_pairs={{0,4},{4,0},{8,12},{12,8},{16,20},{20,16},{24,28},{28,24},{1,5},{5... | collective-permute-start | bytes 786440 | tf_op jit(solution)/shard_map/ppermute | solution.py:400
  154.2 0.7 copy-start.12
  158.3 0.7 copy-start.13
  (6 other events, 4.1 us)

commit v3 on v2

--- a/solution.py
+++ b/solution.py
@@ -321,7 +321,7 @@
                 scratch_shapes=list(scratch),
             ),
             input_output_aliases=aliases or {},
-            compiler_params=pltpu.CompilerParams(vmem_limit_bytes=60 * 1024 * 1024),
+            compiler_params=pltpu.CompilerParams(vmem_limit_bytes=16 * 1024 * 1024),
             cost_estimate=pl.CostEstimate(
                 flops=int(cost * 1e9), bytes_accessed=int(cost * 2.5e6), transcendentals=0
             ),

time: 163 us -> 116 us (0.71)
  Pallas kernels: 111 us -> 51.9 us
  waiting for transfers between devices: 15.1 us -> 32.1 us
  local copies, waits for them, and re-layouts: 11.2 us -> 4.6 us
  starting transfers between devices: 24.3 us -> 26 us
    pallas_call x36, Pallas kernels: 111 us -> 51.9 us  [run(): pl.pallas_call(body, out_shape=[shape for shape, _ in outs], grid_spec=pl...]
    ppermute x8, waiting for transfers between devices: 11.9 us -> 22.6 us  [chain(): arrived[r] = lax.ppermute(value, 'seq', pairs)]
    unnamed x38 -> x16, local copies, waits for them, and re-layouts: 10.6 us -> 4.6 us
    ppermute x4, waiting for transfers between devices: 0.01 us -> 3.37 us  [chain(): theirs.append(lax.ppermute(send, 'seq', swap))]
    ppermute x4, waiting for transfers between devices: 0.01 us -> 3.05 us  [chain(): received.append(lax.ppermute(sent, 'seq', swap))]
  transfers between devices with their start and end apart: 19 -> 19, of which waited for: 5 -> 10; matrix products, arithmetic and copies ran while one was open for 0% -> 0% of each run, Pallas kernels for 53% -> 39%
where the time goes in v3:
time: 116 us; the launch traced here: 115 us
  Pallas kernels  51.9 us (45%)
  waiting for transfers between devices  32.1 us (28%)
  starting transfers between devices  26 us (22%)
  local copies, waits for them, and re-layouts  4.6 us (4%)
    pallas_call x36, Pallas kernels, run(): pl.pallas_call(body, out_shape=[shape for shape, _ in outs], grid_spec=pl...  51.9 us
    ppermute x8, waiting for transfers between devices, chain(): arrived[r] = lax.ppermute(value, 'seq', pairs)  22.6 us
    ppermute x8, starting transfers between devices, chain(): arrived[r] = lax.ppermute(value, 'seq', pairs)  13.8 us
    ppermute x4, starting transfers between devices, chain(): theirs.append(lax.ppermute(send, 'seq', swap))  5.32 us
    ppermute x4, starting transfers between devices, chain(): received.append(lax.ppermute(sent, 'seq', swap))  5.16 us
    unnamed x16, local copies, waits for them, and re-layouts  4.6 us
    ppermute x4, waiting for transfers between devices, chain(): theirs.append(lax.ppermute(send, 'seq', swap))  3.37 us
    ppermute x4, waiting for transfers between devices, chain(): received.append(lax.ppermute(sent, 'seq', swap))  3.05 us
  transfers between devices with their start and end apart: 19, of which 10 were waited for; matrix products, arithmetic and copies ran while one was open for 0% of the time, Pallas kernels for 39%

profile of v3, /device:TPU:0, one launch (start us, length us, event | category | flops | bytes accessed | tf_op | source)
XLA Modules:
  0.0 115.5 jit_solution(10102972564914106309)
XLA Ops:
  0.7 1.6 %copy-done.2 = bf16[512,2048]{1,0:T(8,128)(2,1)S(1)} copy-done((bf16[512,2048]{1,0:T(8,128)(2,1)S(1)}, bf16[512,2048]{1,0:T(8,128)(2,1)}, u32[]{:S(2)}) %copy-start.2) | copy-done | bytes 2097176
  2.2 1.6 %copy-done.4 = bf16[512,2048]{1,0:T(8,128)(2,1)S(1)} copy-done((bf16[512,2048]{1,0:T(8,128)(2,1)S(1)}, bf16[512,2048]{1,0:T(8,128)(2,1)}, u32[]{:S(2)}) %copy-start.4) | copy-done | bytes 2097176
  5.8 3.0 %collective-permute-start.1 = (f32[520,128]{1,0:T(8,128)S(1)}, f32[520,128]{1,0:T(8,128)S(1)}, u32[]{:S(2)}, u32[]{:S(2)}) collective-permute-start(f32[520,128]{1,0:T(8,128)S(1)} %get-tuple-element.55.refs_3_), channel_id=1, source_target_pairs={{0,4},{4,0},{8,12},{12,8},{16,20},{20,16},{24,28},{28,24},{1,5},{5... | collective-permute-start | bytes 798728 | tf_op jit(solution)/shard_map/ppermute | solution.py:369
  12.4 2.2 %shard_map.97.refs_3_.refs_0_ = f32[512,512]{1,0:T(8,128)S(1)} custom-call(s32[1]{0:T(128)} %bitcast.member_ref, s32[1]{0:T(128)} %bitcast.1.pair_ref, bf16[512,2048]{1,0:T(8,128)(2,1)S(1)} %copy-done.1, bf16[512,2048]{1,0:T(8,128)(2,1)S(1)} %copy-done.2, bf16[512,2048]{1,0:T(8,128)(2,1)S(1)} %copy-done.4, ...), custom_call_target="tpu_custom_call" | custom-call | flops 2200000000 | bytes 5500000 | tf_op jit(solution)/shard_map/pallas_call | solution.py:313
  16.1 4.0 %collective-permute-start.2 = (f32[512,128]{1,0:T(8,128)S(1)}, f32[512,128]{1,0:T(8,128)S(1)}, u32[]{:S(2)}, u32[]{:S(2)}) collective-permute-start(f32[512,128]{1,0:T(8,128)S(1)} %shard_map.98.refs_4_), channel_id=1, source_target_pairs={{0,8},{4,12},{1,9},{5,13},{2,10},{6,14},{3,11},{7,15}} | collective-permute-start | bytes 786440 | tf_op jit(solution)/shard_map/ppermute | solution.py:390
  20.1 2.2 %shard_map.99.refs_5_.refs_0_ = f32[512,512]{1,0:T(8,128)S(1)} custom-call(s32[1]{0:T(128)} %bitcast.member_ref, s32[1]{0:T(128)} %bitcast.1.pair_ref, bf16[512,2048]{1,0:T(8,128)(2,1)S(1)} %copy-done.1, bf16[512,2048]{1,0:T(8,128)(2,1)S(1)} %copy-done.3, bf16[512,2048]{1,0:T(8,128)(2,1)S(1)} %copy-done.4, ...), custom_call_target="tpu_custom_call" | custom-call | flops 2200000000 | bytes 5500000 | tf_op jit(solution)/shard_map/pallas_call | solution.py:313
  22.4 1.6 %collective-permute-done.2.refs_4_.refs_2_ = f32[512,128]{1,0:T(8,128)S(1)} collective-permute-done((f32[512,128]{1,0:T(8,128)S(1)}, f32[512,128]{1,0:T(8,128)S(1)}, u32[]{:S(2)}, u32[]{:S(2)}) %collective-permute-start.2) | collective-permute-done | bytes 262176 | tf_op jit(solution)/shard_map/ppermute | solution.py:390
  24.0 4.4 %collective-permute-start.3 = (f32[512,128]{1,0:T(8,128)S(1)}, f32[512,128]{1,0:T(8,128)S(1)}, u32[]{:S(2)}, u32[]{:S(2)}) collective-permute-start(f32[512,128]{1,0:T(8,128)S(1)} %shard_map.100.refs_4_), channel_id=1, source_target_pairs={{0,8},{4,12},{8,16},{12,20},{1,9},{5,13},{9,17},{13,21},{2,10},{6,... | collective-permute-start | bytes 786440 | tf_op jit(solution)/shard_map/ppermute | solution.py:390
  28.5 2.2 %shard_map.101.refs_5_.refs_0_ = f32[512,512]{1,0:T(8,128)S(1)} custom-call(s32[1]{0:T(128)} %bitcast.member_ref, s32[1]{0:T(128)} %bitcast.1.pair_ref, bf16[512,2048]{1,0:T(8,128)(2,1)S(1)} %copy-done.1, bf16[512,2048]{1,0:T(8,128)(2,1)S(1)} %copy-done.3, bf16[512,2048]{1,0:T(8,128)(2,1)S(1)} %copy-done.5, ...), custom_call_target="tpu_custom_call" | custom-call | flops 2200000000 | bytes 5500000 | tf_op jit(solution)/shard_map/pallas_call | solution.py:313
  30.7 1.6 %collective-permute-done.3.refs_4_.refs_3_.refs_2_ = f32[512,128]{1,0:T(8,128)S(1)} collective-permute-done((f32[512,128]{1,0:T(8,128)S(1)}, f32[512,128]{1,0:T(8,128)S(1)}, u32[]{:S(2)}, u32[]{:S(2)}) %collective-permute-start.3) | collective-permute-done | bytes 262176 | tf_op jit(solution)/shard_map/ppermute | solution.py:390
  33.0 2.2 %shard_map.103.refs_3_.refs_0_ = f32[512,512]{1,0:T(8,128)S(1)} custom-call(s32[1]{0:T(128)} %bitcast.member_ref, s32[1]{0:T(128)} %bitcast.1.pair_ref, bf16[512,2048]{1,0:T(8,128)(2,1)S(1)} %copy-done.1, bf16[512,2048]{1,0:T(8,128)(2,1)S(1)} %copy-done.3, bf16[512,2048]{1,0:T(8,128)(2,1)S(1)} %copy-done.5, ...), custom_call_target="tpu_custom_call" | custom-call | flops 2200000000 | bytes 5500000 | tf_op jit(solution)/shard_map/pallas_call | solution.py:313
  36.2 1.6 %collective-permute-start.7 = (f32[512,128]{1,0:T(8,128)S(1)}, f32[512,128]{1,0:T(8,128)S(1)}, u32[]{:S(2)}, u32[]{:S(2)}) collective-permute-start(f32[512,128]{1,0:T(8,128)S(1)} %get-tuple-element.57.refs_7_), channel_id=1, source_target_pairs={{0,4},{4,0},{8,12},{12,8},{16,20},{20,16},{24,28},{28,24},{1,5},{5... | collective-permute-start | bytes 786440 | tf_op jit(solution)/shard_map/ppermute | solution.py:400
  41.3 1.9 %collective-permute-done.7.refs_5_ = f32[512,128]{1,0:T(8,128)S(1)} collective-permute-done((f32[512,128]{1,0:T(8,128)S(1)}, f32[512,128]{1,0:T(8,128)S(1)}, u32[]{:S(2)}, u32[]{:S(2)}) %collective-permute-start.7) | collective-permute-done | bytes 262176 | tf_op jit(solution)/shard_map/ppermute | solution.py:400
  47.5 1.5 %collective-permute-start.9 = (f32[8,512]{1,0:T(8,128)S(1)}, f32[8,512]{1,0:T(8,128)S(1)}, u32[]{:S(2)}, u32[]{:S(2)}) collective-permute-start(f32[8,512]{1,0:T(8,128)S(1)} %get-tuple-element.64.refs_5_), channel_id=1, source_target_pairs={{0,2},{1,3},{2,0},{3,1},{4,6},{5,7},{6,4},{7,5},{8,10},{9,11},{10,... | collective-permute-start | bytes 49160 | tf_op jit(solution)/shard_map/ppermute | solution.py:464
  49.2 2.1 %collective-permute-done.9.refs_7_ = f32[8,512]{1,0:T(8,128)S(1)} collective-permute-done((f32[8,512]{1,0:T(8,128)S(1)}, f32[8,512]{1,0:T(8,128)S(1)}, u32[]{:S(2)}, u32[]{:S(2)}) %collective-permute-start.9) | collective-permute-done | bytes 16416 | tf_op jit(solution)/shard_map/ppermute | solution.py:464
  52.2 1.9 %shard_map.111 = (bf16[512,2048]{1,0:T(8,128)(2,1)}, bf16[512,512]{1,0:T(8,128)(2,1)S(1)}, f32[520,128]{1,0:T(8,128)S(1)}) custom-call(s32[1]{0:T(128)} %bitcast.member_ref, s32[1]{0:T(128)} %bitcast.1.pair_ref, f32[512,512]{1,0:T(8,128)S(1)} %get-tuple-element.67.refs_0_, bf16[512,2048]{1,0:T(8,128)(2,1)S(1)} %copy-done, f32[1,2048]{1,0:T(1,128)S(1)} %bitcast.8, ...), custom_call_target="tpu_custom_call" | custom-call | flops 2000000000 | bytes 5000000 | tf_op jit(solution)/shard_map/pallas_call | solution.py:313
  54.1 1.5 %collective-permute-start.11 = (f32[520,128]{1,0:T(8,128)S(1)}, f32[520,128]{1,0:T(8,128)S(1)}, u32[]{:S(2)}, u32[]{:S(2)}) collective-permute-start(f32[520,128]{1,0:T(8,128)S(1)} %get-tuple-element.69.refs_10_), channel_id=1, source_target_pairs={{0,4},{4,0},{8,12},{12,8},{16,20},{20,16},{24,28},{28,24},{1,5},{5... | collective-permute-start | bytes 798728 | tf_op jit(solution)/shard_map/ppermute | solution.py:369
  55.6 1.9 %shard_map.112 = (bf16[512,2048]{1,0:T(8,128)(2,1)}, bf16[512,512]{1,0:T(8,128)(2,1)S(1)}, f32[520,128]{1,0:T(8,128)S(1)}) custom-call(s32[1]{0:T(128)} %bitcast.member_ref, s32[1]{0:T(128)} %bitcast.1.pair_ref, f32[512,512]{1,0:T(8,128)S(1)} %get-tuple-element.66.refs_0_, bf16[512,2048]{1,0:T(8,128)(2,1)S(1)} %copy-done, ...), custom_call_target="tpu_custom_call", output_to_operand_aliasing={{0}: (11, {})} | custom-call | flops 2000000000 | bytes 5000000 | tf_op jit(solution)/shard_map/pallas_call | solution.py:313
  58.1 1.9 %shard_map.113 = (bf16[512,2048]{1,0:T(8,128)(2,1)}, bf16[512,512]{1,0:T(8,128)(2,1)S(1)}, f32[520,128]{1,0:T(8,128)S(1)}) custom-call(s32[1]{0:T(128)} %bitcast.member_ref, s32[1]{0:T(128)} %bitcast.1.pair_ref, f32[512,512]{1,0:T(8,128)S(1)} %get-tuple-element.65.refs_0_, bf16[512,2048]{1,0:T(8,128)(2,1)S(1)} %copy-done, ...), custom_call_target="tpu_custom_call", output_to_operand_aliasing={{0}: (11, {})} | custom-call | flops 2000000000 | bytes 5000000 | tf_op jit(solution)/shard_map/pallas_call | solution.py:313
  60.0 1.9 %shard_map.114 = (bf16[512,2048]{1,0:T(8,128)(2,1)}, bf16[512,512]{1,0:T(8,128)(2,1)S(1)}, f32[520,128]{1,0:T(8,128)S(1)}) custom-call(s32[1]{0:T(128)} %bitcast.member_ref, s32[1]{0:T(128)} %bitcast.1.pair_ref, f32[512,512]{1,0:T(8,128)S(1)} %get-tuple-element.61.refs_0_, bf16[512,2048]{1,0:T(8,128)(2,1)S(1)} %copy-done, ...), custom_call_target="tpu_custom_call", output_to_operand_aliasing={{0}: (11, {})} | custom-call | flops 2000000000 | bytes 5000000 | tf_op jit(solution)/shard_map/pallas_call | solution.py:313
  61.9 1.6 %collective-permute-done.11.refs_1_.refs_3_ = f32[520,128]{1,0:T(8,128)S(1)} collective-permute-done((f32[520,128]{1,0:T(8,128)S(1)}, f32[520,128]{1,0:T(8,128)S(1)}, u32[]{:S(2)}, u32[]{:S(2)}) %collective-permute-start.11) | collective-permute-done | bytes 266272 | tf_op jit(solution)/shard_map/ppermute | solution.py:369
  64.1 4.3 %shard_map.116 = (bf16[512,2048]{1,0:T(8,128)(2,1)}, f32[512,512]{1,0:T(8,128)S(1)}, f32[512,512]{1,0:T(8,128)S(1)}) custom-call(s32[1]{0:T(128)} %bitcast.member_ref, s32[1]{0:T(128)} %bitcast.1.pair_ref, bf16[512,2048]{1,0:T(8,128)(2,1)S(1)} %copy-done.1, bf16[512,2048]{1,0:T(8,128)(2,1)S(1)} %copy-done.3, bf16[512,2048]{1,0:T(8,128)(2,1)S(1)} %copy-done.5, ...), custom_call_target="tpu_custom_call" | custom-call | flops 4300000256 | bytes 10750000 | tf_op jit(solution)/shard_map/pallas_call | solution.py:313
  69.2 4.3 %shard_map.118 = (bf16[512,2048]{1,0:T(8,128)(2,1)}, f32[512,512]{1,0:T(8,128)S(1)}, f32[512,512]{1,0:T(8,128)S(1)}) custom-call(s32[1]{0:T(128)} %bitcast.member_ref, s32[1]{0:T(128)} %bitcast.1.pair_ref, bf16[512,2048]{1,0:T(8,128)(2,1)S(1)} %copy-done.1, bf16[512,2048]{1,0:T(8,128)(2,1)S(1)} %copy-done.3, ...), custom_call_target="tpu_custom_call", output_to_operand_aliasing={{0}: (8, {})} | custom-call | flops 4300000256 | bytes 10750000 | tf_op jit(solution)/shard_map/pallas_call | solution.py:313
  74.8 4.3 %shard_map.120 = (bf16[512,2048]{1,0:T(8,128)(2,1)}, f32[512,512]{1,0:T(8,128)S(1)}, f32[512,512]{1,0:T(8,128)S(1)}) custom-call(s32[1]{0:T(128)} %bitcast.member_ref, s32[1]{0:T(128)} %bitcast.1.pair_ref, bf16[512,2048]{1,0:T(8,128)(2,1)S(1)} %copy-done.1, bf16[512,2048]{1,0:T(8,128)(2,1)S(1)} %copy-done.3, ...), custom_call_target="tpu_custom_call", output_to_operand_aliasing={{0}: (8, {})} | custom-call | flops 4300000256 | bytes 10750000 | tf_op jit(solution)/shard_map/pallas_call | solution.py:313
  79.1 18.4 %collective-permute-done.15.refs_2_.refs_4_.refs_3_ = f32[512,128]{1,0:T(8,128)S(1)} collective-permute-done((f32[512,128]{1,0:T(8,128)S(1)}, f32[512,128]{1,0:T(8,128)S(1)}, u32[]{:S(2)}, u32[]{:S(2)}) %collective-permute-start.15) | collective-permute-done | bytes 262176 | tf_op jit(solution)/shard_map/ppermute | solution.py:390
  98.9 1.6 %collective-permute-start.18 = (f32[512,128]{1,0:T(8,128)S(1)}, f32[512,128]{1,0:T(8,128)S(1)}, u32[]{:S(2)}, u32[]{:S(2)}) collective-permute-start(f32[512,128]{1,0:T(8,128)S(1)} %get-tuple-element.86.refs_7_), channel_id=1, source_target_pairs={{0,4},{4,0},{8,12},{12,8},{16,20},{20,16},{24,28},{28,24},{1,5},{5... | collective-permute-start | bytes 786440 | tf_op jit(solution)/shard_map/ppermute | solution.py:400
  100.4 4.3 %shard_map.123 = (bf16[512,2048]{1,0:T(8,128)(2,1)}, f32[512,512]{1,0:T(8,128)S(1)}, f32[512,512]{1,0:T(8,128)S(1)}) custom-call(s32[1]{0:T(128)} %bitcast.member_ref, s32[1]{0:T(128)} %bitcast.1.pair_ref, bf16[512,2048]{1,0:T(8,128)(2,1)S(1)} %copy-done.1, bf16[512,2048]{1,0:T(8,128)(2,1)S(1)} %copy-done.3, ...), custom_call_target="tpu_custom_call", output_to_operand_aliasing={{0}: (8, {})} | custom-call | flops 4300000256 | bytes 10750000 | tf_op jit(solution)/shard_map/pallas_call | solution.py:313
  105.8 1.6 %collective-permute-start.17 = (f32[512,128]{1,0:T(8,128)S(1)}, f32[512,128]{1,0:T(8,128)S(1)}, u32[]{:S(2)}, u32[]{:S(2)}) collective-permute-start(f32[512,128]{1,0:T(8,128)S(1)} %get-tuple-element.90.refs_6_), channel_id=1, source_target_pairs={{0,4},{4,0},{8,12},{12,8},{16,20},{20,16},{24,28},{28,24},{1,5},{5... | collective-permute-start | bytes 786440 | tf_op jit(solution)/shard_map/ppermute | solution.py:400
  107.4 2.0 %shard_map.125 = (bf16[512,2048]{1,0:T(8,128)(2,1)}, bf16[512,2048]{1,0:T(8,128)(2,1)}) custom-call(s32[1]{0:T(128)} %bitcast.member_ref, s32[1]{0:T(128)} %bitcast.1.pair_ref, f32[512,512]{1,0:T(8,128)S(1)} %get-tuple-element.81.refs_5_.refs_0_, f32[512,512]{1,0:T(8,128)S(1)} %get-tuple-element.94.refs_1_, bf16[512,2048]{1,0:T(8,128)(2,1)S(1)} %copy-done.3, ...), custom_call_target="tpu_custom_call" | custom-call | flops 2000000000 | bytes 5000000 | tf_op jit(solution)/shard_map/pallas_call | solution.py:313
  109.4 2.0 %shard_map.126 = (bf16[512,2048]{1,0:T(8,128)(2,1)}, bf16[512,2048]{1,0:T(8,128)(2,1)}) custom-call(s32[1]{0:T(128)} %bitcast.member_ref, s32[1]{0:T(128)} %bitcast.1.pair_ref, f32[512,512]{1,0:T(8,128)S(1)} %get-tuple-element.85.refs_3_.refs_0_, f32[512,512]{1,0:T(8,128)S(1)} %get-tuple-element.92.refs_1_, ...), custom_call_target="tpu_custom_call", output_to_operand_aliasing={{0}: (8, {}), {1}: (9, {})} | custom-call | flops 2000000000 | bytes 5000000 | tf_op jit(solution)/shard_map/pallas_call | solution.py:313
  111.5 2.0 %shard_map.127 = (bf16[512,2048]{1,0:T(8,128)(2,1)}, bf16[512,2048]{1,0:T(8,128)(2,1)}) custom-call(s32[1]{0:T(128)} %bitcast.member_ref, s32[1]{0:T(128)} %bitcast.1.pair_ref, f32[512,512]{1,0:T(8,128)S(1)} %get-tuple-element.83.refs_5_.refs_0_, f32[512,512]{1,0:T(8,128)S(1)} %get-tuple-element.91.refs_1_, ...), custom_call_target="tpu_custom_call", output_to_operand_aliasing={{0}: (8, {}), {1}: (9, {})} | custom-call | flops 2000000000 | bytes 5000000 | tf_op jit(solution)/shard_map/pallas_call | solution.py:313
  113.5 2.0 %shard_map.128 = (bf16[512,2048]{1,0:T(8,128)(2,1)}, bf16[512,2048]{1,0:T(8,128)(2,1)}) custom-call(s32[1]{0:T(128)} %bitcast.member_ref, s32[1]{0:T(128)} %bitcast.1.pair_ref, f32[512,512]{1,0:T(8,128)S(1)} %get-tuple-element.88.refs_5_.refs_0_, f32[512,512]{1,0:T(8,128)S(1)} %get-tuple-element.89.refs_1_, ...), custom_call_target="tpu_custom_call", output_to_operand_aliasing={{0}: (8, {}), {1}: (9, {})} | custom-call | flops 2000000000 | bytes 5000000 | tf_op jit(solution)/shard_map/pallas_call | solution.py:313
  (59 shorter events, 23.1 us)
Async XLA Ops:
  0.6 1.6 %copy-start.2 = (bf16[512,2048]{1,0:T(8,128)(2,1)S(1)}, bf16[512,2048]{1,0:T(8,128)(2,1)}, u32[]{:S(2)}) copy-start(bf16[512,2048]{1,0:T(8,128)(2,1)} %refs_2_.31) | copy-start | bytes 6291460
  2.2 1.6 %copy-start.4 = (bf16[512,2048]{1,0:T(8,128)(2,1)S(1)}, bf16[512,2048]{1,0:T(8,128)(2,1)}, u32[]{:S(2)}) copy-start(bf16[512,2048]{1,0:T(8,128)(2,1)} %refs_3_.15) | copy-start | bytes 6291460
  3.8 0.8 copy-start.7
  5.8 10.3 %collective-permute-start.1 = (f32[520,128]{1,0:T(8,128)S(1)}, f32[520,128]{1,0:T(8,128)S(1)}, u32[]{:S(2)}, u32[]{:S(2)}) collective-permute-start(f32[520,128]{1,0:T(8,128)S(1)} %get-tuple-element.55.refs_3_), channel_id=1, source_target_pairs={{0,4},{4,0},{8,12},{12,8},{16,20},{20,16},{24,28},{28,24},{1,5},{5... | collective-permute-start | bytes 798728 | tf_op jit(solution)/shard_map/ppermute | solution.py:369
  9.8 12.6 %collective-permute-start = (f32[520,128]{1,0:T(8,128)S(1)}, f32[520,128]{1,0:T(8,128)S(1)}, u32[]{:S(2)}, u32[]{:S(2)}) collective-permute-start(f32[520,128]{1,0:T(8,128)S(1)} %shard_map.94.refs_3_), channel_id=1, source_target_pairs={{0,4},{4,0},{8,12},{12,8},{16,20},{20,16},{24,28},{28,24},{1,5},{5... | collective-permute-start | bytes 798728 | tf_op jit(solution)/shard_map/ppermute | solution.py:369
  10.8 1.6 %copy-start.1 = (bf16[512,2048]{1,0:T(8,128)(2,1)S(1)}, bf16[512,2048]{1,0:T(8,128)(2,1)}, u32[]{:S(2)}) copy-start(bf16[512,2048]{1,0:T(8,128)(2,1)} %refs_0_.23) | copy-start | bytes 6291460
  14.6 5.5 %copy-start.3 = (bf16[512,2048]{1,0:T(8,128)(2,1)S(1)}, bf16[512,2048]{1,0:T(8,128)(2,1)}, u32[]{:S(2)}) copy-start(bf16[512,2048]{1,0:T(8,128)(2,1)} %refs_2_.31) | copy-start | bytes 6291460
  16.1 7.8 %collective-permute-start.2 = (f32[512,128]{1,0:T(8,128)S(1)}, f32[512,128]{1,0:T(8,128)S(1)}, u32[]{:S(2)}, u32[]{:S(2)}) collective-permute-start(f32[512,128]{1,0:T(8,128)S(1)} %shard_map.98.refs_4_), channel_id=1, source_target_pairs={{0,8},{4,12},{1,9},{5,13},{2,10},{6,14},{3,11},{7,15}} | collective-permute-start | bytes 786440 | tf_op jit(solution)/shard_map/ppermute | solution.py:390
  22.3 6.1 %copy-start.5 = (bf16[512,2048]{1,0:T(8,128)(2,1)S(1)}, bf16[512,2048]{1,0:T(8,128)(2,1)}, u32[]{:S(2)}) copy-start(bf16[512,2048]{1,0:T(8,128)(2,1)} %refs_3_.15) | copy-start | bytes 6291460
  24.0 8.3 %collective-permute-start.3 = (f32[512,128]{1,0:T(8,128)S(1)}, f32[512,128]{1,0:T(8,128)S(1)}, u32[]{:S(2)}, u32[]{:S(2)}) collective-permute-start(f32[512,128]{1,0:T(8,128)S(1)} %shard_map.100.refs_4_), channel_id=1, source_target_pairs={{0,8},{4,12},{8,16},{12,20},{1,9},{5,13},{9,17},{13,21},{2,10},{6,... | collective-permute-start | bytes 786440 | tf_op jit(solution)/shard_map/ppermute | solution.py:390
  32.3 2.9 %collective-permute-start.4 = (f32[512,128]{1,0:T(8,128)S(1)}, f32[512,128]{1,0:T(8,128)S(1)}, u32[]{:S(2)}, u32[]{:S(2)}) collective-permute-start(f32[512,128]{1,0:T(8,128)S(1)} %shard_map.102.refs_4_), channel_id=1, source_target_pairs={{8,16},{12,20},{16,24},{20,28},{9,17},{13,21},{17,25},{21,29},{10,... | collective-permute-start | bytes 786440 | tf_op jit(solution)/shard_map/ppermute | solution.py:390
  35.2 2.6 %copy-start = (bf16[512,2048]{1,0:T(8,128)(2,1)S(1)}, bf16[512,2048]{1,0:T(8,128)(2,1)}, u32[]{:S(2)}) copy-start(bf16[512,2048]{1,0:T(8,128)(2,1)} %refs_1_.35) | copy-start | bytes 6291460
  35.2 2.5 %copy-start.6 = (f32[2048]{0:T(1024)S(1)}, f32[2048]{0:T(1024)}, u32[]{:S(2)}) copy-start(f32[2048]{0:T(1024)} %param.10) | copy-start | bytes 24580
  35.3 3.9 %collective-permute-start.5 = (f32[512,128]{1,0:T(8,128)S(1)}, f32[512,128]{1,0:T(8,128)S(1)}, u32[]{:S(2)}, u32[]{:S(2)}) collective-permute-start(f32[512,128]{1,0:T(8,128)S(1)} %shard_map.104.refs_5_), channel_id=1, source_target_pairs={{16,24},{20,28},{17,25},{21,29},{18,26},{22,30},{19,27},{23,31}} | collective-permute-start | bytes 786440 | tf_op jit(solution)/shard_map/ppermute | solution.py:390
  36.2 7.1 %collective-permute-start.7 = (f32[512,128]{1,0:T(8,128)S(1)}, f32[512,128]{1,0:T(8,128)S(1)}, u32[]{:S(2)}, u32[]{:S(2)}) collective-permute-start(f32[512,128]{1,0:T(8,128)S(1)} %get-tuple-element.57.refs_7_), channel_id=1, source_target_pairs={{0,4},{4,0},{8,12},{12,8},{16,20},{20,16},{24,28},{28,24},{1,5},{5... | collective-permute-start | bytes 786440 | tf_op jit(solution)/shard_map/ppermute | solution.py:400
  39.3 6.8 %collective-permute-start.6 = (f32[512,128]{1,0:T(8,128)S(1)}, f32[512,128]{1,0:T(8,128)S(1)}, u32[]{:S(2)}, u32[]{:S(2)}) collective-permute-start(f32[512,128]{1,0:T(8,128)S(1)} %get-tuple-element.60.refs_7_), channel_id=1, source_target_pairs={{0,4},{4,0},{8,12},{12,8},{16,20},{20,16},{24,28},{28,24},{1,5},{5... | collective-permute-start | bytes 786440 | tf_op jit(solution)/shard_map/ppermute | solution.py:400
  47.5 1.8 %collective-permute-start.10 = (f32[8,512]{1,0:T(8,128)S(1)}, f32[8,512]{1,0:T(8,128)S(1)}, u32[]{:S(2)}, u32[]{:S(2)}) collective-permute-start(f32[8,512]{1,0:T(8,128)S(1)} %get-tuple-element.64.refs_5_), channel_id=1, source_target_pairs={{0,3},{1,0},{2,1},{3,2},{4,7},{5,4},{6,5},{7,6},{8,11},{9,8},{10,9... | collective-permute-start | bytes 49160 | tf_op jit(solution)/shard_map/ppermute | solution.py:464
  47.5 3.8 %collective-permute-start.9 = (f32[8,512]{1,0:T(8,128)S(1)}, f32[8,512]{1,0:T(8,128)S(1)}, u32[]{:S(2)}, u32[]{:S(2)}) collective-permute-start(f32[8,512]{1,0:T(8,128)S(1)} %get-tuple-element.64.refs_5_), channel_id=1, source_target_pairs={{0,2},{1,3},{2,0},{3,1},{4,6},{5,7},{6,4},{7,5},{8,10},{9,11},{10,... | collective-permute-start | bytes 49160 | tf_op jit(solution)/shard_map/ppermute | solution.py:464
  49.1 3.2 %collective-permute-start.8 = (f32[8,512]{1,0:T(8,128)S(1)}, f32[8,512]{1,0:T(8,128)S(1)}, u32[]{:S(2)}, u32[]{:S(2)}) collective-permute-start(f32[8,512]{1,0:T(8,128)S(1)} %get-tuple-element.64.refs_5_), channel_id=1, source_target_pairs={{0,1},{1,2},{2,3},{3,0},{4,5},{5,6},{6,7},{7,4},{8,9},{9,10},{10,1... | collective-permute-start | bytes 49160 | tf_op jit(solution)/shard_map/ppermute | solution.py:464
  54.1 9.3 %collective-permute-start.11 = (f32[520,128]{1,0:T(8,128)S(1)}, f32[520,128]{1,0:T(8,128)S(1)}, u32[]{:S(2)}, u32[]{:S(2)}) collective-permute-start(f32[520,128]{1,0:T(8,128)S(1)} %get-tuple-element.69.refs_10_), channel_id=1, source_target_pairs={{0,4},{4,0},{8,12},{12,8},{16,20},{20,16},{24,28},{28,24},{1,5},{5... | collective-permute-start | bytes 798728 | tf_op jit(solution)/shard_map/ppermute | solution.py:369
  57.5 10.9 %collective-permute-start.12 = (f32[520,128]{1,0:T(8,128)S(1)}, f32[520,128]{1,0:T(8,128)S(1)}, u32[]{:S(2)}, u32[]{:S(2)}) collective-permute-start(f32[520,128]{1,0:T(8,128)S(1)} %get-tuple-element.71.refs_10_), channel_id=1, source_target_pairs={{0,4},{4,0},{8,12},{12,8},{16,20},{20,16},{24,28},{28,24},{1,5},{5... | collective-permute-start | bytes 798728 | tf_op jit(solution)/shard_map/ppermute | solution.py:369
  63.5 5.0 %collective-permute-start.13 = (f32[512,128]{1,0:T(8,128)S(1)}, f32[512,128]{1,0:T(8,128)S(1)}, u32[]{:S(2)}, u32[]{:S(2)}) collective-permute-start(f32[512,128]{1,0:T(8,128)S(1)} %shard_map.115.refs_6_), channel_id=1, source_target_pairs={{24,16},{28,20},{25,17},{29,21},{26,18},{30,22},{27,19},{31,23}} | collective-permute-start | bytes 786440 | tf_op jit(solution)/shard_map/ppermute | solution.py:390
  68.5 5.0 %collective-permute-start.14 = (f32[512,128]{1,0:T(8,128)S(1)}, f32[512,128]{1,0:T(8,128)S(1)}, u32[]{:S(2)}, u32[]{:S(2)}) collective-permute-start(f32[512,128]{1,0:T(8,128)S(1)} %shard_map.117.refs_7_), channel_id=1, source_target_pairs={{24,16},{28,20},{16,8},{20,12},{25,17},{29,21},{17,9},{21,13},{26,... | collective-permute-start | bytes 786440 | tf_op jit(solution)/shard_map/ppermute | solution.py:390
  73.5 24.0 %collective-permute-start.15 = (f32[512,128]{1,0:T(8,128)S(1)}, f32[512,128]{1,0:T(8,128)S(1)}, u32[]{:S(2)}, u32[]{:S(2)}) collective-permute-start(f32[512,128]{1,0:T(8,128)S(1)} %shard_map.119.refs_7_), channel_id=1, source_target_pairs={{16,8},{20,12},{8,0},{12,4},{17,9},{21,13},{9,1},{13,5},{18,10},{2... | collective-permute-start | bytes 786440 | tf_op jit(solution)/shard_map/ppermute | solution.py:390
  97.5 8.3 %collective-permute-start.16 = (f32[512,128]{1,0:T(8,128)S(1)}, f32[512,128]{1,0:T(8,128)S(1)}, u32[]{:S(2)}, u32[]{:S(2)}) collective-permute-start(f32[512,128]{1,0:T(8,128)S(1)} %shard_map.121.refs_5_), channel_id=1, source_target_pairs={{8,0},{12,4},{9,1},{13,5},{10,2},{14,6},{11,3},{15,7}} | collective-permute-start | bytes 786440 | tf_op jit(solution)/shard_map/ppermute | solution.py:390
  98.9 12.6 %collective-permute-start.18 = (f32[512,128]{1,0:T(8,128)S(1)}, f32[512,128]{1,0:T(8,128)S(1)}, u32[]{:S(2)}, u32[]{:S(2)}) collective-permute-start(f32[512,128]{1,0:T(8,128)S(1)} %get-tuple-element.86.refs_7_), channel_id=1, source_target_pairs={{0,4},{4,0},{8,12},{12,8},{16,20},{20,16},{24,28},{28,24},{1,5},{5... | collective-permute-start | bytes 786440 | tf_op jit(solution)/shard_map/ppermute | solution.py:400
  105.8 7.6 %collective-permute-start.17 = (f32[512,128]{1,0:T(8,128)S(1)}, f32[512,128]{1,0:T(8,128)S(1)}, u32[]{:S(2)}, u32[]{:S(2)}) collective-permute-start(f32[512,128]{1,0:T(8,128)S(1)} %get-tuple-element.90.refs_6_), channel_id=1, source_target_pairs={{0,4},{4,0},{8,12},{12,8},{16,20},{20,16},{24,28},{28,24},{1,5},{5... | collective-permute-start | bytes 786440 | tf_op jit(solution)/shard_map/ppermute | solution.py:400

commit v4 on v3

--- a/solution.py
+++ b/solution.py
@@ -73,9 +73,14 @@
     def group(self, info):
         return info[0][0] if self.slot == "mine" else 1 - info[0][0]
 
+    def head(self, info, j):
+        return (2 * self.chunk + self.group(info)) * self.half + pl.program_id(0) * self.per_step + j
+
     def row(self, cumul_ref, info, j):
-        head = (2 * self.chunk + self.group(info)) * self.half + pl.program_id(0) * self.per_step + j
-        return cumul_ref[pl.ds(head, 1), :]
+        return cumul_ref[pl.ds(self.head(info, j), 1), :]
+
+    def wide_cols(self, info, j):
+        return pl.ds(pl.multiple_of(self.head(info, j) * HEAD_DIM, HEAD_DIM), HEAD_DIM)
 
     def state_rows(self, j):
         start = (pl.program_id(0) * self.per_step + j) * HEAD_DIM
@@ -92,9 +97,8 @@
 def pieces_kernel(part, info, key_ref, value_ref, cumul_ref, out_ref):
     for j in range(part.per_step):
         row = part.row(cumul_ref, info, j)
-        out_ref[part.state_rows(j), :] = outer_sum(
-            key_ref[:, cols(j)], trail_row(row), value_ref[:, cols(j)]
-        )
+        at = part.wide_cols(info, j)
+        out_ref[part.state_rows(j), :] = outer_sum(key_ref[:, at], trail_row(row), value_ref[:, at])
     store_decays(part, info, cumul_ref, out_ref)
 
 
@@ -110,7 +114,8 @@
     for j in range(part.per_step):
         row = part.row(cumul_ref, info, j)
         col = column(row)
-        query, key, value = query_ref[:, cols(j)], key_ref[:, cols(j)], value_ref[:, cols(j)]
+        at = part.wide_cols(info, j)
+        query, key, value = query_ref[:, at], key_ref[:, at], value_ref[:, at]
         for top in range(0, BLOCK, TILE):
             end = top + TILE
             scores = dot(query[top:end], key[:end], NT)
@@ -119,7 +124,7 @@
                 lax.broadcasted_iota(jnp.int32, (TILE, end), 1)
             )
             weights = (scores * jnp.exp(jnp.where(causal, spread, -1e30))).astype(bf16)
-            out_ref[top:end, cols(j)] = dot(weights, value[:end])
+            out_ref[top:end, part.state_rows(j)] = dot(weights, value[:end])
 
 
 def output_kernel(
@@ -132,11 +137,12 @@
     for j in range(part.per_step):
         lead = jnp.exp(column(part.row(cumul_ref, info, j)))
         high, low = halves(state_ref[part.state_rows(j), :])
-        query = query_ref[:, cols(j)]
-        out = inner_ref[:, cols(j)] + lead * (dot(query, high) + dot(query, low))
-        out_ref[:, cols(j)] = out
+        at, here = part.wide_cols(info, j), part.state_rows(j)
+        query = query_ref[:, at]
+        out = inner_ref[:, here] + lead * (dot(query, high) + dot(query, low))
+        out_ref[:, here] = out
         squares += out * out
-        products += cot_ref[:, cols(j)].astype(f32) * gain_ref[:, cols(j)] * out
+        products += cot_ref[:, at].astype(f32) * gain_ref[:, at] * out
 
     @pl.when(step == 0)
     def _():
@@ -168,14 +174,15 @@
     mean_term = inverse * sums[1:2] / features
     inverse_col, mean_col = column(inverse), column(mean_term)
     for j in range(part.per_step):
-        gain = gain_ref[:, cols(j)]
-        normed = out_ref[:, cols(j)] * inverse_col
+        at, here = part.wide_cols(info, j), part.state_rows(j)
+        gain = gain_ref[:, at]
+        normed = out_ref[:, here] * inverse_col
         attended_ref[:, cols(j)] = (normed * gain).astype(bf16)
-        scaled_grad = cot_ref[:, cols(j)].astype(f32) * gain
+        scaled_grad = cot_ref[:, at].astype(f32) * gain
         grad = (inverse_col * (scaled_grad - normed * mean_col)).astype(bf16)
-        grad_ref[:, cols(j)] = grad
+        grad_ref[:, here] = grad
         row = part.row(cumul_ref, info, j)
-        piece_ref[part.state_rows(j), :] = outer_sum(query_ref[:, cols(j)], jnp.exp(row), grad)
+        piece_ref[part.state_rows(j), :] = outer_sum(query_ref[:, at], jnp.exp(row), grad)
     store_decays(part, info, cumul_ref, piece_ref)
 
 
@@ -186,8 +193,9 @@
     for j in range(part.per_step):
         row = part.row(cumul_ref, info, j)
         col = column(row)
-        query, key = query_ref[:, cols(j)], key_ref[:, cols(j)]
-        value, grad = value_ref[:, cols(j)], grad_ref[:, cols(j)]
+        at, here = part.wide_cols(info, j), part.state_rows(j)
+        query, key = query_ref[:, at], key_ref[:, at]
+        value, grad = value_ref[:, at], grad_ref[:, here]
         high, low = halves(state_ref[part.state_rows(j), :])
         outer = jnp.exp(col) * (dot(grad, high, NT) + dot(grad, low, NT))
         for top in range(0, BLOCK, TILE):
@@ -201,8 +209,8 @@
             decays = jnp.exp(jnp.where(causal, spread, -1e30))
             weights = (scores * decays).astype(bf16)
             grad_weights = (grad_scores * decays).astype(bf16)
-            inner_value_ref[top:end, cols(j)] = dot(weights, grad[top:])
-            inner_key_ref[top:end, cols(j)] = dot(grad_weights, query[top:])
+            inner_value_ref[top:end, here] = dot(weights, grad[top:])
+            inner_key_ref[top:end, here] = dot(grad_weights, query[top:])
             inner_query = dot(grad_weights, key[top:end], TN)
             outer = inner_query + outer if top == 0 else jnp.concatenate(
                 [outer[:top], outer[top:] + inner_query], axis=0
@@ -217,12 +225,13 @@
     for j in range(part.per_step):
         trail = column(trail_row(part.row(cumul_ref, info, j)))
         high, low = halves(state_ref[part.state_rows(j), :])
-        key, value = key_ref[:, cols(j)], value_ref[:, cols(j)]
+        at, here = part.wide_cols(info, j), part.state_rows(j)
+        key, value = key_ref[:, at], value_ref[:, at]
         grad_key_ref[:, cols(j)] = (
-            inner_key_ref[:, cols(j)] + trail * (dot(value, high, NT) + dot(value, low, NT))
+            inner_key_ref[:, here] + trail * (dot(value, high, NT) + dot(value, low, NT))
         ).astype(bf16)
         grad_value_ref[:, cols(j)] = (
-            inner_value_ref[:, cols(j)] + trail * (dot(key, high) + dot(key, low))
+            inner_value_ref[:, here] + trail * (dot(key, high) + dot(key, low))
         ).astype(bf16)
 
 
@@ -321,7 +330,7 @@
                 scratch_shapes=list(scratch),
             ),
             input_output_aliases=aliases or {},
-            compiler_params=pltpu.CompilerParams(vmem_limit_bytes=16 * 1024 * 1024),
+            compiler_params=pltpu.CompilerParams(vmem_limit_bytes=24 * 1024 * 1024),
             cost_estimate=pl.CostEstimate(
                 flops=int(cost * 1e9), bytes_accessed=int(cost * 2.5e6), transcendentals=0
             ),
@@ -337,17 +346,11 @@
         return shape, fixed(shape.shape)
 
     class Views(Part):
-        def full(self, array, rows=tokens):
-            return array, self.full_spec(rows)
-
-        def full_spec(self, rows=tokens):
+        def full_spec(self):
             return pl.BlockSpec(
-                (rows, self.per_step * HEAD_DIM),
+                (tokens, self.per_step * HEAD_DIM),
                 lambda i, *info: (0, (2 * self.chunk + self.group(info)) * self.steps + i),
             )
-
-        def local(self, array):
-            return array, pl.BlockSpec((tokens, self.per_step * HEAD_DIM), lambda i, *info: (0, i))
 
         def call(self, kernel, ins, outs, **options):
             return run(functools.partial(kernel, self), self.steps, ins, outs, **options)
@@ -413,14 +416,14 @@
         if not held_cumul:
             piece, cumul = part.call(
                 first_pieces_kernel,
-                [part.full(key_vecs), part.full(value_vecs), plain(log_decay.T)],
+                [plain(key_vecs), plain(value_vecs), plain(log_decay.T)],
                 [give(wide_state), give(jax.ShapeDtypeStruct((heads, tokens), f32))], cost=1.0,
             )
             held_cumul.append(cumul)
             return piece
         cumul = held_cumul[0]
         return part.call(
-            pieces_kernel, [part.full(key_vecs), part.full(value_vecs), plain(cumul)],
+            pieces_kernel, [plain(key_vecs), plain(value_vecs), plain(cumul)],
             [give(wide_state)], after=after, cost=1.0,
         )[0]
 
@@ -434,17 +437,17 @@
     def inner_work(part, after):
         inner[part], = part.call(
             inner_kernel,
-            [part.full(queries), part.full(key_vecs), part.full(value_vecs), cumul_in()],
-            [part.local(local)], after=after, cost=2.2,
+            [plain(queries), plain(key_vecs), plain(value_vecs), cumul_in()],
+            [give(local)], after=after, cost=2.2,
         )
         return inner[part]
 
     def output_work(part, before, after):
         outs[part], sums = part.call(
             output_kernel,
-            [part.local(inner[part]), part.full(queries), part.full(cotangent), part.full(gain, 1),
+            [plain(inner[part]), plain(queries), plain(cotangent), plain(gain),
              cumul_in(), plain(before), plain(state_sums[0])],
-            [part.local(local), give(sums_shape)],
+            [give(local), give(sums_shape)],
             scratch=[pltpu.VMEM((tokens, HEAD_DIM), f32)] * 2, after=after, cost=1.4,
         )
         state_sums[0] = sums
@@ -475,9 +478,9 @@
         before = target(attended)
         whole_out, grads[part], piece = part.call(
             functools.partial(grad_kernel, features),
-            [part.local(outs[part]), part.full(cotangent), part.full(gain, 1), part.full(queries),
+            [plain(outs[part]), plain(cotangent), plain(gain), plain(queries),
              cumul_in()] + [plain(share) for share in shares],
-            [(whole, part.full_spec()), part.local(local_low), give(wide_state)],
+            [(whole, part.full_spec()), give(local_low), give(wide_state)],
             after=before + tuple(after), aliases={7 + head_count: 0} if before else None, cost=2.0,
         )
         attended.append(whole_out)
@@ -487,9 +490,9 @@
         held = target(grad_queries)
         whole_out, *inner_grads[part] = part.call(
             backward_kernel,
-            [part.full(queries), part.full(key_vecs), part.full(value_vecs),
-             part.local(grads[part]), cumul_in(), plain(before)],
-            [(whole, part.full_spec()), part.local(local), part.local(local)],
+            [plain(queries), plain(key_vecs), plain(value_vecs),
+             plain(grads[part]), cumul_in(), plain(before)],
+            [(whole, part.full_spec()), give(local), give(local)],
             after=held + tuple(after), aliases={8: 0} if held else None, cost=4.3,
         )
         grad_queries.append(whole_out)
@@ -499,8 +502,8 @@
         held = target(grad_keys) + target(grad_values)
         whole_key, whole_value = part.call(
             final_kernel,
-            [part.local(inner_grads[part][0]), part.local(inner_grads[part][1]),
-             part.full(key_vecs), part.full(value_vecs), cumul_in(), plain(before)],
+            [plain(inner_grads[part][0]), plain(inner_grads[part][1]),
+             plain(key_vecs), plain(value_vecs), cumul_in(), plain(before)],
             [(whole, part.full_spec())] * 2,
             after=held + tuple(after), aliases={8: 0, 9: 1} if held else None, cost=2.0,
         )

time: 116 us -> 115 us (level)
  Pallas kernels: 51.9 us -> 45.6 us
  waiting for transfers between devices: 32.1 us -> 37.5 us
    pallas_call x36, Pallas kernels: 51.9 us -> 45.6 us  [run(): pl.pallas_call(body, out_shape=[shape for shape, _ in outs], grid_spec=pl...]
    ppermute x8, waiting for transfers between devices: 22.6 us -> 26.2 us  [chain(): arrived[r] = lax.ppermute(value, 'seq', pairs)]
  transfers between devices with their start and end apart: 19 -> 19, of which waited for: 10 -> 10; matrix products, arithmetic and copies ran while one was open for 0% -> 0% of each run, Pallas kernels for 39% -> 35%
where the time goes in v4:
time: 115 us
  Pallas kernels  45.6 us (40%)
  waiting for transfers between devices  37.5 us (33%)
  starting transfers between devices  26.2 us (23%)
  local copies, waits for them, and re-layouts  4.73 us (4%)
    pallas_call x36, Pallas kernels, run(): pl.pallas_call(body, out_shape=[shape for shape, _ in outs], grid_spec=pl...  45.6 us
    ppermute x8, waiting for transfers between devices, chain(): arrived[r] = lax.ppermute(value, 'seq', pairs)  26.2 us
    ppermute x8, starting transfers between devices, chain(): arrived[r] = lax.ppermute(value, 'seq', pairs)  13.9 us
    ppermute x4, starting transfers between devices, chain(): theirs.append(lax.ppermute(send, 'seq', swap))  5.39 us
    ppermute x4, starting transfers between devices, chain(): received.append(lax.ppermute(sent, 'seq', swap))  5.15 us
    unnamed x16, local copies, waits for them, and re-layouts  4.73 us
    ppermute x4, waiting for transfers between devices, chain(): received.append(lax.ppermute(sent, 'seq', swap))  4.2 us
    ppermute x4, waiting for transfers between devices, chain(): theirs.append(lax.ppermute(send, 'seq', swap))  4.07 us
  transfers between devices with their start and end apart: 19, of which 10 were waited for; matrix products, arithmetic and copies ran while one was open for 0% of the time, Pallas kernels for 35%

profile of v4, /device:TPU:0, one launch (start us, length us, event | category | flops | bytes accessed | tf_op | source)
XLA Modules:
  0.0 115.0 jit_solution(916787630729968758)
XLA Ops:
  0.7 1.6 %copy-done.2 = bf16[512,2048]{1,0:T(8,128)(2,1)S(1)} copy-done((bf16[512,2048]{1,0:T(8,128)(2,1)S(1)}, bf16[512,2048]{1,0:T(8,128)(2,1)}, u32[]{:S(2)}) %copy-start.2) | copy-done | bytes 2097176
  2.2 1.6 %copy-done.4 = bf16[512,2048]{1,0:T(8,128)(2,1)S(1)} copy-done((bf16[512,2048]{1,0:T(8,128)(2,1)S(1)}, bf16[512,2048]{1,0:T(8,128)(2,1)}, u32[]{:S(2)}) %copy-start.4) | copy-done | bytes 2097176
  5.7 3.0 %collective-permute-start.1 = (f32[520,128]{1,0:T(8,128)S(1)}, f32[520,128]{1,0:T(8,128)S(1)}, u32[]{:S(2)}, u32[]{:S(2)}) collective-permute-start(f32[520,128]{1,0:T(8,128)S(1)} %get-tuple-element.55.refs_3_), channel_id=1, source_target_pairs={{0,4},{4,0},{8,12},{12,8},{16,20},{20,16},{24,28},{28,24},{1,5},{5... | collective-permute-start | bytes 798728 | tf_op jit(solution)/shard_map/ppermute | solution.py:372
  12.0 1.9 %shard_map.97.refs_3_.refs_0_ = f32[512,512]{1,0:T(8,128)S(1)} custom-call(s32[1]{0:T(128)} %bitcast.member_ref, s32[1]{0:T(128)} %bitcast.1.pair_ref, bf16[512,2048]{1,0:T(8,128)(2,1)S(1)} %copy-done.1, bf16[512,2048]{1,0:T(8,128)(2,1)S(1)} %copy-done.2, bf16[512,2048]{1,0:T(8,128)(2,1)S(1)} %copy-done.4, ...), custom_call_target="tpu_custom_call" | custom-call | flops 2200000000 | bytes 5500000 | tf_op jit(solution)/shard_map/pallas_call | solution.py:322
  13.9 2.0 %collective-permute-done.1.refs_1_.refs_3_ = f32[520,128]{1,0:T(8,128)S(1)} collective-permute-done((f32[520,128]{1,0:T(8,128)S(1)}, f32[520,128]{1,0:T(8,128)S(1)}, u32[]{:S(2)}, u32[]{:S(2)}) %collective-permute-start.1) | collective-permute-done | bytes 266272 | tf_op jit(solution)/shard_map/ppermute | solution.py:372
  16.0 4.0 %collective-permute-start.2 = (f32[512,128]{1,0:T(8,128)S(1)}, f32[512,128]{1,0:T(8,128)S(1)}, u32[]{:S(2)}, u32[]{:S(2)}) collective-permute-start(f32[512,128]{1,0:T(8,128)S(1)} %shard_map.98.refs_4_), channel_id=1, source_target_pairs={{0,8},{4,12},{1,9},{5,13},{2,10},{6,14},{3,11},{7,15}} | collective-permute-start | bytes 786440 | tf_op jit(solution)/shard_map/ppermute | solution.py:393
  20.0 1.9 %shard_map.99.refs_5_.refs_0_ = f32[512,512]{1,0:T(8,128)S(1)} custom-call(s32[1]{0:T(128)} %bitcast.member_ref, s32[1]{0:T(128)} %bitcast.1.pair_ref, bf16[512,2048]{1,0:T(8,128)(2,1)S(1)} %copy-done.1, bf16[512,2048]{1,0:T(8,128)(2,1)S(1)} %copy-done.3, bf16[512,2048]{1,0:T(8,128)(2,1)S(1)} %copy-done.4, ...), custom_call_target="tpu_custom_call" | custom-call | flops 2200000000 | bytes 5500000 | tf_op jit(solution)/shard_map/pallas_call | solution.py:322
  21.9 1.9 %collective-permute-done.2.refs_4_.refs_2_ = f32[512,128]{1,0:T(8,128)S(1)} collective-permute-done((f32[512,128]{1,0:T(8,128)S(1)}, f32[512,128]{1,0:T(8,128)S(1)}, u32[]{:S(2)}, u32[]{:S(2)}) %collective-permute-start.2) | collective-permute-done | bytes 262176 | tf_op jit(solution)/shard_map/ppermute | solution.py:393
  23.9 4.4 %collective-permute-start.3 = (f32[512,128]{1,0:T(8,128)S(1)}, f32[512,128]{1,0:T(8,128)S(1)}, u32[]{:S(2)}, u32[]{:S(2)}) collective-permute-start(f32[512,128]{1,0:T(8,128)S(1)} %shard_map.100.refs_4_), channel_id=1, source_target_pairs={{0,8},{4,12},{8,16},{12,20},{1,9},{5,13},{9,17},{13,21},{2,10},{6,... | collective-permute-start | bytes 786440 | tf_op jit(solution)/shard_map/ppermute | solution.py:393
  28.3 1.9 %shard_map.101.refs_5_.refs_0_ = f32[512,512]{1,0:T(8,128)S(1)} custom-call(s32[1]{0:T(128)} %bitcast.member_ref, s32[1]{0:T(128)} %bitcast.1.pair_ref, bf16[512,2048]{1,0:T(8,128)(2,1)S(1)} %copy-done.1, bf16[512,2048]{1,0:T(8,128)(2,1)S(1)} %copy-done.3, bf16[512,2048]{1,0:T(8,128)(2,1)S(1)} %copy-done.5, ...), custom_call_target="tpu_custom_call" | custom-call | flops 2200000000 | bytes 5500000 | tf_op jit(solution)/shard_map/pallas_call | solution.py:322
  30.2 1.9 %collective-permute-done.3.refs_4_.refs_3_.refs_2_ = f32[512,128]{1,0:T(8,128)S(1)} collective-permute-done((f32[512,128]{1,0:T(8,128)S(1)}, f32[512,128]{1,0:T(8,128)S(1)}, u32[]{:S(2)}, u32[]{:S(2)}) %collective-permute-start.3) | collective-permute-done | bytes 262176 | tf_op jit(solution)/shard_map/ppermute | solution.py:393
  32.8 1.9 %shard_map.103.refs_3_.refs_0_ = f32[512,512]{1,0:T(8,128)S(1)} custom-call(s32[1]{0:T(128)} %bitcast.member_ref, s32[1]{0:T(128)} %bitcast.1.pair_ref, bf16[512,2048]{1,0:T(8,128)(2,1)S(1)} %copy-done.1, bf16[512,2048]{1,0:T(8,128)(2,1)S(1)} %copy-done.3, bf16[512,2048]{1,0:T(8,128)(2,1)S(1)} %copy-done.5, ...), custom_call_target="tpu_custom_call" | custom-call | flops 2200000000 | bytes 5500000 | tf_op jit(solution)/shard_map/pallas_call | solution.py:322
  35.7 1.6 %collective-permute-start.7 = (f32[512,128]{1,0:T(8,128)S(1)}, f32[512,128]{1,0:T(8,128)S(1)}, u32[]{:S(2)}, u32[]{:S(2)}) collective-permute-start(f32[512,128]{1,0:T(8,128)S(1)} %get-tuple-element.57.refs_7_), channel_id=1, source_target_pairs={{0,4},{4,0},{8,12},{12,8},{16,20},{20,16},{24,28},{28,24},{1,5},{5... | collective-permute-start | bytes 786440 | tf_op jit(solution)/shard_map/ppermute | solution.py:403
  40.3 2.4 %collective-permute-done.7.refs_5_ = f32[512,128]{1,0:T(8,128)S(1)} collective-permute-done((f32[512,128]{1,0:T(8,128)S(1)}, f32[512,128]{1,0:T(8,128)S(1)}, u32[]{:S(2)}, u32[]{:S(2)}) %collective-permute-start.7) | collective-permute-done | bytes 262176 | tf_op jit(solution)/shard_map/ppermute | solution.py:403
  43.7 1.7 %collective-permute-done.6.refs_5_ = f32[512,128]{1,0:T(8,128)S(1)} collective-permute-done((f32[512,128]{1,0:T(8,128)S(1)}, f32[512,128]{1,0:T(8,128)S(1)}, u32[]{:S(2)}, u32[]{:S(2)}) %collective-permute-start.6) | collective-permute-done | bytes 262176 | tf_op jit(solution)/shard_map/ppermute | solution.py:403
  48.3 2.0 %collective-permute-done.9.refs_7_ = f32[8,512]{1,0:T(8,128)S(1)} collective-permute-done((f32[8,512]{1,0:T(8,128)S(1)}, f32[8,512]{1,0:T(8,128)S(1)}, u32[]{:S(2)}, u32[]{:S(2)}) %collective-permute-start.9) | collective-permute-done | bytes 16416 | tf_op jit(solution)/shard_map/ppermute | solution.py:467
  51.2 1.7 %shard_map.111 = (bf16[512,2048]{1,0:T(8,128)(2,1)}, bf16[512,512]{1,0:T(8,128)(2,1)S(1)}, f32[520,128]{1,0:T(8,128)S(1)}) custom-call(s32[1]{0:T(128)} %bitcast.member_ref, s32[1]{0:T(128)} %bitcast.1.pair_ref, f32[512,512]{1,0:T(8,128)S(1)} %get-tuple-element.67.refs_0_, bf16[512,2048]{1,0:T(8,128)(2,1)S(1)} %copy-done, f32[1,2048]{1,0:T(1,128)S(1)} %bitcast.8, ...), custom_call_target="tpu_custom_call" | custom-call | flops 2000000000 | bytes 5000000 | tf_op jit(solution)/shard_map/pallas_call | solution.py:322
  54.5 1.7 %shard_map.112 = (bf16[512,2048]{1,0:T(8,128)(2,1)}, bf16[512,512]{1,0:T(8,128)(2,1)S(1)}, f32[520,128]{1,0:T(8,128)S(1)}) custom-call(s32[1]{0:T(128)} %bitcast.member_ref, s32[1]{0:T(128)} %bitcast.1.pair_ref, f32[512,512]{1,0:T(8,128)S(1)} %get-tuple-element.66.refs_0_, bf16[512,2048]{1,0:T(8,128)(2,1)S(1)} %copy-done, ...), custom_call_target="tpu_custom_call", output_to_operand_aliasing={{0}: (11, {})} | custom-call | flops 2000000000 | bytes 5000000 | tf_op jit(solution)/shard_map/pallas_call | solution.py:322
  56.7 1.7 %shard_map.113 = (bf16[512,2048]{1,0:T(8,128)(2,1)}, bf16[512,512]{1,0:T(8,128)(2,1)S(1)}, f32[520,128]{1,0:T(8,128)S(1)}) custom-call(s32[1]{0:T(128)} %bitcast.member_ref, s32[1]{0:T(128)} %bitcast.1.pair_ref, f32[512,512]{1,0:T(8,128)S(1)} %get-tuple-element.65.refs_0_, bf16[512,2048]{1,0:T(8,128)(2,1)S(1)} %copy-done, ...), custom_call_target="tpu_custom_call", output_to_operand_aliasing={{0}: (11, {})} | custom-call | flops 2000000000 | bytes 5000000 | tf_op jit(solution)/shard_map/pallas_call | solution.py:322
  58.4 1.7 %shard_map.114 = (bf16[512,2048]{1,0:T(8,128)(2,1)}, bf16[512,512]{1,0:T(8,128)(2,1)S(1)}, f32[520,128]{1,0:T(8,128)S(1)}) custom-call(s32[1]{0:T(128)} %bitcast.member_ref, s32[1]{0:T(128)} %bitcast.1.pair_ref, f32[512,512]{1,0:T(8,128)S(1)} %get-tuple-element.61.refs_0_, bf16[512,2048]{1,0:T(8,128)(2,1)S(1)} %copy-done, ...), custom_call_target="tpu_custom_call", output_to_operand_aliasing={{0}: (11, {})} | custom-call | flops 2000000000 | bytes 5000000 | tf_op jit(solution)/shard_map/pallas_call | solution.py:322
  60.1 2.2 %collective-permute-done.11.refs_1_.refs_3_ = f32[520,128]{1,0:T(8,128)S(1)} collective-permute-done((f32[520,128]{1,0:T(8,128)S(1)}, f32[520,128]{1,0:T(8,128)S(1)}, u32[]{:S(2)}, u32[]{:S(2)}) %collective-permute-start.11) | collective-permute-done | bytes 266272 | tf_op jit(solution)/shard_map/ppermute | solution.py:372
  63.2 3.9 %shard_map.116 = (bf16[512,2048]{1,0:T(8,128)(2,1)}, f32[512,512]{1,0:T(8,128)S(1)}, f32[512,512]{1,0:T(8,128)S(1)}) custom-call(s32[1]{0:T(128)} %bitcast.member_ref, s32[1]{0:T(128)} %bitcast.1.pair_ref, bf16[512,2048]{1,0:T(8,128)(2,1)S(1)} %copy-done.1, bf16[512,2048]{1,0:T(8,128)(2,1)S(1)} %copy-done.3, bf16[512,2048]{1,0:T(8,128)(2,1)S(1)} %copy-done.5, ...), custom_call_target="tpu_custom_call" | custom-call | flops 4300000256 | bytes 10750000 | tf_op jit(solution)/shard_map/pallas_call | solution.py:322
  67.8 4.0 %shard_map.118 = (bf16[512,2048]{1,0:T(8,128)(2,1)}, f32[512,512]{1,0:T(8,128)S(1)}, f32[512,512]{1,0:T(8,128)S(1)}) custom-call(s32[1]{0:T(128)} %bitcast.member_ref, s32[1]{0:T(128)} %bitcast.1.pair_ref, bf16[512,2048]{1,0:T(8,128)(2,1)S(1)} %copy-done.1, bf16[512,2048]{1,0:T(8,128)(2,1)S(1)} %copy-done.3, ...), custom_call_target="tpu_custom_call", output_to_operand_aliasing={{0}: (8, {})} | custom-call | flops 4300000256 | bytes 10750000 | tf_op jit(solution)/shard_map/pallas_call | solution.py:322
  73.0 4.0 %shard_map.120 = (bf16[512,2048]{1,0:T(8,128)(2,1)}, f32[512,512]{1,0:T(8,128)S(1)}, f32[512,512]{1,0:T(8,128)S(1)}) custom-call(s32[1]{0:T(128)} %bitcast.member_ref, s32[1]{0:T(128)} %bitcast.1.pair_ref, bf16[512,2048]{1,0:T(8,128)(2,1)S(1)} %copy-done.1, bf16[512,2048]{1,0:T(8,128)(2,1)S(1)} %copy-done.3, ...), custom_call_target="tpu_custom_call", output_to_operand_aliasing={{0}: (8, {})} | custom-call | flops 4300000256 | bytes 10750000 | tf_op jit(solution)/shard_map/pallas_call | solution.py:322
  77.0 21.0 %collective-permute-done.15.refs_2_.refs_4_.refs_3_ = f32[512,128]{1,0:T(8,128)S(1)} collective-permute-done((f32[512,128]{1,0:T(8,128)S(1)}, f32[512,128]{1,0:T(8,128)S(1)}, u32[]{:S(2)}, u32[]{:S(2)}) %collective-permute-start.15) | collective-permute-done | bytes 262176 | tf_op jit(solution)/shard_map/ppermute | solution.py:393
  99.4 1.6 %collective-permute-start.18 = (f32[512,128]{1,0:T(8,128)S(1)}, f32[512,128]{1,0:T(8,128)S(1)}, u32[]{:S(2)}, u32[]{:S(2)}) collective-permute-start(f32[512,128]{1,0:T(8,128)S(1)} %get-tuple-element.86.refs_7_), channel_id=1, source_target_pairs={{0,4},{4,0},{8,12},{12,8},{16,20},{20,16},{24,28},{28,24},{1,5},{5... | collective-permute-start | bytes 786440 | tf_op jit(solution)/shard_map/ppermute | solution.py:403
  101.0 3.9 %shard_map.123 = (bf16[512,2048]{1,0:T(8,128)(2,1)}, f32[512,512]{1,0:T(8,128)S(1)}, f32[512,512]{1,0:T(8,128)S(1)}) custom-call(s32[1]{0:T(128)} %bitcast.member_ref, s32[1]{0:T(128)} %bitcast.1.pair_ref, bf16[512,2048]{1,0:T(8,128)(2,1)S(1)} %copy-done.1, bf16[512,2048]{1,0:T(8,128)(2,1)S(1)} %copy-done.3, ...), custom_call_target="tpu_custom_call", output_to_operand_aliasing={{0}: (8, {})} | custom-call | flops 4300000256 | bytes 10750000 | tf_op jit(solution)/shard_map/pallas_call | solution.py:322
  106.4 1.6 %collective-permute-start.17 = (f32[512,128]{1,0:T(8,128)S(1)}, f32[512,128]{1,0:T(8,128)S(1)}, u32[]{:S(2)}, u32[]{:S(2)}) collective-permute-start(f32[512,128]{1,0:T(8,128)S(1)} %get-tuple-element.90.refs_6_), channel_id=1, source_target_pairs={{0,4},{4,0},{8,12},{12,8},{16,20},{20,16},{24,28},{28,24},{1,5},{5... | collective-permute-start | bytes 786440 | tf_op jit(solution)/shard_map/ppermute | solution.py:403
  108.0 1.7 %shard_map.125 = (bf16[512,2048]{1,0:T(8,128)(2,1)}, bf16[512,2048]{1,0:T(8,128)(2,1)}) custom-call(s32[1]{0:T(128)} %bitcast.member_ref, s32[1]{0:T(128)} %bitcast.1.pair_ref, f32[512,512]{1,0:T(8,128)S(1)} %get-tuple-element.81.refs_5_.refs_0_, f32[512,512]{1,0:T(8,128)S(1)} %get-tuple-element.94.refs_1_, bf16[512,2048]{1,0:T(8,128)(2,1)S(1)} %copy-done.3, ...), custom_call_target="tpu_custom_call" | custom-call | flops 2000000000 | bytes 5000000 | tf_op jit(solution)/shard_map/pallas_call | solution.py:322
  109.7 1.8 %shard_map.126 = (bf16[512,2048]{1,0:T(8,128)(2,1)}, bf16[512,2048]{1,0:T(8,128)(2,1)}) custom-call(s32[1]{0:T(128)} %bitcast.member_ref, s32[1]{0:T(128)} %bitcast.1.pair_ref, f32[512,512]{1,0:T(8,128)S(1)} %get-tuple-element.85.refs_3_.refs_0_, f32[512,512]{1,0:T(8,128)S(1)} %get-tuple-element.92.refs_1_, ...), custom_call_target="tpu_custom_call", output_to_operand_aliasing={{0}: (8, {}), {1}: (9, {})} | custom-call | flops 2000000000 | bytes 5000000 | tf_op jit(solution)/shard_map/pallas_call | solution.py:322
  111.5 1.8 %shard_map.127 = (bf16[512,2048]{1,0:T(8,128)(2,1)}, bf16[512,2048]{1,0:T(8,128)(2,1)}) custom-call(s32[1]{0:T(128)} %bitcast.member_ref, s32[1]{0:T(128)} %bitcast.1.pair_ref, f32[512,512]{1,0:T(8,128)S(1)} %get-tuple-element.83.refs_5_.refs_0_, f32[512,512]{1,0:T(8,128)S(1)} %get-tuple-element.91.refs_1_, ...), custom_call_target="tpu_custom_call", output_to_operand_aliasing={{0}: (8, {}), {1}: (9, {})} | custom-call | flops 2000000000 | bytes 5000000 | tf_op jit(solution)/shard_map/pallas_call | solution.py:322
  113.2 1.8 %shard_map.128 = (bf16[512,2048]{1,0:T(8,128)(2,1)}, bf16[512,2048]{1,0:T(8,128)(2,1)}) custom-call(s32[1]{0:T(128)} %bitcast.member_ref, s32[1]{0:T(128)} %bitcast.1.pair_ref, f32[512,512]{1,0:T(8,128)S(1)} %get-tuple-element.88.refs_5_.refs_0_, f32[512,512]{1,0:T(8,128)S(1)} %get-tuple-element.89.refs_1_, ...), custom_call_target="tpu_custom_call", output_to_operand_aliasing={{0}: (8, {}), {1}: (9, {})} | custom-call | flops 2000000000 | bytes 5000000 | tf_op jit(solution)/shard_map/pallas_call | solution.py:322
  (59 shorter events, 22.2 us)
Async XLA Ops:
  0.6 1.6 %copy-start.2 = (bf16[512,2048]{1,0:T(8,128)(2,1)S(1)}, bf16[512,2048]{1,0:T(8,128)(2,1)}, u32[]{:S(2)}) copy-start(bf16[512,2048]{1,0:T(8,128)(2,1)} %refs_2_.31) | copy-start | bytes 6291460
  2.2 1.6 %copy-start.4 = (bf16[512,2048]{1,0:T(8,128)(2,1)S(1)}, bf16[512,2048]{1,0:T(8,128)(2,1)}, u32[]{:S(2)}) copy-start(bf16[512,2048]{1,0:T(8,128)(2,1)} %refs_3_.15) | copy-start | bytes 6291460
  3.8 0.8 copy-start.7
  5.7 10.3 %collective-permute-start.1 = (f32[520,128]{1,0:T(8,128)S(1)}, f32[520,128]{1,0:T(8,128)S(1)}, u32[]{:S(2)}, u32[]{:S(2)}) collective-permute-start(f32[520,128]{1,0:T(8,128)S(1)} %get-tuple-element.55.refs_3_), channel_id=1, source_target_pairs={{0,4},{4,0},{8,12},{12,8},{16,20},{20,16},{24,28},{28,24},{1,5},{5... | collective-permute-start | bytes 798728 | tf_op jit(solution)/shard_map/ppermute | solution.py:372
  9.5 12.4 %collective-permute-start = (f32[520,128]{1,0:T(8,128)S(1)}, f32[520,128]{1,0:T(8,128)S(1)}, u32[]{:S(2)}, u32[]{:S(2)}) collective-permute-start(f32[520,128]{1,0:T(8,128)S(1)} %shard_map.94.refs_3_), channel_id=1, source_target_pairs={{0,4},{4,0},{8,12},{12,8},{16,20},{20,16},{24,28},{28,24},{1,5},{5... | collective-permute-start | bytes 798728 | tf_op jit(solution)/shard_map/ppermute | solution.py:372
  10.4 1.6 %copy-start.1 = (bf16[512,2048]{1,0:T(8,128)(2,1)S(1)}, bf16[512,2048]{1,0:T(8,128)(2,1)}, u32[]{:S(2)}) copy-start(bf16[512,2048]{1,0:T(8,128)(2,1)} %refs_0_.23) | copy-start | bytes 6291460
  13.9 6.1 %copy-start.3 = (bf16[512,2048]{1,0:T(8,128)(2,1)S(1)}, bf16[512,2048]{1,0:T(8,128)(2,1)}, u32[]{:S(2)}) copy-start(bf16[512,2048]{1,0:T(8,128)(2,1)} %refs_2_.31) | copy-start | bytes 6291460
  16.0 7.8 %collective-permute-start.2 = (f32[512,128]{1,0:T(8,128)S(1)}, f32[512,128]{1,0:T(8,128)S(1)}, u32[]{:S(2)}, u32[]{:S(2)}) collective-permute-start(f32[512,128]{1,0:T(8,128)S(1)} %shard_map.98.refs_4_), channel_id=1, source_target_pairs={{0,8},{4,12},{1,9},{5,13},{2,10},{6,14},{3,11},{7,15}} | collective-permute-start | bytes 786440 | tf_op jit(solution)/shard_map/ppermute | solution.py:393
  21.9 6.4 %copy-start.5 = (bf16[512,2048]{1,0:T(8,128)(2,1)S(1)}, bf16[512,2048]{1,0:T(8,128)(2,1)}, u32[]{:S(2)}) copy-start(bf16[512,2048]{1,0:T(8,128)(2,1)} %refs_3_.15) | copy-start | bytes 6291460
  23.9 8.3 %collective-permute-start.3 = (f32[512,128]{1,0:T(8,128)S(1)}, f32[512,128]{1,0:T(8,128)S(1)}, u32[]{:S(2)}, u32[]{:S(2)}) collective-permute-start(f32[512,128]{1,0:T(8,128)S(1)} %shard_map.100.refs_4_), channel_id=1, source_target_pairs={{0,8},{4,12},{8,16},{12,20},{1,9},{5,13},{9,17},{13,21},{2,10},{6,... | collective-permute-start | bytes 786440 | tf_op jit(solution)/shard_map/ppermute | solution.py:393
  32.2 2.6 %collective-permute-start.4 = (f32[512,128]{1,0:T(8,128)S(1)}, f32[512,128]{1,0:T(8,128)S(1)}, u32[]{:S(2)}, u32[]{:S(2)}) collective-permute-start(f32[512,128]{1,0:T(8,128)S(1)} %shard_map.102.refs_4_), channel_id=1, source_target_pairs={{8,16},{12,20},{16,24},{20,28},{9,17},{13,21},{17,25},{21,29},{10,... | collective-permute-start | bytes 786440 | tf_op jit(solution)/shard_map/ppermute | solution.py:393
  34.8 2.6 %copy-start = (bf16[512,2048]{1,0:T(8,128)(2,1)S(1)}, bf16[512,2048]{1,0:T(8,128)(2,1)}, u32[]{:S(2)}) copy-start(bf16[512,2048]{1,0:T(8,128)(2,1)} %refs_1_.35) | copy-start | bytes 6291460
  34.8 2.5 %copy-start.6 = (f32[2048]{0:T(1024)S(1)}, f32[2048]{0:T(1024)}, u32[]{:S(2)}) copy-start(f32[2048]{0:T(1024)} %param.10) | copy-start | bytes 24580
  34.8 3.6 %collective-permute-start.5 = (f32[512,128]{1,0:T(8,128)S(1)}, f32[512,128]{1,0:T(8,128)S(1)}, u32[]{:S(2)}, u32[]{:S(2)}) collective-permute-start(f32[512,128]{1,0:T(8,128)S(1)} %shard_map.104.refs_5_), channel_id=1, source_target_pairs={{16,24},{20,28},{17,25},{21,29},{18,26},{22,30},{19,27},{23,31}} | collective-permute-start | bytes 786440 | tf_op jit(solution)/shard_map/ppermute | solution.py:393
  35.7 6.9 %collective-permute-start.7 = (f32[512,128]{1,0:T(8,128)S(1)}, f32[512,128]{1,0:T(8,128)S(1)}, u32[]{:S(2)}, u32[]{:S(2)}) collective-permute-start(f32[512,128]{1,0:T(8,128)S(1)} %get-tuple-element.57.refs_7_), channel_id=1, source_target_pairs={{0,4},{4,0},{8,12},{12,8},{16,20},{20,16},{24,28},{28,24},{1,5},{5... | collective-permute-start | bytes 786440 | tf_op jit(solution)/shard_map/ppermute | solution.py:403
  38.5 6.9 %collective-permute-start.6 = (f32[512,128]{1,0:T(8,128)S(1)}, f32[512,128]{1,0:T(8,128)S(1)}, u32[]{:S(2)}, u32[]{:S(2)}) collective-permute-start(f32[512,128]{1,0:T(8,128)S(1)} %get-tuple-element.60.refs_7_), channel_id=1, source_target_pairs={{0,4},{4,0},{8,12},{12,8},{16,20},{20,16},{24,28},{28,24},{1,5},{5... | collective-permute-start | bytes 786440 | tf_op jit(solution)/shard_map/ppermute | solution.py:403
  46.5 1.8 %collective-permute-start.10 = (f32[8,512]{1,0:T(8,128)S(1)}, f32[8,512]{1,0:T(8,128)S(1)}, u32[]{:S(2)}, u32[]{:S(2)}) collective-permute-start(f32[8,512]{1,0:T(8,128)S(1)} %get-tuple-element.64.refs_5_), channel_id=1, source_target_pairs={{0,3},{1,0},{2,1},{3,2},{4,7},{5,4},{6,5},{7,6},{8,11},{9,8},{10,9... | collective-permute-start | bytes 49160 | tf_op jit(solution)/shard_map/ppermute | solution.py:467
  46.5 3.8 %collective-permute-start.9 = (f32[8,512]{1,0:T(8,128)S(1)}, f32[8,512]{1,0:T(8,128)S(1)}, u32[]{:S(2)}, u32[]{:S(2)}) collective-permute-start(f32[8,512]{1,0:T(8,128)S(1)} %get-tuple-element.64.refs_5_), channel_id=1, source_target_pairs={{0,2},{1,3},{2,0},{3,1},{4,6},{5,7},{6,4},{7,5},{8,10},{9,11},{10,... | collective-permute-start | bytes 49160 | tf_op jit(solution)/shard_map/ppermute | solution.py:467
  48.1 3.2 %collective-permute-start.8 = (f32[8,512]{1,0:T(8,128)S(1)}, f32[8,512]{1,0:T(8,128)S(1)}, u32[]{:S(2)}, u32[]{:S(2)}) collective-permute-start(f32[8,512]{1,0:T(8,128)S(1)} %get-tuple-element.64.refs_5_), channel_id=1, source_target_pairs={{0,1},{1,2},{2,3},{3,0},{4,5},{5,6},{6,7},{7,4},{8,9},{9,10},{10,1... | collective-permute-start | bytes 49160 | tf_op jit(solution)/shard_map/ppermute | solution.py:467
  53.0 9.3 %collective-permute-start.11 = (f32[520,128]{1,0:T(8,128)S(1)}, f32[520,128]{1,0:T(8,128)S(1)}, u32[]{:S(2)}, u32[]{:S(2)}) collective-permute-start(f32[520,128]{1,0:T(8,128)S(1)} %get-tuple-element.69.refs_10_), channel_id=1, source_target_pairs={{0,4},{4,0},{8,12},{12,8},{16,20},{20,16},{24,28},{28,24},{1,5},{5... | collective-permute-start | bytes 798728 | tf_op jit(solution)/shard_map/ppermute | solution.py:372
  56.2 10.9 %collective-permute-start.12 = (f32[520,128]{1,0:T(8,128)S(1)}, f32[520,128]{1,0:T(8,128)S(1)}, u32[]{:S(2)}, u32[]{:S(2)}) collective-permute-start(f32[520,128]{1,0:T(8,128)S(1)} %get-tuple-element.71.refs_10_), channel_id=1, source_target_pairs={{0,4},{4,0},{8,12},{12,8},{16,20},{20,16},{24,28},{28,24},{1,5},{5... | collective-permute-start | bytes 798728 | tf_op jit(solution)/shard_map/ppermute | solution.py:372
  62.3 4.8 %collective-permute-start.13 = (f32[512,128]{1,0:T(8,128)S(1)}, f32[512,128]{1,0:T(8,128)S(1)}, u32[]{:S(2)}, u32[]{:S(2)}) collective-permute-start(f32[512,128]{1,0:T(8,128)S(1)} %shard_map.115.refs_6_), channel_id=1, source_target_pairs={{24,16},{28,20},{25,17},{29,21},{26,18},{30,22},{27,19},{31,23}} | collective-permute-start | bytes 786440 | tf_op jit(solution)/shard_map/ppermute | solution.py:393
  67.1 4.6 %collective-permute-start.14 = (f32[512,128]{1,0:T(8,128)S(1)}, f32[512,128]{1,0:T(8,128)S(1)}, u32[]{:S(2)}, u32[]{:S(2)}) collective-permute-start(f32[512,128]{1,0:T(8,128)S(1)} %shard_map.117.refs_7_), channel_id=1, source_target_pairs={{24,16},{28,20},{16,8},{20,12},{25,17},{29,21},{17,9},{21,13},{26,... | collective-permute-start | bytes 786440 | tf_op jit(solution)/shard_map/ppermute | solution.py:393
  71.7 26.3 %collective-permute-start.15 = (f32[512,128]{1,0:T(8,128)S(1)}, f32[512,128]{1,0:T(8,128)S(1)}, u32[]{:S(2)}, u32[]{:S(2)}) collective-permute-start(f32[512,128]{1,0:T(8,128)S(1)} %shard_map.119.refs_7_), channel_id=1, source_target_pairs={{16,8},{20,12},{8,0},{12,4},{17,9},{21,13},{9,1},{13,5},{18,10},{2... | collective-permute-start | bytes 786440 | tf_op jit(solution)/shard_map/ppermute | solution.py:393
  98.0 8.3 %collective-permute-start.16 = (f32[512,128]{1,0:T(8,128)S(1)}, f32[512,128]{1,0:T(8,128)S(1)}, u32[]{:S(2)}, u32[]{:S(2)}) collective-permute-start(f32[512,128]{1,0:T(8,128)S(1)} %shard_map.121.refs_5_), channel_id=1, source_target_pairs={{8,0},{12,4},{9,1},{13,5},{10,2},{14,6},{11,3},{15,7}} | collective-permute-start | bytes 786440 | tf_op jit(solution)/shard_map/ppermute | solution.py:393
  99.4 12.0 %collective-permute-start.18 = (f32[512,128]{1,0:T(8,128)S(1)}, f32[512,128]{1,0:T(8,128)S(1)}, u32[]{:S(2)}, u32[]{:S(2)}) collective-permute-start(f32[512,128]{1,0:T(8,128)S(1)} %get-tuple-element.86.refs_7_), channel_id=1, source_target_pairs={{0,4},{4,0},{8,12},{12,8},{16,20},{20,16},{24,28},{28,24},{1,5},{5... | collective-permute-start | bytes 786440 | tf_op jit(solution)/shard_map/ppermute | solution.py:403
  106.4 6.8 %collective-permute-start.17 = (f32[512,128]{1,0:T(8,128)S(1)}, f32[512,128]{1,0:T(8,128)S(1)}, u32[]{:S(2)}, u32[]{:S(2)}) collective-permute-start(f32[512,128]{1,0:T(8,128)S(1)} %get-tuple-element.90.refs_6_), channel_id=1, source_target_pairs={{0,4},{4,0},{8,12},{12,8},{16,20},{20,16},{24,28},{28,24},{1,5},{5... | collective-permute-start | bytes 786440 | tf_op jit(solution)/shard_map/ppermute | solution.py:403
